TPU v7x, 32 devices: a whole 2x2x4 slice. The times are simulated.
32 devices in a mesh: seq: 8 (over z, y), dp: 4 (over x, core).
Axes of the slice: x: 2, y: 2, z: 4, core: 2. Of those that a mesh axis runs over, the one named last changes fastest.
Arguments:
- tokens: bfloat16 [4, 1024, 1536], P('dp', 'seq'), may hold values from -6 to 6
- w_in: bfloat16 [1536, 1536], P('dp'), may hold values from -0.15625 to 0.15625
- w_out: bfloat16 [1536, 1536], P('dp'), may hold values from -0.15625 to 0.15625
- first_factor: bfloat16 [8, 128, 128], P('seq'), may hold values from -0.5 to 0.5
- second_factor: bfloat16 [128, 8, 8], P('seq'), may hold values from -2 to 2
- cotangent: bfloat16 [4, 1024, 1536], P('dp', 'seq'), may hold values from -6 to 6
Outputs:
- mixed: bfloat16 [4, 1024, 1536], P('dp', 'seq')
- input_grad: bfloat16 [4, 1024, 1536], P('dp', 'seq')
- out_weight_grad: float32 [1536, 1536], P(('seq', 'dp'))
All inputs are finite; a program needn't handle non-finite values.
Results may differ from a plain program's by a relative error of at most 0.0071.
Values may be sent and summed in bfloat16 or wider, within the bound.
No kernel may reach another device: no remote copies, remote signals or barrier semaphores. Data moves between devices by JAX's collectives and lax.ppermute only.
A program may use at most 128 MiB of HBM per device.

v0:
```python
import jax
import jax.numpy as jnp
from jax import lax
from jax.sharding import PartitionSpec as P


def second_forward(factor, piece):
    return jnp.einsum("sab,bsd->asd", factor, piece, preferred_element_type=jnp.float32).astype(
        jnp.bfloat16
    )


def second_adjoint(factor, piece):
    return jnp.einsum("sab,asd->bsd", factor, piece, preferred_element_type=jnp.float32).astype(
        jnp.bfloat16
    )


def on_device(tokens, w_in, w_out, first_factor, second_factor, cotangent):
    inputs = tokens[0]
    upstream = cotangent[0]
    rows, width = inputs.shape
    block = first_factor.shape[1]
    nblocks = rows // block
    whole_in, whole_out = (
        lax.all_gather(w_in, "dp", axis=0, tiled=True),
        lax.all_gather(w_out, "dp", axis=0, tiled=True),
    )
    projected = jnp.dot(inputs, whole_in, preferred_element_type=jnp.float32)
    projected = projected.astype(jnp.bfloat16).reshape(nblocks, block, width)
    first_mix = jnp.einsum(
        "bst,btd->bsd", first_factor, projected, preferred_element_type=jnp.float32
    ).astype(jnp.bfloat16)
    second_mix = second_forward(
        second_factor, lax.all_to_all(first_mix, "seq", split_axis=1, concat_axis=0, tiled=True)
    )
    monarch = lax.all_to_all(second_mix, "seq", split_axis=0, concat_axis=1, tiled=True).reshape(
        rows, width
    )
    inputs_wide = inputs.astype(jnp.float32)
    sigma = jax.nn.sigmoid(inputs_wide)
    gate = jax.nn.silu(inputs_wide)
    monarch_wide = monarch.astype(jnp.float32)
    gated = (monarch_wide * gate).astype(jnp.bfloat16)
    mixed = jnp.dot(gated, whole_out, preferred_element_type=jnp.float32)
    gated_grad = jnp.dot(upstream, whole_out.T, preferred_element_type=jnp.float32)
    monarch_grad = (gated_grad * gate).astype(jnp.bfloat16).reshape(nblocks, block, width)
    first_grad = second_adjoint(
        second_factor, lax.all_to_all(monarch_grad, "seq", split_axis=1, concat_axis=0, tiled=True)
    )
    first_back = lax.all_to_all(first_grad, "seq", split_axis=0, concat_axis=1, tiled=True)
    projected_grad = jnp.einsum(
        "bst,bsd->btd", first_factor, first_back, preferred_element_type=jnp.float32
    )
    projected_grad = projected_grad.astype(jnp.bfloat16).reshape(rows, width)
    gate_term = gated_grad * monarch_wide * (sigma * (1.0 + inputs_wide * (1.0 - sigma)))
    carried = jnp.dot(projected_grad, whole_in.T, preferred_element_type=jnp.float32)
    input_grad = (carried + gate_term).astype(jnp.bfloat16)
    seq_count = lax.axis_size("seq")
    dp_count = lax.axis_size("dp")
    summed = lax.psum_scatter(
        lax.dot_general(
            gated, upstream, (((0,), (0,)), ((), ())), preferred_element_type=jnp.float32
        ),
        ("seq", "dp"),
        scatter_dimension=0,
        tiled=True,
    )
    weight_grad = summed / jnp.sqrt(jnp.float32(rows * seq_count * dp_count))
    return (mixed.astype(jnp.bfloat16)[None], input_grad[None], weight_grad)


def solution(mesh):
    placed = (
        P("dp", "seq", None),
        P("dp", None),
        P("dp", None),
        P("seq", None, None),
        P("seq", None, None),
        P("dp", "seq", None),
    )
    return jax.shard_map(
        on_device,
        mesh=mesh,
        in_specs=placed,
        out_specs=(P("dp", "seq", None), P("dp", "seq", None), P(("seq", "dp"), None)),
        check_vma=False,
    )
```

profile of v0, /device:TPU:0, one launch (start us, length us, event | category | flops | bytes accessed | tf_op | source)
XLA Modules:
  0.0 239.7 jit_solution(8930923431436796886)
XLA Ops:
  7.2 0.0 copy-start
  7.2 0.0 all-gather.3.cloned.1.call-start
  7.2 0.7 all-gather.3.cloned.1.call-update
  7.9 0.0 all-gather.5.cloned.1.call-start
  8.0 0.7 all-gather.5.cloned.1.call-update
  8.7 0.0 copy-start.3
  8.7 41.1 %all-gather.3.cloned.1.call-done = bf16[1536,1536]{1,0:T(8,128)(2,1)} async-done(((bf16[384,1536]{1,0:T(8,128)(2,1)}), bf16[1536,1536]{1,0:T(8,128)(2,1)}) %all-gather.3.cloned.1.call-update) | async-done | bytes 4718608 | tf_op jit(solution)/shard_map/all_gather | solution.py:26
  49.8 3.4 %fusion.2 = bf16[1,128,1536]{1,2,0:T(8,128)(2,1)S(1)} fusion(bf16[1536,1536]{1,0:T(8,128)(2,1)} %all-gather.3.cloned.1.call-done, bf16[1,128,1536]{2,1,0:T(8,128)(2,1)} %param.6, bf16[1,128,128]{2,1,0:T(8,128)(2,1)} %param.9), kind=kOutput, calls=%fused_computation.9 | convolution fusion | flops 654704640 | bytes 5537792 | tf_op jit(solution)/shard_map/bst,btd->bsd/dot_general | solution.py:31
  53.2 0.0 copy-start.1
  53.2 0.7 copy.30
  53.9 0.5 broadcast.8
  54.4 3.0 %reduce = bf16[128,1536]{1,0:T(8,128)(2,1)S(1)} reduce(bf16[128,1,1536]{2,1,0:T(2,128)(2,1)S(1)} %bitcast.63, bf16[]{:T(256)} %broadcast.8), dimensions={1}, to_apply=%bitcast.46.reduce_sub_computation | reduce | bytes 786434
  57.4 1.0 reshape.62
  58.5 5.5 %all-to-all-start = ((bf16[8,2,12288]{2,1,0:T(2,128)(2,1)}), bf16[8,2,12288]{2,1,0:T(2,128)(2,1)S(1)}, u32[]{:S(2)}, u32[]{:S(2)}) async-start(bf16[8,2,12288]{2,1,0:T(2,128)(2,1)} %reshape.62), calls=%async_computation | async-start | bytes 786432 | tf_op jit(solution)/shard_map/all_to_all | solution.py:35
  64.0 0.0 reduce-scatter.2.cloned.1.call-start
  64.0 0.0 copy-done.3
  64.0 0.1 copy.36
  64.1 11.9 %all-to-all-done = bf16[8,2,12288]{2,1,0:T(2,128)(2,1)S(1)} async-done(((bf16[8,2,12288]{2,1,0:T(2,128)(2,1)}), bf16[8,2,12288]{2,1,0:T(2,128)(2,1)S(1)}, u32[]{:S(2)}, u32[]{:S(2)}) %all-to-all-start) | async-done | bytes 393248 | tf_op jit(solution)/shard_map/all_to_all | solution.py:35
  76.1 0.4 reshape.63
  76.5 0.1 copy.38
  76.5 0.4 fusion.3
  76.9 0.1 copy.33
  77.0 15.7 %all_to_all.42 = bf16[8,16,1536]{2,1,0:T(8,128)(2,1)S(1)} all-to-all(bf16[8,16,1536]{2,1,0:T(8,128)(2,1)S(1)} %copy.33), channel_id=1, replica_groups=mesh['seq'=8,'dp'=4] {'seq'}, dimensions={0} | all-to-all | bytes 786432 | tf_op jit(solution)/shard_map/all_to_all | solution.py:37
  92.7 0.0 copy-done.1
  92.7 0.2 fusion.17
  92.9 0.0 copy-done
  93.0 5.0 %fusion.19 = f32[1536,1536]{1,0:T(8,128)} fusion(bf16[128,1536]{1,0:T(8,128)(2,1)S(1)} %bitcast.67, bf16[1,128,1536]{2,1,0:T(8,128)(2,1)S(1)} %copy-done), kind=kOutput, calls=%fused_computation.34 | convolution fusion | flops 603979776 | bytes 10223616 | tf_op jit(solution)/shard_map/dot_general | solution.py:62
  98.0 0.0 reduce-scatter.2.cloned.1.call-update
  98.0 0.0 all-gather.5.cloned.1.call-done
  98.1 4.0 %bitcast_multiply_fusion = (f32[128,1536]{1,0:T(8,128)S(1)}, bf16[1,128,1536]{2,1,0:T(8,128)(2,1)S(1)}, bf16[128,1536]{1,0:T(8,128)(2,1)S(1)}) fusion(bf16[8,16,1536]{2,1,0:T(8,128)(2,1)S(1)} %all_to_all.42, bf16[1,128,1536]{2,1,0:T(8,128)(2,1)S(1)} %copy-done.1, bf16[1536,1536]{1,0:T(8,128)(2,1)} %all-gather.5.cloned.1.call-done, ...), kind=kOutput, calls=%fused_computation.28 | convolution fusion | flops 606142464 | bytes 7471104 | tf_op jit(solution)/shard_map/dot_general | solution.py:46
  102.1 0.6 copy.45
  102.7 3.0 %reduce.1 = bf16[128,1536]{1,0:T(8,128)(2,1)S(1)} reduce(bf16[128,1,1536]{2,1,0:T(2,128)(2,1)S(1)} %bitcast.64, bf16[]{:T(256)} %broadcast.8), dimensions={1}, to_apply=%bitcast.62.reduce_sub_computation | reduce | bytes 786434
  105.7 0.3 reshape.64
  106.0 15.0 %all_to_all.43 = bf16[8,2,12288]{2,1,0:T(2,128)(2,1)S(1)} all-to-all(bf16[8,2,12288]{2,1,0:T(2,128)(2,1)S(1)} %reshape.64), channel_id=1, replica_groups=mesh['seq'=8,'dp'=4] {'seq'}, dimensions={0} | all-to-all | bytes 786432 | tf_op jit(solution)/shard_map/all_to_all | solution.py:49
  121.0 0.4 reshape.65
  121.4 0.0 copy-start.2
  121.4 0.1 copy.39
  121.4 0.3 fusion.4
  121.8 0.9 copy.37
  122.6 3.5 %all-to-all-start.3 = ((bf16[8,16,1536]{2,1,0:T(8,128)(2,1)}), bf16[8,16,1536]{2,1,0:T(8,128)(2,1)S(1)}, u32[]{:S(2)}, u32[]{:S(2)}) async-start(bf16[8,16,1536]{2,1,0:T(8,128)(2,1)} %copy.37), calls=%async_computation.3 | async-start | bytes 786432 | tf_op jit(solution)/shard_map/all_to_all | solution.py:51
  126.1 4.1 %fusion.5 = bf16[1,128,1536]{2,1,0:T(8,128)(2,1)} fusion(bf16[128,1536]{1,0:T(8,128)(2,1)S(1)} %get-tuple-element.5, bf16[1536,1536]{1,0:T(8,128)(2,1)} %all-gather.5.cloned.1.call-done), kind=kOutput, calls=%fused_computation.12 | convolution fusion | flops 604176384 | bytes 5505024 | tf_op jit(solution)/shard_map/dot_general | solution.py:45
  130.2 7.1 %all-to-all-done.3 = bf16[8,16,1536]{2,1,0:T(8,128)(2,1)S(1)} async-done(((bf16[8,16,1536]{2,1,0:T(8,128)(2,1)}), bf16[8,16,1536]{2,1,0:T(8,128)(2,1)S(1)}, u32[]{:S(2)}, u32[]{:S(2)}) %all-to-all-start.3) | async-done | bytes 393248 | tf_op jit(solution)/shard_map/all_to_all | solution.py:51
  137.2 0.0 copy-done.2
  137.2 5.1 %fusion.1 = bf16[1,128,1536]{2,1,0:T(8,128)(2,1)} fusion(bf16[1536,1536]{1,0:T(8,128)(2,1)} %all-gather.3.cloned.1.call-done, bf16[128,1536]{1,0:T(8,128)(2,1)S(1)} %bitcast.71, f32[128,1536]{1,0:T(8,128)S(1)} %get-tuple-element.3, bf16[1,128,1536]{2,1,0:T(8,128)(2,1)S(1)} %copy-done.1, bf16[1,128,128]{2,1,0:T(8,128)(2,1)S(1)} %copy-done.2), kind=kOutput, calls=%fused_computation.8 | convolution fusion | flops 656670720 | bytes 6717440 | tf_op jit(solution)/shard_map/dot_general | solution.py:57
  142.3 89.1 %reduce-scatter.2.cloned.1.call-done = f32[48,1536]{1,0:T(8,128)} async-done(((f32[1536,1536]{1,0:T(8,128)}), f32[48,1536]{1,0:T(8,128)}) %reduce-scatter.2.cloned.1.call-update) | async-done | bytes 294928 | tf_op jit(solution)/shard_map/reduce_scatter | solution.py:61
  231.4 1.7 broadcast_multiply_fusion
Async XLA Ops:
  7.2 85.8 %copy-start = (bf16[1,128,1536]{2,1,0:T(8,128)(2,1)S(1)}, bf16[1,128,1536]{2,1,0:T(8,128)(2,1)}, u32[]{:S(2)}) copy-start(bf16[1,128,1536]{2,1,0:T(8,128)(2,1)} %param.11) | copy-start | bytes 1179652
  7.2 42.6 %all-gather.3.cloned.1.call-start = ((), (), s32[]{:S(2)}) async-start(), calls=%async_computation.5 | async-start | bytes 5898240 | tf_op jit(solution)/shard_map/all_gather | solution.py:26
  7.9 90.1 %all-gather.5.cloned.1.call-start = ((), (), s32[]{:S(2)}) async-start(), calls=%async_computation.6 | async-start | bytes 5898240 | tf_op jit(solution)/shard_map/all_gather | solution.py:27
  8.7 55.4 %copy-start.3 = (bf16[16,8,8]{0,2,1:T(8,128)(2,1)S(1)}, bf16[16,8,8]{0,2,1:T(8,128)(2,1)}, u32[]{:S(2)}) copy-start(bf16[16,8,8]{0,2,1:T(8,128)(2,1)} %param.10) | copy-start | bytes 6148
  53.2 39.5 %copy-start.1 = (bf16[1,128,1536]{2,1,0:T(8,128)(2,1)S(1)}, bf16[1,128,1536]{2,1,0:T(8,128)(2,1)}, u32[]{:S(2)}) copy-start(bf16[1,128,1536]{2,1,0:T(8,128)(2,1)} %param.6) | copy-start | bytes 1179652
  58.5 17.6 %all-to-all-start = ((bf16[8,2,12288]{2,1,0:T(2,128)(2,1)}), bf16[8,2,12288]{2,1,0:T(2,128)(2,1)S(1)}, u32[]{:S(2)}, u32[]{:S(2)}) async-start(bf16[8,2,12288]{2,1,0:T(2,128)(2,1)} %reshape.62), calls=%async_computation | async-start | bytes 786432 | tf_op jit(solution)/shard_map/all_to_all | solution.py:35
  64.0 167.5 %reduce-scatter.2.cloned.1.call-start = ((), (), s32[]{:S(2)}) async-start(), calls=%async_computation.7 | async-start | bytes 9732096 | tf_op jit(solution)/shard_map/reduce_scatter | solution.py:61
  121.4 15.9 %copy-start.2 = (bf16[1,128,128]{2,1,0:T(8,128)(2,1)S(1)}, bf16[1,128,128]{2,1,0:T(8,128)(2,1)}, u32[]{:S(2)}) copy-start(bf16[1,128,128]{2,1,0:T(8,128)(2,1)} %param.9) | copy-start | bytes 98308
  122.6 14.6 %all-to-all-start.3 = ((bf16[8,16,1536]{2,1,0:T(8,128)(2,1)}), bf16[8,16,1536]{2,1,0:T(8,128)(2,1)S(1)}, u32[]{:S(2)}, u32[]{:S(2)}) async-start(bf16[8,16,1536]{2,1,0:T(8,128)(2,1)} %copy.37), calls=%async_computation.3 | async-start | bytes 786432 | tf_op jit(solution)/shard_map/all_to_all | solution.py:51
Sparse Core Ops, SparseCore 0:
  9.6 40.1 all-gather.2
  51.3 37.4 all-gather.4
  98.1 133.2 reduce-scatter.1
where the time goes:
time: 240 us
  waiting for transfers between devices  151 us (63%)
  blocking collectives  30.7 us (13%)
  matrix products  22.3 us (9%)
  between operations  13.9 us (6%)
  starting transfers between devices  9.08 us (4%)
  other arithmetic  7.94 us (3%)
  local copies, waits for them, and re-layouts  5.11 us (2%)
    reduce_scatter x1, waiting for transfers between devices, on_device(): lax.psum_scatter(lax.dot_general(gated, upstream, (((0,), (0,)), ((), ())...  89.1 us
    all_gather x1, waiting for transfers between devices, on_device(): lax.all_gather(w_in, 'dp', axis=0, tiled=True)  41.1 us
    all_to_all x1, blocking collectives, on_device(): lax.all_to_all(second_mix, 'seq', split_axis=0, concat_axis=1, tiled=True)  15.7 us
    all_to_all x1, blocking collectives, on_device(): lax.all_to_all(monarch_grad, 'seq', split_axis=1, concat_axis=0, tiled=True)  15 us
    all_to_all x1, waiting for transfers between devices, on_device(): lax.all_to_all(first_mix, 'seq', split_axis=1, concat_axis=0, tiled=True)  11.9 us
    all_to_all x1, waiting for transfers between devices, on_device(): lax.all_to_all(first_grad, 'seq', split_axis=0, concat_axis=1, tiled=True)  7.05 us
    unnamed x2, other arithmetic  6 us
    all_to_all x1, starting transfers between devices, on_device(): lax.all_to_all(first_mix, 'seq', split_axis=1, concat_axis=0, tiled=True)  5.52 us
  transfers between devices with their start and end apart: 5, of which 4 were waited for; matrix products, arithmetic and copies ran while one was open for 14% of the time, Pallas kernels for 0%

commit v1 on v0

v1 whole, which is shorter than its diff:
```python
import jax
import jax.numpy as jnp
from jax import lax
from jax.sharding import PartitionSpec as P

F32 = jnp.float32
BF16 = jnp.bfloat16


def dot(a, b, ca, cb):
    return lax.dot_general(a, b, (((ca,), (cb,)), ((), ())), preferred_element_type=F32)


def swap(x, axis, bit):
    n = lax.axis_size(axis)
    return lax.ppermute(x, axis, [(i, i ^ bit) for i in range(n)])


def everywhere(x):
    far = swap(x, "dp", 2)
    return x, swap(x, "dp", 1), far, swap(far, "dp", 1)


def spread(x):
    return lax.all_to_all(x, "seq", split_axis=0, concat_axis=0, tiled=True)


def on_device(tokens, w_in, w_out, first_factor, second_factor, cotangent):
    inputs = tokens[0]
    upstream = cotangent[0]
    first = first_factor[0]
    rows, width = inputs.shape
    nseq = lax.axis_size("seq")
    ndp = lax.axis_size("dp")
    me = lax.axis_index("dp")
    my_s = lax.axis_index("seq")
    part = width // ndp
    offs = rows // nseq
    outer = nseq // 2
    piece = width // (nseq * ndp)

    def columns(x, r):
        return lax.dynamic_slice_in_dim(x, (me ^ r) * part, part, axis=1)

    mix = dot(first, inputs, 1, 0).astype(BF16).reshape(nseq, offs, width)
    mix = spread(mix)
    mix = jnp.einsum("sab,bsd->asd", second_factor, mix, preferred_element_type=F32).astype(BF16)
    mix = spread(mix).reshape(rows, width)

    cots = everywhere(upstream)
    toward = jnp.concatenate([columns(inputs, 2), columns(inputs, 3)], axis=1)
    toward = swap(toward, "dp", 2)
    side = swap(jnp.concatenate([columns(inputs, 1), toward[:, part:]], axis=1), "dp", 1)
    mine = (columns(inputs, 0), side[:, :part], toward[:, :part], side[:, part:])

    grads = []
    for cot, tok in zip(cots, mine):
        gate = jax.nn.silu(tok.astype(F32))
        grads.append((dot(cot, w_out, 1, 1) * gate).astype(BF16))
    grads = jnp.stack(grads)
    grads = jnp.stack(
        [lax.dynamic_index_in_dim(grads, me ^ j, 0, keepdims=False) for j in range(ndp)]
    )
    grads = grads.reshape(ndp, nseq, offs, part).transpose(1, 0, 2, 3)
    grads = grads.reshape(nseq * ndp, offs, part)
    grads = lax.all_to_all(grads, ("seq", "dp"), split_axis=0, concat_axis=0, tiled=True)
    grads = grads.reshape(nseq, ndp, offs, part)
    back = jnp.einsum("sab,ajsc->bjsc", second_factor, grads, preferred_element_type=F32)
    back = spread(back.astype(BF16))
    back = back.transpose(0, 2, 1, 3).reshape(rows, width)
    back = dot(first, back, 0, 0).astype(BF16)

    w_ins = everywhere(w_in)
    w_outs = everywhere(w_out)

    wide = inputs.astype(F32)
    gate = jax.nn.silu(wide)
    monarch = sum(dot(columns(mix, r), w_ins[r], 1, 0) for r in range(ndp))
    monarch = monarch.astype(BF16)
    gated = (monarch.astype(F32) * gate).astype(BF16)

    pairs = [upstream, cots[2]]
    other = [swap(c, "seq", 1) for c in pairs]
    quad = [pairs[0], cots[1], pairs[1], cots[3]]
    far = [other[0], swap(other[0], "dp", 1), other[1], swap(other[1], "dp", 1)]
    send = gated.T.reshape(outer, 2 * ndp, piece, rows).transpose(1, 0, 2, 3)
    groups = [[z * 2 * ndp + i for i in range(2 * ndp)] for z in range(outer)]
    got = lax.all_to_all(
        send, ("seq", "dp"), split_axis=0, concat_axis=0, tiled=True, axis_index_groups=groups
    )
    got = got.reshape(2 * ndp, outer * piece, rows)
    here = (my_s % 2) * ndp + me
    total = 0.0
    for r, cot in enumerate(quad + far):
        total = total + dot(lax.dynamic_index_in_dim(got, here ^ r, 0, keepdims=False), cot, 1, 0)
    total = total.astype(BF16).reshape(outer, piece, width)
    lines = [[2 * z + y for z in range(outer)] for y in range(2)]
    total = lax.all_to_all(
        total, "seq", split_axis=0, concat_axis=0, tiled=True, axis_index_groups=lines
    )
    total = jnp.sum(total.astype(F32), axis=0)
    weight_grad = total / jnp.sqrt(F32(rows * nseq * ndp))

    mixed = sum(dot(columns(gated, r), w_outs[r], 1, 0) for r in range(ndp)).astype(BF16)
    out = []
    for r in range(ndp):
        x = columns(wide, r)
        sigma = jax.nn.sigmoid(x)
        slope = sigma * (1.0 + x * (1.0 - sigma))
        term = dot(upstream, w_outs[r], 1, 1) * columns(monarch, r).astype(F32) * slope
        out.append((dot(back, w_ins[r], 1, 1) + term).astype(BF16))
    out = jnp.concatenate(out, axis=1)
    input_grad = jnp.concatenate(
        [lax.dynamic_slice_in_dim(out, (me ^ j) * part, part, axis=1) for j in range(ndp)], axis=1
    )
    return mixed[None], input_grad[None], weight_grad


def solution(mesh):
    placed = (
        P("dp", "seq", None),
        P("dp", None),
        P("dp", None),
        P("seq", None, None),
        P("seq", None, None),
        P("dp", "seq", None),
    )
    return jax.shard_map(
        on_device,
        mesh=mesh,
        in_specs=placed,
        out_specs=(P("dp", "seq", None), P("dp", "seq", None), P(("seq", "dp"), None)),
        check_vma=False,
    )
```

time: 240 us -> 169 us (0.70)
  waiting for transfers between devices: 151 us -> 69.4 us
  blocking collectives: 30.7 us -> 0 us
  starting transfers between devices: 9.08 us -> 37.3 us
  matrix products: 22.3 us -> 46.9 us
  between operations: 13.9 us -> 1.19 us
  local copies, waits for them, and re-layouts: 5.11 us -> 7.77 us
  other arithmetic: 7.94 us -> 5.32 us
    reduce_scatter x1 -> x0, waiting for transfers between devices: 89.1 us -> none  [on_device(): lax.psum_scatter(lax.dot_general(gated, upstream, (((0,), (0,)), ((), ())...]
    ppermute x0 -> x15, waiting for transfers between devices: none -> 45.9 us  [swap(): return lax.ppermute(x, axis, [(i, i ^ bit) for i in range(n)])]
    all_gather x2 -> x0, waiting for transfers between devices: 41.1 us -> none  [the longest x1 41.1 us: on_device(): lax.all_gather(w_in, 'dp', axis=0, tiled=True)]
    all_to_all x2 -> x0, blocking collectives: 30.7 us -> none  [the longest x1 15.7 us: on_device(): lax.all_to_all(second_mix, 'seq', split_axis=0, concat_axis=1, tiled=True)]
    dot_general x7 -> x31, matrix products: 22.3 us -> 46.9 us  [the longest x29 44.2 us: dot(): lax.dot_general(a, b, (((ca,), (cb,)), ((), ())), preferred_element_type=...]
    all_to_all x2 -> x6, starting transfers between devices: 8.97 us -> 27.1 us  [the longest x3 14.9 us: spread(): return lax.all_to_all(x, 'seq', split_axis=0, concat_axis=0, tiled=True)]
    ppermute x0 -> x15, starting transfers between devices: none -> 10.3 us  [swap(): return lax.ppermute(x, axis, [(i, i ^ bit) for i in range(n)])]
    unnamed x2 -> x0, other arithmetic: 6 us -> none
  transfers between devices with their start and end apart: 5 -> 21, of which waited for: 4 -> 6; matrix products, arithmetic and copies ran while one was open for 14% -> 34% of each run, Pallas kernels for 0% -> 0%
where the time goes in v1:
time: 169 us; the launch traced here: 168 us
  waiting for transfers between devices  69.4 us (41%)
  matrix products  46.9 us (28%)
  starting transfers between devices  37.3 us (22%)
  local copies, waits for them, and re-layouts  7.77 us (5%)
  other arithmetic  5.32 us (3%)
    ppermute x15, waiting for transfers between devices, swap(): return lax.ppermute(x, axis, [(i, i ^ bit) for i in range(n)])  45.9 us
    dot_general x29, matrix products, dot(): lax.dot_general(a, b, (((ca,), (cb,)), ((), ())), preferred_element_type=...  44.2 us
    all_to_all x3, starting transfers between devices, spread(): return lax.all_to_all(x, 'seq', split_axis=0, concat_axis=0, tiled=True)  14.9 us
    all_to_all x1, waiting for transfers between devices, on_device(): lax.all_to_all(total, 'seq', split_axis=0, concat_axis=0, tiled=True, axi...  12.2 us
    all_to_all x3, waiting for transfers between devices, spread(): return lax.all_to_all(x, 'seq', split_axis=0, concat_axis=0, tiled=True)  11.3 us
    ppermute x15, starting transfers between devices, swap(): return lax.ppermute(x, axis, [(i, i ^ bit) for i in range(n)])  10.3 us
    all_to_all x1, starting transfers between devices, on_device(): lax.all_to_all(grads, ('seq', 'dp'), split_axis=0, concat_axis=0, tiled=T...  5.04 us
    all_to_all x1, starting transfers between devices, on_device(): lax.all_to_all(total, 'seq', split_axis=0, concat_axis=0, tiled=True, axi...  3.61 us
  transfers between devices with their start and end apart: 21, of which 6 were waited for; matrix products, arithmetic and copies ran while one was open for 34% of the time, Pallas kernels for 0%

profile of v1, /device:TPU:0, one launch (start us, length us, event | category | flops | bytes accessed | tf_op | source)
XLA Modules:
  0.0 167.9 jit_solution(13203412226842850426)
XLA Ops:
  1.2 2.6 %collective-permute-start.9 = (bf16[128,1536]{1,0:T(8,128)(2,1)}, bf16[128,1536]{1,0:T(8,128)(2,1)}, u32[]{:S(2)}, u32[]{:S(2)}) collective-permute-start(bf16[128,1536]{1,0:T(8,128)(2,1)} %bitcast.128), channel_id=1, source_target_pairs={{0,2},{1,3},{2,0},{3,1},{4,6},{5,7},{6,4},{7,5},{8,10},{9,11},{10,... | collective-permute-start | bytes 1179656 | tf_op jit(solution)/shard_map/ppermute | solution.py:16
  4.2 2.0 %convolution_convert_fusion.2 = bf16[128,1536]{1,0:T(8,128)(2,1)} fusion(bf16[1,128,1536]{2,1,0:T(8,128)(2,1)} %param.6, bf16[1,128,128]{2,1,0:T(8,128)(2,1)S(1)} %copy-done), kind=kOutput, calls=%fused_computation.18 | convolution fusion | flops 50528256 | bytes 819200 | tf_op jit(solution)/shard_map/dot_general | solution.py:11
  6.2 6.1 %all-to-all-start = ((bf16[8,16,1536]{2,1,0:T(8,128)(2,1)}), bf16[8,16,1536]{2,1,0:T(8,128)(2,1)}, u32[]{:S(2)}, u32[]{:S(2)}) async-start(bf16[8,16,1536]{2,1,0:T(8,128)(2,1)} %bitcast.139), calls=%async_computation | async-start | bytes 786432 | tf_op jit(solution)/shard_map/all_to_all | solution.py:25
  13.7 1.5 collective-permute-start.7
  15.8 27.5 %collective-permute-done.7 = bf16[128,768]{1,0:T(8,128)(2,1)} collective-permute-done((bf16[128,768]{1,0:T(8,128)(2,1)}, bf16[128,768]{1,0:T(8,128)(2,1)}, u32[]{:S(2)}, u32[]{:S(2)}) %collective-permute-start.7) | collective-permute-done | bytes 196640 | tf_op jit(solution)/shard_map/ppermute | solution.py:16
  43.3 0.9 slice.16
  44.2 0.9 pad_maximum_fusion.4
  45.7 1.5 fusion.17
  47.2 1.8 %collective-permute-start.1 = (bf16[384,1536]{1,0:T(8,128)(2,1)}, bf16[384,1536]{1,0:T(8,128)(2,1)}, u32[]{:S(2)}, u32[]{:S(2)}) collective-permute-start(bf16[384,1536]{1,0:T(8,128)(2,1)} %param.7), channel_id=1, source_target_pairs={{0,2},{1,3},{2,0},{3,1},{4,6},{5,7},{6,4},{7,5},{8,10},{9,11},{10,... | collective-permute-start | bytes 3538952 | tf_op jit(solution)/shard_map/ppermute | solution.py:16
  49.0 1.5 fusion.18
  52.2 5.0 %all-to-all-start.2 = ((bf16[32,16,384]{2,1,0:T(8,128)(2,1)}), bf16[32,16,384]{2,1,0:T(8,128)(2,1)}, u32[]{:S(2)}, u32[]{:S(2)}) async-start(bf16[32,16,384]{2,1,0:T(8,128)(2,1)} %bitcast.140), calls=%async_computation.2 | async-start | bytes 786432 | tf_op jit(solution)/shard_map/all_to_all | solution.py:66
  57.3 1.8 %collective-permute-start.11 = (bf16[128,1536]{1,0:T(8,128)(2,1)S(1)}, bf16[128,1536]{1,0:T(8,128)(2,1)}, u32[]{:S(2)}, u32[]{:S(2)}) collective-permute-start(bf16[128,1536]{1,0:T(8,128)(2,1)S(1)} %bitcast.129), channel_id=1, source_target_pairs={{0,4},{4,0},{8,12},{12,8},{16,20},{20,16},{24,28},{28,24},{1,5},{5... | collective-permute-start | bytes 1179656 | tf_op jit(solution)/shard_map/ppermute | solution.py:16
  59.4 1.0 bitcast_convert_fusion
  60.6 12.1 %collective-permute-done.11 = bf16[128,1536]{1,0:T(8,128)(2,1)} collective-permute-done((bf16[128,1536]{1,0:T(8,128)(2,1)S(1)}, bf16[128,1536]{1,0:T(8,128)(2,1)}, u32[]{:S(2)}, u32[]{:S(2)}) %collective-permute-start.11) | collective-permute-done | bytes 393248 | tf_op jit(solution)/shard_map/ppermute | solution.py:16
  72.7 1.3 fusion.6
  74.9 6.3 %collective-permute-done.13 = bf16[128,1536]{1,0:T(8,128)(2,1)} collective-permute-done((bf16[128,1536]{1,0:T(8,128)(2,1)}, bf16[128,1536]{1,0:T(8,128)(2,1)}, u32[]{:S(2)}, u32[]{:S(2)}) %collective-permute-start.13) | collective-permute-done | bytes 393248 | tf_op jit(solution)/shard_map/ppermute | solution.py:16
  81.2 4.7 %all-to-all-start.1 = ((bf16[8,16,1536]{2,1,0:T(8,128)(2,1)}), bf16[8,16,1536]{2,1,0:T(8,128)(2,1)}, u32[]{:S(2)}, u32[]{:S(2)}) async-start(bf16[8,16,1536]{2,1,0:T(8,128)(2,1)} %copy.23), calls=%async_computation.1 | async-start | bytes 786432 | tf_op jit(solution)/shard_map/all_to_all | solution.py:25
  86.3 1.2 fusion.86
  88.0 2.5 %fusion.88 = f32[128,384]{1,0:T(8,128)} fusion(bf16[384,1536]{1,0:T(8,128)(2,1)} %collective-permute-done.3, bf16[1,128,1536]{2,1,0:T(8,128)(2,1)S(1)} %copy-done.1), kind=kOutput, calls=%fused_computation.140 | convolution fusion | flops 150994944 | bytes 1769472 | tf_op jit(solution)/shard_map/dot_general | solution.py:11
  90.4 1.3 fusion.7
  91.8 0.9 copy.27
  92.7 5.8 %all-to-all-done.1 = bf16[8,16,1536]{2,1,0:T(8,128)(2,1)} async-done(((bf16[8,16,1536]{2,1,0:T(8,128)(2,1)}), bf16[8,16,1536]{2,1,0:T(8,128)(2,1)}, u32[]{:S(2)}, u32[]{:S(2)}) %all-to-all-start.1) | async-done | bytes 393248 | tf_op jit(solution)/shard_map/all_to_all | solution.py:25
  98.4 4.1 %all-to-all-start.3 = ((bf16[8,4,16,384]{3,1,2,0:T(4,128)(2,1)}), bf16[8,4,16,384]{3,1,2,0:T(4,128)(2,1)}, u32[]{:S(2)}, u32[]{:S(2)}) async-start(bf16[8,4,16,384]{3,1,2,0:T(4,128)(2,1)} %copy.27), calls=%async_computation.3 | async-start | bytes 786432 | tf_op jit(solution)/shard_map/all_to_all | solution.py:25
  102.5 1.7 %fusion.44 = f32[128,1536]{1,0:T(8,128)S(1)} fusion(bf16[384,1536]{1,0:T(8,128)(2,1)} %param.7, bf16[128,1536]{1,0:T(8,128)(2,1)} %bitcast.4, s32[]{:T(128)S(6)} %select_n.77), kind=kOutput, calls=%fused_computation.88 | convolution fusion | flops 150994944 | bytes 2064388 | tf_op jit(solution)/shard_map/dot_general | solution.py:11
  104.2 1.7 %convolution_add_fusion.10 = f32[128,1536]{1,0:T(8,128)S(1)} fusion(f32[128,1536]{1,0:T(8,128)S(1)} %fusion.44, bf16[384,1536]{1,0:T(8,128)(2,1)} %collective-permute-done, bf16[128,1536]{1,0:T(8,128)(2,1)} %bitcast.4, s32[]{:T(128)S(6)} %select_n.78), kind=kOutput, calls=%fused_computation.13 | convolution fusion | flops 151191552 | bytes 2850820 | tf_op jit(solution)/shard_map/dot_general | solution.py:11
  105.9 2.6 %convolution_add_fusion.9 = f32[128,1536]{1,0:T(8,128)} fusion(f32[128,1536]{1,0:T(8,128)S(1)} %convolution_add_fusion.10, bf16[384,1536]{1,0:T(8,128)(2,1)} %collective-permute-done.1, bf16[128,1536]{1,0:T(8,128)(2,1)} %bitcast.4, s32[]{:T(128)S(6)} %select_n.79), kind=kOutput, calls=%fused_computation.12 | convolution fusion | flops 151191552 | bytes 2850820 | tf_op jit(solution)/shard_map/dot_general | solution.py:11
  108.5 5.5 %all-to-all-done.3 = bf16[8,4,16,384]{3,1,2,0:T(4,128)(2,1)} async-done(((bf16[8,4,16,384]{3,1,2,0:T(4,128)(2,1)}), bf16[8,4,16,384]{3,1,2,0:T(4,128)(2,1)}, u32[]{:S(2)}, u32[]{:S(2)}) %all-to-all-start.3) | async-done | bytes 393248 | tf_op jit(solution)/shard_map/all_to_all | solution.py:25
  114.1 1.1 copy.33
  115.2 1.0 convolution_convert_fusion
  116.3 2.6 %multiply_convert_fusion = (bf16[128,1536]{1,0:T(8,128)(2,1)}, bf16[128,1536]{1,0:T(8,128)(2,1)}) fusion(bf16[1,128,1536]{2,1,0:T(8,128)(2,1)S(1)} %copy-done.3, f32[128,1536]{1,0:T(8,128)S(1)} %copy-done.9, bf16[384,1536]{1,0:T(8,128)(2,1)} %collective-permute-done.2, bf16[128,1536]{1,0:T(8,128)(2,1)} %bitcast.4, s32[]{:T(128)S(6)} %select_n.80), kind=kOutput, calls=%fused_computation.43 | convolution fusion | flops 152961024 | bytes 3244036 | tf_op jit(solution)/shard_map/dot_general | solution.py:11
  118.9 1.2 copy.28
  120.9 3.5 %all-to-all-start.4 = ((bf16[8,4,48,128]{3,2,1,0:T(8,128)(2,1)}), bf16[8,4,48,128]{3,2,1,0:T(8,128)(2,1)S(1)}, u32[]{:S(2)}, u32[]{:S(2)}) async-start(bf16[8,4,48,128]{3,2,1,0:T(8,128)(2,1)} %copy.29), calls=%async_computation.4 | async-start | bytes 786432 | tf_op jit(solution)/shard_map/all_to_all | solution.py:88
  124.4 2.1 %fusion.12 = bf16[128,384]{1,0:T(8,128)(2,1)S(1)} fusion(bf16[1536,128]{1,0:T(8,128)(2,1)} %convolution_convert_fusion, bf16[384,1536]{1,0:T(8,128)(2,1)} %param.7, f32[128,1536]{1,0:T(8,128)} %bitcast_convert_fusion, s32[]{:T(128)S(6)} %select_n.77, f32[128,384]{1,0:T(8,128)S(1)} %fusion.90, bf16[128,1536]{1,0:T(8,128)(2,1)} %get-tuple-element.15), kind=kOutput, calls=%fused_computation.36 | convolution fusion | flops 151584768 | bytes 2162692 | tf_op jit(solution)/shard_map/dot_general | solution.py:11
  126.5 1.8 %fusion.13 = bf16[128,384]{1,0:T(8,128)(2,1)S(1)} fusion(bf16[1536,128]{1,0:T(8,128)(2,1)S(1)} %copy-done.7, bf16[384,1536]{1,0:T(8,128)(2,1)} %collective-permute-done, f32[128,1536]{1,0:T(8,128)S(1)} %copy-done.8, s32[]{:T(128)S(6)} %select_n.78, f32[128,384]{1,0:T(8,128)S(1)} %copy-done.13, bf16[128,1536]{1,0:T(8,128)(2,1)S(1)} %copy-done.15), kind=kOutput, calls=%fused_computation.37 | convolution fusion | flops 151584768 | bytes 2162692 | tf_op jit(solution)/shard_map/dot_general | solution.py:11
  128.3 2.5 %fusion.14 = bf16[128,384]{1,0:T(8,128)(2,1)} fusion(bf16[1536,128]{1,0:T(8,128)(2,1)S(1)} %copy-done.7, bf16[384,1536]{1,0:T(8,128)(2,1)} %collective-permute-done.1, f32[128,1536]{1,0:T(8,128)S(1)} %copy-done.8, s32[]{:T(128)S(6)} %select_n.79, f32[128,384]{1,0:T(8,128)S(1)} %copy-done.12, bf16[128,1536]{1,0:T(8,128)(2,1)S(1)} %copy-done.15), kind=kOutput, calls=%fused_computation.38 | convolution fusion | flops 151584768 | bytes 2162692 | tf_op jit(solution)/shard_map/dot_general | solution.py:11
  131.2 1.8 %fusion.8 = f32[128,384]{1,0:T(8,128)S(1)} fusion(bf16[384,1536]{1,0:T(8,128)(2,1)} %collective-permute-done.5, f32[128,1536]{1,0:T(8,128)S(1)} %copy-done.8, s32[]{:T(128)S(6)} %select_n.80, bf16[128,1536]{1,0:T(8,128)(2,1)S(1)} %copy-done.15, bf16[1,128,1536]{2,1,0:T(8,128)(2,1)S(1)} %copy-done.1), kind=kOutput, calls=%fused_computation.25 | convolution fusion | flops 151486464 | bytes 2064388 | tf_op jit(solution)/shard_map/dot_general | solution.py:11
  133.0 1.8 %fusion.15 = bf16[128,384]{1,0:T(8,128)(2,1)S(1)} fusion(f32[128,384]{1,0:T(8,128)S(1)} %fusion.8, bf16[1536,128]{1,0:T(8,128)(2,1)S(1)} %copy-done.7, bf16[384,1536]{1,0:T(8,128)(2,1)} %collective-permute-done.2), kind=kOutput, calls=%fused_computation.39 | convolution fusion | flops 151093248 | bytes 1867776 | tf_op jit(solution)/shard_map/dot_general | solution.py:11
  134.8 2.6 %convolution_add_fusion.7 = f32[128,1536]{1,0:T(8,128)} fusion(f32[128,1536]{1,0:T(8,128)S(1)} %fusion.39, bf16[384,1536]{1,0:T(8,128)(2,1)} %collective-permute-done.3, bf16[128,1536]{1,0:T(8,128)(2,1)S(1)} %copy-done.5, s32[]{:T(128)S(6)} %select_n.78), kind=kOutput, calls=%fused_computation.10 | convolution fusion | flops 151191552 | bytes 2850820 | tf_op jit(solution)/shard_map/dot_general | solution.py:11
  137.6 1.3 fusion.51
  138.9 1.3 convolution_add_fusion.4
  140.2 1.3 convolution_add_fusion.3
  141.9 1.3 fusion.48
  143.2 1.3 fusion.1
  144.5 2.1 %fusion.2 = bf16[192,1536]{1,0:T(8,128)(2,1)} fusion(f32[192,1536]{1,0:T(8,128)S(1)} %fusion.1, bf16[128,1536]{1,0:T(8,128)(2,1)} %collective-permute-done.14, bf16[8,192,128]{2,1,0:T(8,128)(2,1)S(1)} %bitcast.137, s32[]{:T(128)S(6)} %select_n.93), kind=kOutput, calls=%fused_computation.7 | convolution fusion | flops 76087296 | bytes 2211844 | tf_op jit(solution)/shard_map/dot_general | solution.py:11
  146.7 3.6 %all-to-all-start.5 = ((bf16[4,48,1536]{2,1,0:T(8,128)(2,1)}), bf16[4,48,1536]{2,1,0:T(8,128)(2,1)S(1)}, u32[]{:S(2)}, u32[]{:S(2)}) async-start(bf16[4,48,1536]{2,1,0:T(8,128)(2,1)} %bitcast.36), calls=%async_computation.5 | async-start | bytes 1179648 | tf_op jit(solution)/shard_map/all_to_all | solution.py:98
  150.3 0.9 pad_maximum_fusion.2
  151.7 2.4 %fusion.5 = bf16[1,128,1536]{2,1,0:T(8,128)(2,1)} fusion(f32[128,1536]{1,0:T(8,128)S(1)} %convolution_add_fusion.6, bf16[384,1536]{1,0:T(8,128)(2,1)} %collective-permute-done.5, bf16[128,1536]{1,0:T(8,128)(2,1)S(1)} %copy-done.6, s32[]{:T(128)S(6)} %select_n.80), kind=kOutput, calls=%fused_computation.19 | convolution fusion | flops 151388160 | bytes 2457604 | tf_op jit(solution)/shard_map/dot_general | solution.py:11
  154.8 12.2 %all-to-all-done.5 = bf16[4,48,1536]{2,1,0:T(8,128)(2,1)S(1)} async-done(((bf16[4,48,1536]{2,1,0:T(8,128)(2,1)}), bf16[4,48,1536]{2,1,0:T(8,128)(2,1)S(1)}, u32[]{:S(2)}, u32[]{:S(2)}) %all-to-all-start.5) | async-done | bytes 589856 | tf_op jit(solution)/shard_map/all_to_all | solution.py:98
  (79 shorter events, 11.2 us)
Async XLA Ops:
  0.6 3.6 %copy-start = (bf16[1,128,128]{2,1,0:T(8,128)(2,1)S(1)}, bf16[1,128,128]{2,1,0:T(8,128)(2,1)}, u32[]{:S(2)}) copy-start(bf16[1,128,128]{2,1,0:T(8,128)(2,1)} %param.9) | copy-start | bytes 98308
  0.6 11.6 %copy-start.3 = (bf16[1,128,1536]{2,1,0:T(8,128)(2,1)S(1)}, bf16[1,128,1536]{2,1,0:T(8,128)(2,1)}, u32[]{:S(2)}) copy-start(bf16[1,128,1536]{2,1,0:T(8,128)(2,1)} %param.6) | copy-start | bytes 1179652
  0.7 14.5 %copy-start.1 = (bf16[1,128,1536]{2,1,0:T(8,128)(2,1)S(1)}, bf16[1,128,1536]{2,1,0:T(8,128)(2,1)}, u32[]{:S(2)}) copy-start(bf16[1,128,1536]{2,1,0:T(8,128)(2,1)} %param.11) | copy-start | bytes 1179652
  0.7 14.5 %copy-start.2 = (bf16[384,1536]{1,0:T(8,128)(2,1)S(1)}, bf16[384,1536]{1,0:T(8,128)(2,1)}, u32[]{:S(2)}) copy-start(bf16[384,1536]{1,0:T(8,128)(2,1)} %param.8) | copy-start | bytes 3538948
  0.7 46.5 %collective-permute-start.6 = (bf16[128,1536]{1,0:T(8,128)(2,1)}, bf16[128,1536]{1,0:T(8,128)(2,1)}, u32[]{:S(2)}, u32[]{:S(2)}) collective-permute-start(bf16[128,1536]{1,0:T(8,128)(2,1)} %bitcast.127), channel_id=1, source_target_pairs={{0,1},{1,0},{2,3},{3,2},{4,5},{5,4},{6,7},{7,6},{8,9},{9,8},{10,11... | collective-permute-start | bytes 1179656 | tf_op jit(solution)/shard_map/ppermute | solution.py:16
  1.2 44.0 %collective-permute-start.9 = (bf16[128,1536]{1,0:T(8,128)(2,1)}, bf16[128,1536]{1,0:T(8,128)(2,1)}, u32[]{:S(2)}, u32[]{:S(2)}) collective-permute-start(bf16[128,1536]{1,0:T(8,128)(2,1)} %bitcast.128), channel_id=1, source_target_pairs={{0,2},{1,3},{2,0},{3,1},{4,6},{5,7},{6,4},{7,5},{8,10},{9,11},{10,... | collective-permute-start | bytes 1179656 | tf_op jit(solution)/shard_map/ppermute | solution.py:16
  3.8 84.0 %collective-permute-start.3 = (bf16[384,1536]{1,0:T(8,128)(2,1)}, bf16[384,1536]{1,0:T(8,128)(2,1)}, u32[]{:S(2)}, u32[]{:S(2)}) collective-permute-start(bf16[384,1536]{1,0:T(8,128)(2,1)} %param.8), channel_id=1, source_target_pairs={{0,1},{1,0},{2,3},{3,2},{4,5},{5,4},{6,7},{7,6},{8,9},{9,8},{10,11... | collective-permute-start | bytes 3538952 | tf_op jit(solution)/shard_map/ppermute | solution.py:16
  3.9 82.0 %collective-permute-start.4 = (bf16[384,1536]{1,0:T(8,128)(2,1)}, bf16[384,1536]{1,0:T(8,128)(2,1)S(1)}, u32[]{:S(2)}, u32[]{:S(2)}) collective-permute-start(bf16[384,1536]{1,0:T(8,128)(2,1)} %param.8), channel_id=1, source_target_pairs={{0,2},{1,3},{2,0},{3,1},{4,6},{5,7},{6,4},{7,5},{8,10},{9,11},{10,... | collective-permute-start | bytes 3538952 | tf_op jit(solution)/shard_map/ppermute | solution.py:16
  6.2 46.0 %all-to-all-start = ((bf16[8,16,1536]{2,1,0:T(8,128)(2,1)}), bf16[8,16,1536]{2,1,0:T(8,128)(2,1)}, u32[]{:S(2)}, u32[]{:S(2)}) async-start(bf16[8,16,1536]{2,1,0:T(8,128)(2,1)} %bitcast.139), calls=%async_computation | async-start | bytes 786432 | tf_op jit(solution)/shard_map/all_to_all | solution.py:25
  13.7 29.6 %collective-permute-start.7 = (bf16[128,768]{1,0:T(8,128)(2,1)}, bf16[128,768]{1,0:T(8,128)(2,1)}, u32[]{:S(2)}, u32[]{:S(2)}) collective-permute-start(bf16[128,768]{1,0:T(8,128)(2,1)} %pad_maximum_fusion.3), channel_id=1, source_target_pairs={{0,2},{1,3},{2,0},{3,1},{4,6},{5,7},{6,4},{7,5},{8,10},{9,11},{10,... | collective-permute-start | bytes 589832 | tf_op jit(solution)/shard_map/ppermute | solution.py:16
  45.1 3.9 %collective-permute-start.8 = (bf16[128,768]{1,0:T(8,128)(2,1)S(1)}, bf16[128,768]{1,0:T(8,128)(2,1)S(1)}, u32[]{:S(2)}, u32[]{:S(2)}) collective-permute-start(bf16[128,768]{1,0:T(8,128)(2,1)S(1)} %pad_maximum_fusion.4), channel_id=1, source_target_pairs={{0,1},{1,0},{2,3},{3,2},{4,5},{5,4},{6,7},{7,6},{8,9},{9,8},{10,11... | collective-permute-start | bytes 589832 | tf_op jit(solution)/shard_map/ppermute | solution.py:16
  45.2 5.4 %collective-permute-start.10 = (bf16[128,1536]{1,0:T(8,128)(2,1)}, bf16[128,1536]{1,0:T(8,128)(2,1)S(1)}, u32[]{:S(2)}, u32[]{:S(2)}) collective-permute-start(bf16[128,1536]{1,0:T(8,128)(2,1)} %collective-permute-done.9), channel_id=1, source_target_pairs={{0,1},{1,0},{2,3},{3,2},{4,5},{5,4},{6,7},{7,6},{8,9},{9,8},{10,11... | collective-permute-start | bytes 1179656 | tf_op jit(solution)/shard_map/ppermute | solution.py:16
  47.2 40.2 %collective-permute-start.1 = (bf16[384,1536]{1,0:T(8,128)(2,1)}, bf16[384,1536]{1,0:T(8,128)(2,1)}, u32[]{:S(2)}, u32[]{:S(2)}) collective-permute-start(bf16[384,1536]{1,0:T(8,128)(2,1)} %param.7), channel_id=1, source_target_pairs={{0,2},{1,3},{2,0},{3,1},{4,6},{5,7},{6,4},{7,5},{8,10},{9,11},{10,... | collective-permute-start | bytes 3538952 | tf_op jit(solution)/shard_map/ppermute | solution.py:16
  50.6 0.8 copy-start.10
  52.2 8.1 %copy-start.14 = (bf16[16,8,8]{0,2,1:T(8,128)(2,1)S(1)}, bf16[16,8,8]{0,2,1:T(8,128)(2,1)}, u32[]{:S(2)}) copy-start(bf16[16,8,8]{0,2,1:T(8,128)(2,1)} %param.10) | copy-start | bytes 6148
  52.2 29.0 %all-to-all-start.2 = ((bf16[32,16,384]{2,1,0:T(8,128)(2,1)}), bf16[32,16,384]{2,1,0:T(8,128)(2,1)}, u32[]{:S(2)}, u32[]{:S(2)}) async-start(bf16[32,16,384]{2,1,0:T(8,128)(2,1)} %bitcast.140), calls=%async_computation.2 | async-start | bytes 786432 | tf_op jit(solution)/shard_map/all_to_all | solution.py:66
  57.3 15.4 %collective-permute-start.11 = (bf16[128,1536]{1,0:T(8,128)(2,1)S(1)}, bf16[128,1536]{1,0:T(8,128)(2,1)}, u32[]{:S(2)}, u32[]{:S(2)}) collective-permute-start(bf16[128,1536]{1,0:T(8,128)(2,1)S(1)} %bitcast.129), channel_id=1, source_target_pairs={{0,4},{4,0},{8,12},{12,8},{16,20},{20,16},{24,28},{28,24},{1,5},{5... | collective-permute-start | bytes 1179656 | tf_op jit(solution)/shard_map/ppermute | solution.py:16
  59.0 22.2 %collective-permute-start.13 = (bf16[128,1536]{1,0:T(8,128)(2,1)}, bf16[128,1536]{1,0:T(8,128)(2,1)}, u32[]{:S(2)}, u32[]{:S(2)}) collective-permute-start(bf16[128,1536]{1,0:T(8,128)(2,1)} %collective-permute-done.9), channel_id=1, source_target_pairs={{0,4},{4,0},{8,12},{12,8},{16,20},{20,16},{24,28},{28,24},{1,5},{5... | collective-permute-start | bytes 1179656 | tf_op jit(solution)/shard_map/ppermute | solution.py:16
  72.7 31.5 %collective-permute-start = (bf16[384,1536]{1,0:T(8,128)(2,1)}, bf16[384,1536]{1,0:T(8,128)(2,1)}, u32[]{:S(2)}, u32[]{:S(2)}) collective-permute-start(bf16[384,1536]{1,0:T(8,128)(2,1)} %param.7), channel_id=1, source_target_pairs={{0,1},{1,0},{2,3},{3,2},{4,5},{5,4},{6,7},{7,6},{8,9},{9,8},{10,11... | collective-permute-start | bytes 3538952 | tf_op jit(solution)/shard_map/ppermute | solution.py:16
  81.2 62.0 %collective-permute-start.12 = (bf16[128,1536]{1,0:T(8,128)(2,1)}, bf16[128,1536]{1,0:T(8,128)(2,1)}, u32[]{:S(2)}, u32[]{:S(2)}) collective-permute-start(bf16[128,1536]{1,0:T(8,128)(2,1)} %collective-permute-done.11), channel_id=1, source_target_pairs={{0,1},{1,0},{2,3},{3,2},{4,5},{5,4},{6,7},{7,6},{8,9},{9,8},{10,11... | collective-permute-start | bytes 1179656 | tf_op jit(solution)/shard_map/ppermute | solution.py:16
  81.2 17.2 %all-to-all-start.1 = ((bf16[8,16,1536]{2,1,0:T(8,128)(2,1)}), bf16[8,16,1536]{2,1,0:T(8,128)(2,1)}, u32[]{:S(2)}, u32[]{:S(2)}) async-start(bf16[8,16,1536]{2,1,0:T(8,128)(2,1)} %copy.23), calls=%async_computation.1 | async-start | bytes 786432 | tf_op jit(solution)/shard_map/all_to_all | solution.py:25
  86.0 58.6 %collective-permute-start.14 = (bf16[128,1536]{1,0:T(8,128)(2,1)}, bf16[128,1536]{1,0:T(8,128)(2,1)}, u32[]{:S(2)}, u32[]{:S(2)}) collective-permute-start(bf16[128,1536]{1,0:T(8,128)(2,1)} %collective-permute-done.13), channel_id=1, source_target_pairs={{0,1},{1,0},{2,3},{3,2},{4,5},{5,4},{6,7},{7,6},{8,9},{9,8},{10,11... | collective-permute-start | bytes 1179656 | tf_op jit(solution)/shard_map/ppermute | solution.py:16
  87.4 43.8 %collective-permute-start.5 = (bf16[384,1536]{1,0:T(8,128)(2,1)S(1)}, bf16[384,1536]{1,0:T(8,128)(2,1)}, u32[]{:S(2)}, u32[]{:S(2)}) collective-permute-start(bf16[384,1536]{1,0:T(8,128)(2,1)S(1)} %collective-permute-done.4), channel_id=1, source_target_pairs={{0,1},{1,0},{2,3},{3,2},{4,5},{5,4},{6,7},{7,6},{8,9},{9,8},{10,11... | collective-permute-start | bytes 3538952 | tf_op jit(solution)/shard_map/ppermute | solution.py:16
  87.7 28.5 %collective-permute-start.2 = (bf16[384,1536]{1,0:T(8,128)(2,1)}, bf16[384,1536]{1,0:T(8,128)(2,1)}, u32[]{:S(2)}, u32[]{:S(2)}) collective-permute-start(bf16[384,1536]{1,0:T(8,128)(2,1)} %collective-permute-done.1), channel_id=1, source_target_pairs={{0,1},{1,0},{2,3},{3,2},{4,5},{5,4},{6,7},{7,6},{8,9},{9,8},{10,11... | collective-permute-start | bytes 3538952 | tf_op jit(solution)/shard_map/ppermute | solution.py:16
  98.4 15.7 %all-to-all-start.3 = ((bf16[8,4,16,384]{3,1,2,0:T(4,128)(2,1)}), bf16[8,4,16,384]{3,1,2,0:T(4,128)(2,1)}, u32[]{:S(2)}, u32[]{:S(2)}) async-start(bf16[8,4,16,384]{3,1,2,0:T(4,128)(2,1)} %copy.27), calls=%async_computation.3 | async-start | bytes 786432 | tf_op jit(solution)/shard_map/all_to_all | solution.py:25
  114.1 2.2 %copy-start.9 = (f32[128,1536]{1,0:T(8,128)S(1)}, f32[128,1536]{1,0:T(8,128)}, u32[]{:S(2)}) copy-start(f32[128,1536]{1,0:T(8,128)} %convolution_add_fusion.9) | copy-start | bytes 2359300
  120.9 16.5 %all-to-all-start.4 = ((bf16[8,4,48,128]{3,2,1,0:T(8,128)(2,1)}), bf16[8,4,48,128]{3,2,1,0:T(8,128)(2,1)S(1)}, u32[]{:S(2)}, u32[]{:S(2)}) async-start(bf16[8,4,48,128]{3,2,1,0:T(8,128)(2,1)} %copy.29), calls=%async_computation.4 | async-start | bytes 786432 | tf_op jit(solution)/shard_map/all_to_all | solution.py:88
  124.4 2.1 %copy-start.7 = (bf16[1536,128]{1,0:T(8,128)(2,1)S(1)}, bf16[1536,128]{1,0:T(8,128)(2,1)}, u32[]{:S(2)}) copy-start(bf16[1536,128]{1,0:T(8,128)(2,1)} %convolution_convert_fusion) | copy-start | bytes 1179652
  124.4 2.1 %copy-start.8 = (f32[128,1536]{1,0:T(8,128)S(1)}, f32[128,1536]{1,0:T(8,128)}, u32[]{:S(2)}) copy-start(f32[128,1536]{1,0:T(8,128)} %bitcast_convert_fusion) | copy-start | bytes 2359300
  124.4 2.1 %copy-start.13 = (f32[128,384]{1,0:T(8,128)S(1)}, f32[128,384]{1,0:T(8,128)}, u32[]{:S(2)}) copy-start(f32[128,384]{1,0:T(8,128)} %fusion.88) | copy-start | bytes 589828
  124.4 2.1 %copy-start.15 = (bf16[128,1536]{1,0:T(8,128)(2,1)S(1)}, bf16[128,1536]{1,0:T(8,128)(2,1)}, u32[]{:S(2)}) copy-start(bf16[128,1536]{1,0:T(8,128)(2,1)} %get-tuple-element.15) | copy-start | bytes 1179652
  126.5 1.8 %copy-start.12 = (f32[128,384]{1,0:T(8,128)S(1)}, f32[128,384]{1,0:T(8,128)}, u32[]{:S(2)}) copy-start(f32[128,384]{1,0:T(8,128)} %fusion.86) | copy-start | bytes 589828
  128.3 2.5 %copy-start.5 = (bf16[128,1536]{1,0:T(8,128)(2,1)S(1)}, bf16[128,1536]{1,0:T(8,128)(2,1)}, u32[]{:S(2)}) copy-start(bf16[128,1536]{1,0:T(8,128)(2,1)} %get-tuple-element.14) | copy-start | bytes 1179652
  140.2 1.4 copy-start.11
  146.7 4.6 %copy-start.4 = (f32[128,1536]{1,0:T(8,128)S(1)}, f32[128,1536]{1,0:T(8,128)}, u32[]{:S(2)}) copy-start(f32[128,1536]{1,0:T(8,128)} %convolution_add_fusion.7) | copy-start | bytes 2359300
  146.7 4.6 %copy-start.6 = (bf16[128,1536]{1,0:T(8,128)(2,1)S(1)}, bf16[128,1536]{1,0:T(8,128)(2,1)}, u32[]{:S(2)}) copy-start(bf16[128,1536]{1,0:T(8,128)(2,1)} %get-tuple-element.14) | copy-start | bytes 1179652
  146.7 20.4 %all-to-all-start.5 = ((bf16[4,48,1536]{2,1,0:T(8,128)(2,1)}), bf16[4,48,1536]{2,1,0:T(8,128)(2,1)S(1)}, u32[]{:S(2)}, u32[]{:S(2)}) async-start(bf16[4,48,1536]{2,1,0:T(8,128)(2,1)} %bitcast.36), calls=%async_computation.5 | async-start | bytes 1179648 | tf_op jit(solution)/shard_map/all_to_all | solution.py:98

commit v2 on v0

v2 whole, which is shorter than its diff:
```python
import functools

import jax
import jax.numpy as jnp
from jax import lax
from jax.experimental import pallas as pl
from jax.experimental.pallas import tpu as pltpu
from jax.sharding import PartitionSpec as P

F32 = jnp.float32
BF16 = jnp.bfloat16
VMEM = pl.BlockSpec(memory_space=pltpu.VMEM)
SMEM = pl.BlockSpec(memory_space=pltpu.SMEM)
MIB = 1024 * 1024


def dot(a, b, ca, cb):
    return lax.dot_general(a, b, (((ca,), (cb,)), ((), ())), preferred_element_type=F32)


def swap(x, axis, bit):
    n = lax.axis_size(axis)
    return lax.ppermute(x, axis, [(i, i ^ bit) for i in range(n)])


def after(x, *others):
    return lax.optimization_barrier((x, others))[0]


def relative(x, index):
    bit = 1
    while bit < x.shape[0]:
        flipped = x.reshape((-1, 2, bit) + x.shape[1:])[:, ::-1].reshape(x.shape)
        x = jnp.where(index & bit != 0, flipped, x)
        bit *= 2
    return x


def spread(x):
    return lax.all_to_all(x, "seq", split_axis=0, concat_axis=0, tiled=True)


def aligned(start, step):
    return pl.multiple_of(start * step, step)


def call(kernel, outs, *args, flops=0, scratch=(), room=60):
    nbytes = sum(x.size * x.dtype.itemsize for x in args + tuple(outs))
    return pl.pallas_call(
        kernel,
        out_shape=list(outs),
        in_specs=[SMEM if x.dtype == jnp.int32 else VMEM for x in args],
        out_specs=[VMEM] * len(outs),
        scratch_shapes=list(scratch),
        compiler_params=pltpu.CompilerParams(vmem_limit_bytes=room * MIB),
        cost_estimate=pl.CostEstimate(flops=flops, bytes_accessed=nbytes, transcendentals=0),
    )(*args)


def shape(dims, dtype=BF16):
    return jax.ShapeDtypeStruct(dims, dtype)


def grad_kernel(part, where, w, tok, cot, near, far, side, *refs):
    me = where[0]
    width = cot.shape[1]
    out = refs[-1]
    if len(refs) > 1:
        out[:, :, 0] = refs[0][...]
    pairs = (
        (cot[...], tok[:, pl.ds(aligned(me, part), part)]),
        (near[:, :width], near[:, width:]),
        (far[:, part : part + width], far[:, :part]),
        (side[:, part : part + width], side[:, part + width :]),
    )
    for r, (x, t) in enumerate(pairs):
        grad = (dot(x, w[...], 1, 1) * jax.nn.silu(t.astype(F32))).astype(BF16)
        if len(refs) > 1:
            offs = out.shape[3]
            for s in range(out.shape[0]):
                out[s, me ^ r, 1] = grad[s * offs : (s + 1) * offs]
        else:
            out[me ^ r] = grad


def gate_kernel(part, piece, tile, where, mix, w0, w1, w2, w3, tok, mon_out, gated_out, t_out, held):
    me, z = where[0], where[1]
    rows, width = tok.shape
    if len(mix.shape) == 5:
        lhs = [mix[:, pl.ds(me ^ r, 1), 0].reshape(rows, part) for r in range(4)]
    else:
        lhs = [mix[:, pl.ds(aligned(me ^ r, part), part)] for r in range(4)]
    for c in range(0, width, tile):
        cols = slice(c, c + tile)
        total = dot(lhs[0], w0[:, cols], 1, 0)
        for x, w in zip(lhs[1:], (w1, w2, w3)):
            total += dot(x, w[:, cols], 1, 0)
        mon = total.astype(BF16)
        mon_out[:, cols] = mon
        wide = tok[:, cols].astype(F32)
        gated = (mon.astype(F32) * jax.nn.silu(wide)).astype(BF16)
        gated_out[:, cols] = gated
        held[cols, :] = gated.T
    if len(t_out.shape) == 3:
        near, outer = t_out.shape[0], t_out.shape[1] // piece
        for i in range(near):
            for rel in range(outer):
                src = (rel ^ z) * near + i
                t_out[i, rel * piece : (rel + 1) * piece, :] = held[pl.ds(aligned(src, piece), piece), :]
    else:
        t_out[...] = held[...]


def carry_kernel(part, where, back, first, term, w0, w1, w2, w3, out):
    me = where[0]
    if len(back.shape) == 4:
        nseq, ndp, offs, _ = back.shape
        parts = [back[:, d].reshape(nseq * offs, part) for d in range(ndp)]
        back = jnp.concatenate(parts, axis=1)
    else:
        back = back[...]
    grad = dot(first[...], back, 0, 0).astype(BF16)
    for r, w in enumerate((w0, w1, w2, w3)):
        cols = pl.ds(aligned(me ^ r, part), part)
        out[:, cols] = (dot(grad, w[...], 1, 1) + term[:, cols]).astype(BF16)


def last_kernel(part, where, gated, mon, tok, cot, w0, w1, w2, w3, w4, w5, mixed, out):
    me = where[0]
    weights = (w0, w1, w2, w3, w4, w5)
    half = part // 2
    for r, some in enumerate(((w0,), (w1,), (w2, w3), (w4, w5))):
        cols = pl.ds(aligned(me ^ r, part), part)
        wide = tok[:, cols].astype(F32)
        sigma = jax.nn.sigmoid(wide)
        slope = sigma * (1.0 + wide * (1.0 - sigma))
        grad = jnp.concatenate([dot(cot[...], w[...], 1, 1) for w in some], axis=1)
        out[:, cols] = grad * mon[:, cols].astype(F32) * slope
    lhs = [gated[:, pl.ds(aligned(me ^ r, part), part)] for r in range(4)]
    lhs = lhs[:2] + [x[:, h : h + half] for x in lhs[2:] for h in (0, half)]
    for c in range(0, mixed.shape[1], part):
        cols = slice(c, c + part)
        total = dot(lhs[0], w0[:, cols], 1, 0)
        for x, w in zip(lhs[1:], weights[1:]):
            total += dot(x, w[:, cols], 1, 0)
        mixed[:, cols] = total.astype(BF16)


def weight_kernel(tile, starts, where, got, *refs):
    cots, out = refs[: len(starts)], refs[len(starts) :]
    width = out[0].shape[-1]
    here = where[2]
    for c in range(0, width, tile):
        cols = slice(c, c + tile)
        total = 0.0
        for r, (cot, start) in enumerate(zip(cots, starts)):
            total += dot(got[here ^ r], cot[:, c + start : c + start + tile], 1, 0)
        if len(out) == 1:
            out[0][:, cols] = total
            continue
        kept, sent = out
        n, piece, _ = kept.shape
        for i in range(n):
            kept[i, :, cols] = total[2 * i * piece : (2 * i + 1) * piece]
            sent[i, :, cols] = total[(2 * i + 1) * piece : (2 * i + 2) * piece].astype(BF16)


def on_device(tokens, w_in, w_out, first_factor, second_factor, cotangent):
    inputs = tokens[0]
    upstream = cotangent[0]
    first = first_factor[0]
    rows, width = inputs.shape
    nseq = lax.axis_size("seq")
    ndp = lax.axis_size("dp")
    me = lax.axis_index("dp")
    my_s = lax.axis_index("seq")
    flat = my_s * ndp + me
    part = width // ndp
    offs = rows // nseq
    piece = width // (nseq * ndp)
    flops = 2 * rows * width * width

    def columns(x, r):
        return lax.dynamic_slice_in_dim(x, (me ^ r) * part, part, axis=1)

    def unchunk(x):
        return x.transpose(0, 2, 1, 3).reshape(rows, width)

    def halve(x, bit, other=()):
        x = x.reshape(x.shape[0] // 2, 2, piece, width)
        got = swap(x[:, 1].astype(BF16), "seq", 2 * bit)
        got, other = lax.optimization_barrier((got, other))
        return x[:, 0] + got.astype(F32), other

    join = lax.optimization_barrier
    near = 2 * ndp
    outer = nseq // 2
    here = flat % near
    where = jnp.stack([me, flat // near, here]).astype(jnp.int32)

    def cut(x):
        return x.reshape(nseq, offs, ndp, part).transpose(0, 2, 1, 3)

    def exchange(x):
        flat_x = x.reshape((nseq * ndp,) + x.shape[2:])
        flat_x = lax.all_to_all(
            flat_x, ("seq", "dp"), split_axis=0, concat_axis=0, tiled=True
        )
        return flat_x.reshape(x.shape)

    cot_far = swap(jnp.concatenate([columns(inputs, 2), upstream, columns(inputs, 3)], axis=1), "dp", 2)
    cot_near = swap(jnp.concatenate([upstream, columns(inputs, 1)], axis=1), "dp", 1)
    mix, cot_near = join((dot(first, inputs, 1, 0).astype(BF16), cot_near))
    arrived = exchange(cut(mix))
    cot_side = swap(cot_far, "dp", 1)
    arrived, cot_near, cot_far, cot_side, w_late, up = join(
        (arrived, cot_near, cot_far, cot_side, w_in, upstream)
    )

    mix = jnp.einsum("sab,bjsd->ajsd", second_factor, arrived, preferred_element_type=F32)
    w_far = swap(w_late, "dp", 2)
    w_near = swap(w_late, "dp", 1)
    pair = jnp.concatenate([up, cot_far[:, part : part + width]], axis=1)
    pair = swap(pair, "seq", 1)
    pair_side = swap(pair, "dp", 1)
    w_side = swap(w_far, "dp", 1)
    mix = mix.astype(BF16)
    split = offs % 16 == 0 and piece % 16 == 0
    (both,) = call(
        functools.partial(grad_kernel, part),
        [shape((nseq, ndp, 2, offs, part) if split else (ndp, rows, part))],
        where,
        w_out,
        inputs,
        upstream,
        cot_near,
        cot_far,
        cot_side,
        *([mix] if split else []),
        flops=flops,
        room=40,
    )
    if not split:
        both = both.reshape(ndp, nseq, offs, part).transpose(1, 0, 2, 3)
        both = jnp.stack([mix, both], axis=2)
    both = exchange(both)
    both, w_far, w_near, w_side, pair, pair_side, w_late = join(
        (both, w_far, w_near, w_side, pair, pair_side, w_out)
    )
    out_a = swap(w_late[: part // 2], "dp", 2)
    out_b = swap(w_late[part // 2 :], "dp", 2)

    mix = both if split else unchunk(both[:, :, 0])
    back = jnp.einsum("sab,ajsc->bjsc", second_factor, both[:, :, 1], preferred_element_type=F32)
    back = back.astype(BF16)
    w_ins = (w_in, w_near, w_far, w_side)
    monarch, gated, turned = call(
        functools.partial(gate_kernel, part, piece, part),
        [
            shape((rows, width)),
            shape((rows, width)),
            shape((near, outer * piece, rows) if split else (width, rows)),
        ],
        where,
        mix,
        *w_ins,
        inputs,
        flops=flops,
        scratch=[pltpu.VMEM((width, rows), BF16)],
    )
    if not split:
        turned = relative(turned.reshape(outer, near, piece, rows), flat // near)
        turned = turned.transpose(1, 0, 2, 3).reshape(near, outer * piece, rows)
    groups = [[z * near + i for i in range(near)] for z in range(outer)]
    got = lax.all_to_all(
        turned, ("seq", "dp"), split_axis=0, concat_axis=0, tiled=True, axis_index_groups=groups
    )
    got, back, out_a = join((got, back, out_a))

    back = spread(back)
    halves = (outer // 2, piece, width)
    total = call(
        functools.partial(
            weight_kernel, part, (0, 0, part, part, 0, 0, width, width)
        ),
        [shape(halves, F32), shape(halves)] if split else [shape((outer * piece, width), F32)],
        where,
        got,
        upstream,
        cot_near,
        cot_far,
        cot_side,
        pair,
        pair_side,
        pair,
        pair_side,
        flops=flops,
    )
    if not split:
        total = total[0].reshape(outer // 2, 2, piece, width)
        total = (total[:, 0], total[:, 1].astype(BF16))
    kept, sent = total
    sent = swap(sent, "seq", 2)
    sent, back, out_b = join((sent, back, out_b))
    total = kept + sent.astype(F32)
    bit = 2

    w_outs = (
        w_out,
        swap(w_late, "dp", 1),
        out_a,
        out_b,
        swap(out_a, "dp", 1),
        swap(out_b, "dp", 1),
    )
    mixed, term = call(
        functools.partial(last_kernel, part),
        [shape((rows, width)), shape((rows, width), F32)],
        where,
        gated,
        monarch,
        inputs,
        upstream,
        *w_outs,
        flops=2 * flops,
        room=40,
    )
    if offs % 16 != 0:
        back = unchunk(back)
    (input_grad,) = call(
        functools.partial(carry_kernel, part),
        [shape((rows, width))],
        where,
        back,
        first,
        term,
        *w_ins,
        flops=flops,
        room=40,
    )
    ready = (mixed, input_grad)
    while total.shape[0] > 1:
        total, ready = halve(total, bit, ready)
        bit *= 2
    mixed, input_grad = ready
    weight_grad = total[0] / jnp.sqrt(F32(rows * nseq * ndp))
    return mixed[None], input_grad[None], weight_grad


def solution(mesh):
    placed = (
        P("dp", "seq", None),
        P("dp", None),
        P("dp", None),
        P("seq", None, None),
        P("seq", None, None),
        P("dp", "seq", None),
    )
    return jax.shard_map(
        on_device,
        mesh=mesh,
        in_specs=placed,
        out_specs=(P("dp", "seq", None), P("dp", "seq", None), P(("seq", "dp"), None)),
        check_vma=False,
    )
```

time: 240 us -> 126 us (0.53)
  waiting for transfers between devices: 151 us -> 52.4 us
  blocking collectives: 30.7 us -> 0 us
  starting transfers between devices: 9.08 us -> 32.5 us
  matrix products: 22.3 us -> 0.95 us
  Pallas kernels: 0 us -> 21.2 us
  between operations: 13.9 us -> 0.97 us
  local copies, waits for them, and re-layouts: 5.11 us -> 12.4 us
  other arithmetic: 7.94 us -> 5.05 us
    reduce_scatter x1 -> x0, waiting for transfers between devices: 89.1 us -> none  [on_device(): lax.psum_scatter(lax.dot_general(gated, upstream, (((0,), (0,)), ((), ())...]
    ppermute x0 -> x15, waiting for transfers between devices: none -> 41.4 us  [swap(): return lax.ppermute(x, axis, [(i, i ^ bit) for i in range(n)])]
    all_gather x2 -> x0, waiting for transfers between devices: 41.1 us -> none  [the longest x1 41.1 us: on_device(): lax.all_gather(w_in, 'dp', axis=0, tiled=True)]
    all_to_all x2 -> x0, blocking collectives: 30.7 us -> none  [the longest x1 15.7 us: on_device(): lax.all_to_all(second_mix, 'seq', split_axis=0, concat_axis=1, tiled=True)]
    dot_general x7 -> x3, matrix products: 22.3 us -> 0.95 us  [the longest x1 0.36 us: on_device(): jnp.einsum('sab,bjsd->ajsd', second_factor, arrived, preferred_element_ty...]
    pallas_call x0 -> x5, Pallas kernels: none -> 21.2 us  [call(): pl.pallas_call(kernel, out_shape=list(outs), in_specs=[SMEM if x.dtype ==...]
    ppermute x0 -> x15, starting transfers between devices: none -> 14.3 us  [swap(): return lax.ppermute(x, axis, [(i, i ^ bit) for i in range(n)])]
    all_to_all x2 -> x4, starting transfers between devices: 8.97 us -> 18.2 us  [the longest x2 9.28 us: exchange(): lax.all_to_all(flat_x, ('seq', 'dp'), split_axis=0, concat_axis=0, tiled=...]
  transfers between devices with their start and end apart: 5 -> 19, of which waited for: 4 -> 9; matrix products, arithmetic and copies ran while one was open for 14% -> 7% of each run, Pallas kernels for 0% -> 17%
where the time goes in v2:
time: 126 us; the launch traced here: 125 us
  waiting for transfers between devices  52.4 us (42%)
  starting transfers between devices  32.5 us (26%)
  Pallas kernels  21.2 us (17%)
  local copies, waits for them, and re-layouts  12.4 us (10%)
  other arithmetic  5.05 us (4%)
    ppermute x15, waiting for transfers between devices, swap(): return lax.ppermute(x, axis, [(i, i ^ bit) for i in range(n)])  41.4 us
    pallas_call x5, Pallas kernels, call(): pl.pallas_call(kernel, out_shape=list(outs), in_specs=[SMEM if x.dtype ==...  21.2 us
    ppermute x15, starting transfers between devices, swap(): return lax.ppermute(x, axis, [(i, i ^ bit) for i in range(n)])  14.3 us
    all_to_all x2, starting transfers between devices, exchange(): lax.all_to_all(flat_x, ('seq', 'dp'), split_axis=0, concat_axis=0, tiled=...  9.28 us
    all_to_all x1, waiting for transfers between devices, on_device(): lax.all_to_all(turned, ('seq', 'dp'), split_axis=0, concat_axis=0, tiled=...  8.48 us
    unnamed x57, local copies, waits for them, and re-layouts  6.14 us
    all_to_all x1, starting transfers between devices, spread(): return lax.all_to_all(x, 'seq', split_axis=0, concat_axis=0, tiled=True)  5.31 us
    all_to_all x1, starting transfers between devices, on_device(): lax.all_to_all(turned, ('seq', 'dp'), split_axis=0, concat_axis=0, tiled=...  3.58 us
  transfers between devices with their start and end apart: 19, of which 9 were waited for; matrix products, arithmetic and copies ran while one was open for 7% of the time, Pallas kernels for 17%

profile of v2, /device:TPU:0, one launch (start us, length us, event | category | flops | bytes accessed | tf_op | source)
XLA Modules:
  0.0 125.4 jit_solution(3798815016230892568)
XLA Ops:
  0.7 1.1 dynamic-slice_bitcast_fusion.1
  1.8 1.1 pad_maximum_fusion.2
  2.8 0.5 collective-permute-start
  3.4 0.9 pad_maximum_fusion.1
  4.2 2.5 %collective-permute-start.1 = (bf16[128,2304]{1,0:T(8,128)(2,1)}, bf16[128,2304]{1,0:T(8,128)(2,1)S(1)}, u32[]{:S(2)}, u32[]{:S(2)}) collective-permute-start(bf16[128,2304]{1,0:T(8,128)(2,1)} %pad_maximum_fusion.1), channel_id=1, source_target_pairs={{0,2},{1,3},{2,0},{3,1},{4,6},{5,7},{6,4},{7,5},{8,10},{9,11},{10,... | collective-permute-start | bytes 1769480 | tf_op jit(solution)/shard_map/ppermute | solution.py:23
  7.1 0.8 copy-done.12
  7.9 0.8 copy.14
  8.7 5.0 %all-to-all-start = ((bf16[32,16,384]{2,1,0:T(8,128)(2,1)}), bf16[32,16,384]{2,1,0:T(8,128)(2,1)S(1)}, u32[]{:S(2)}, u32[]{:S(2)}) async-start(bf16[32,16,384]{2,1,0:T(8,128)(2,1)} %bitcast.8), calls=%async_computation | async-start | bytes 786432 | tf_op jit(solution)/shard_map/all_to_all | solution.py:206
  13.8 9.8 %collective-permute-done.1.far.refs_2_ = bf16[128,2304]{1,0:T(8,128)(2,1)S(1)} collective-permute-done((bf16[128,2304]{1,0:T(8,128)(2,1)}, bf16[128,2304]{1,0:T(8,128)(2,1)S(1)}, u32[]{:S(2)}, u32[]{:S(2)}) %collective-permute-start.1) | collective-permute-done | bytes 589856 | tf_op jit(solution)/shard_map/ppermute | solution.py:23
  23.6 2.0 %collective-permute-done.2.side.refs_3_ = bf16[128,2304]{1,0:T(8,128)(2,1)S(1)} collective-permute-done((bf16[128,2304]{1,0:T(8,128)(2,1)S(1)}, bf16[128,2304]{1,0:T(8,128)(2,1)S(1)}, u32[]{:S(2)}, u32[]{:S(2)}) %collective-permute-start.2) | collective-permute-done | bytes 589856 | tf_op jit(solution)/shard_map/ppermute | solution.py:23
  25.6 0.8 copy-done.10
  26.5 0.5 all-to-all-done
  26.9 1.8 %collective-permute-start.3 = (bf16[384,1536]{1,0:T(8,128)(2,1)S(1)}, bf16[384,1536]{1,0:T(8,128)(2,1)}, u32[]{:S(2)}, u32[]{:S(2)}) collective-permute-start(bf16[384,1536]{1,0:T(8,128)(2,1)S(1)} %copy-done.5), channel_id=1, source_target_pairs={{0,2},{1,3},{2,0},{3,1},{4,6},{5,7},{6,4},{7,5},{8,10},{9,11},{10,... | collective-permute-start | bytes 3538952 | tf_op jit(solution)/shard_map/ppermute | solution.py:23
  28.9 0.4 fusion.4
  29.6 1.2 slice.19
  30.8 1.0 pad_maximum_fusion
  31.8 1.7 %collective-permute-start.6 = (bf16[128,3072]{1,0:T(8,128)(2,1)}, bf16[128,3072]{1,0:T(8,128)(2,1)}, u32[]{:S(2)}, u32[]{:S(2)}) collective-permute-start(bf16[128,3072]{1,0:T(8,128)(2,1)} %pad_maximum_fusion), channel_id=1, source_target_pairs={{0,4},{4,0},{8,12},{12,8},{16,20},{20,16},{24,28},{28,24},{1,5},{5... | collective-permute-start | bytes 2359304 | tf_op jit(solution)/shard_map/ppermute | solution.py:23
  33.6 2.0 %shard_map.85 = bf16[8,4,2,16,384]{4,3,2,1,0:T(8,128)(2,1)S(1)} custom-call(s32[3]{0:T(128)S(1)} %pad_add_fusion.where, bf16[384,1536]{1,0:T(8,128)(2,1)S(1)} %copy-done.2, bf16[128,1536]{1,0:T(8,128)(2,1)S(1)} %bitcast.57, bf16[128,1536]{1,0:T(8,128)(2,1)S(1)} %bitcast.54, bf16[128,1920]{1,0:T(8,128)(2,1)S(1)} %copy-done.13, ...), custom_call_target="tpu_custom_call" | custom-call | flops 603979776 | bytes 4816908 | tf_op jit(solution)/shard_map/pallas_call | solution.py:49
  35.6 0.9 copy-done.9
  36.5 4.3 %all-to-all-start.1 = ((bf16[32,2,16,384]{3,2,1,0:T(8,128)(2,1)}), bf16[32,2,16,384]{3,2,1,0:T(8,128)(2,1)}, u32[]{:S(2)}, u32[]{:S(2)}) async-start(bf16[32,2,16,384]{3,2,1,0:T(8,128)(2,1)} %bitcast.59), calls=%async_computation.1 | async-start | bytes 1572864 | tf_op jit(solution)/shard_map/all_to_all | solution.py:206
  40.7 0.3 collective-permute-start.4
  41.0 21.2 %collective-permute-done.3.w2 = bf16[384,1536]{1,0:T(8,128)(2,1)} collective-permute-done((bf16[384,1536]{1,0:T(8,128)(2,1)S(1)}, bf16[384,1536]{1,0:T(8,128)(2,1)}, u32[]{:S(2)}, u32[]{:S(2)}) %collective-permute-start.3) | collective-permute-done | bytes 1179680 | tf_op jit(solution)/shard_map/ppermute | solution.py:23
  62.2 0.5 collective-permute-start.7
  62.7 2.0 %all-to-all-done.1 = bf16[32,2,16,384]{3,2,1,0:T(8,128)(2,1)} async-done(((bf16[32,2,16,384]{3,2,1,0:T(8,128)(2,1)}), bf16[32,2,16,384]{3,2,1,0:T(8,128)(2,1)}, u32[]{:S(2)}, u32[]{:S(2)}) %all-to-all-start.1) | async-done | bytes 786464 | tf_op jit(solution)/shard_map/all_to_all | solution.py:206
  64.7 1.8 %collective-permute-done.7.refs_5_.refs_7_ = bf16[128,3072]{1,0:T(8,128)(2,1)} collective-permute-done((bf16[128,3072]{1,0:T(8,128)(2,1)}, bf16[128,3072]{1,0:T(8,128)(2,1)}, u32[]{:S(2)}, u32[]{:S(2)}) %collective-permute-start.7) | collective-permute-done | bytes 786464 | tf_op jit(solution)/shard_map/ppermute | solution.py:23
  66.5 1.1 fusion.12
  67.6 1.8 %collective-permute-start.8 = (bf16[192,1536]{1,0:T(8,128)(2,1)}, bf16[192,1536]{1,0:T(8,128)(2,1)S(1)}, u32[]{:S(2)}, u32[]{:S(2)}) collective-permute-start(bf16[192,1536]{1,0:T(8,128)(2,1)} %get-tuple-element.66), channel_id=1, source_target_pairs={{0,2},{1,3},{2,0},{3,1},{4,6},{5,7},{6,4},{7,5},{8,10},{9,11},{10,... | collective-permute-start | bytes 1769480 | tf_op jit(solution)/shard_map/ppermute | solution.py:23
  69.4 4.9 %shard_map.86 = (bf16[128,1536]{1,0:T(8,128)(2,1)}, bf16[128,1536]{1,0:T(8,128)(2,1)}, bf16[8,192,128]{2,1,0:T(8,128)(2,1)}) custom-call(s32[3]{0:T(128)} %copy-done.22, bf16[8,4,2,16,384]{4,3,2,1,0:T(8,128)(2,1)} %bitcast.15.mix, bf16[384,1536]{1,0:T(8,128)(2,1)} %w0.5, bf16[384,1536]{1,0:T(8,128)(2,1)} %collective-permute-done.4.w1, ...), custom_call_target="tpu_custom_call" | custom-call | flops 603979776 | bytes 7077900 | tf_op jit(solution)/shard_map/pallas_call | solution.py:49
  74.3 3.6 %all-to-all-start.2 = ((bf16[8,192,128]{2,1,0:T(8,128)(2,1)}), bf16[8,192,128]{2,1,0:T(8,128)(2,1)S(1)}, u32[]{:S(2)}, u32[]{:S(2)}) async-start(bf16[8,192,128]{2,1,0:T(8,128)(2,1)} %get-tuple-element.46), calls=%async_computation.2 | async-start | bytes 786432 | tf_op jit(solution)/shard_map/all_to_all | solution.py:275
  77.8 1.0 slice_bitcast_fusion
  78.9 0.3 fusion.2
  79.2 0.9 copy.38
  80.1 8.5 %all-to-all-done.2.got = bf16[8,192,128]{2,1,0:T(8,128)(2,1)S(1)} async-done(((bf16[8,192,128]{2,1,0:T(8,128)(2,1)}), bf16[8,192,128]{2,1,0:T(8,128)(2,1)S(1)}, u32[]{:S(2)}, u32[]{:S(2)}) %all-to-all-start.2) | async-done | bytes 393248 | tf_op jit(solution)/shard_map/all_to_all | solution.py:275
  88.6 5.3 %all-to-all-start.3 = ((bf16[8,4,16,384]{3,2,1,0:T(8,128)(2,1)}), bf16[8,4,16,384]{3,2,1,0:T(8,128)(2,1)S(1)}, u32[]{:S(2)}, u32[]{:S(2)}) async-start(bf16[8,4,16,384]{3,2,1,0:T(8,128)(2,1)} %bitcast.49), calls=%async_computation.3 | async-start | bytes 786432 | tf_op jit(solution)/shard_map/all_to_all | solution.py:40
  93.9 1.5 %collective-permute-start.10 = (bf16[192,1536]{1,0:T(8,128)(2,1)}, bf16[192,1536]{1,0:T(8,128)(2,1)}, u32[]{:S(2)}, u32[]{:S(2)}) collective-permute-start(bf16[192,1536]{1,0:T(8,128)(2,1)} %get-tuple-element.65), channel_id=1, source_target_pairs={{0,2},{1,3},{2,0},{3,1},{4,6},{5,7},{6,4},{7,5},{8,10},{9,11},{10,... | collective-permute-start | bytes 1769480 | tf_op jit(solution)/shard_map/ppermute | solution.py:23
  95.4 5.1 %shard_map.87 = (f32[2,48,1536]{2,1,0:T(8,128)}, bf16[2,48,1536]{2,1,0:T(8,128)(2,1)}) custom-call(s32[3]{0:T(128)} %copy-done.22, bf16[8,192,128]{2,1,0:T(8,128)(2,1)} %copy-done.24, bf16[128,1536]{1,0:T(8,128)(2,1)} %bitcast.51, bf16[128,1920]{1,0:T(8,128)(2,1)} %copy-done.12, bf16[128,2304]{1,0:T(8,128)(2,1)} %copy-done.7, bf16[128,2304]{1,0:T(8,128)(2,1)} %copy-done.10, ...), custom_call_target="tpu_custom_call" | custom-call | flops 603979776 | bytes 6488076 | tf_op jit(solution)/shard_map/pallas_call | solution.py:49
  100.5 2.1 %collective-permute-start.9 = (bf16[2,48,1536]{2,1,0:T(8,128)(2,1)}, bf16[2,48,1536]{2,1,0:T(8,128)(2,1)}, u32[]{:S(2)}, u32[]{:S(2)}) collective-permute-start(bf16[2,48,1536]{2,1,0:T(8,128)(2,1)} %get-tuple-element.52), channel_id=1, source_target_pairs={{0,8},{4,12},{8,0},{12,4},{16,24},{20,28},{24,16},{28,20},{1,9},{5... | collective-permute-start | bytes 884744 | tf_op jit(solution)/shard_map/ppermute | solution.py:23
  102.6 0.5 collective-permute-start.13
  103.1 4.9 %collective-permute-done.10.w3 = bf16[192,1536]{1,0:T(8,128)(2,1)} collective-permute-done((bf16[192,1536]{1,0:T(8,128)(2,1)}, bf16[192,1536]{1,0:T(8,128)(2,1)}, u32[]{:S(2)}, u32[]{:S(2)}) %collective-permute-start.10) | collective-permute-done | bytes 589856 | tf_op jit(solution)/shard_map/ppermute | solution.py:23
  108.0 1.7 %collective-permute-done.9 = bf16[2,48,1536]{2,1,0:T(8,128)(2,1)} collective-permute-done((bf16[2,48,1536]{2,1,0:T(8,128)(2,1)}, bf16[2,48,1536]{2,1,0:T(8,128)(2,1)}, u32[]{:S(2)}, u32[]{:S(2)}) %collective-permute-start.9) | collective-permute-done | bytes 294944 | tf_op jit(solution)/shard_map/ppermute | solution.py:23
  109.8 1.3 %add_bitcast_fusion = f32[1,2,48,1536]{3,2,1,0:T(8,128)S(1)} fusion(f32[2,48,1536]{2,1,0:T(8,128)} %get-tuple-element.51, bf16[2,48,1536]{2,1,0:T(8,128)(2,1)} %collective-permute-done.9), kind=kLoop, calls=%fused_computation.5 | loop fusion | flops 294912 | bytes 1474560 | tf_op jit(solution)/shard_map/reshape | solution.py:190
  111.0 1.1 collective-permute-start.11
  112.2 1.0 copy-done.14
  113.3 1.3 %copy-done.15 = bf16[384,1536]{1,0:T(8,128)(2,1)S(1)} copy-done((bf16[384,1536]{1,0:T(8,128)(2,1)S(1)}, bf16[384,1536]{1,0:T(8,128)(2,1)}, u32[]{:S(2)}) %copy-start.15) | copy-done | bytes 1179672
  114.5 1.0 copy-done.19
  115.5 4.8 %shard_map.88 = (bf16[128,1536]{1,0:T(8,128)(2,1)}, f32[128,1536]{1,0:T(8,128)S(1)}) custom-call(s32[3]{0:T(128)S(1)} %copy-done.23, bf16[128,1536]{1,0:T(8,128)(2,1)S(1)} %copy-done.19, bf16[128,1536]{1,0:T(8,128)(2,1)S(1)} %copy-done.18, bf16[128,1536]{1,0:T(8,128)(2,1)S(1)} %bitcast.58, bf16[128,1536]{1,0:T(8,128)(2,1)S(1)} %bitcast.55, ...), custom_call_target="tpu_custom_call" | custom-call | flops 1207959552 | bytes 7471116 | tf_op jit(solution)/shard_map/pallas_call | solution.py:49
  120.3 4.3 %shard_map.89 = bf16[128,1536]{1,0:T(8,128)(2,1)} custom-call(s32[3]{0:T(128)S(1)} %copy-done.23, bf16[8,4,16,384]{3,2,1,0:T(8,128)(2,1)S(1)} %all-to-all-done.3.back, bf16[128,128]{1,0:T(8,128)(2,1)S(1)} %bitcast.61, f32[128,1536]{1,0:T(8,128)S(1)} %get-tuple-element.61.term, bf16[384,1536]{1,0:T(8,128)(2,1)S(1)} %copy-done.6, ...), custom_call_target="tpu_custom_call" | custom-call | flops 603979776 | bytes 6324236 | tf_op jit(solution)/shard_map/pallas_call | solution.py:49
  124.7 0.8 fusion.8
  (70 shorter events, 1.0 us)
Async XLA Ops:
  0.6 2.7 %copy-start = (bf16[1,128,1536]{2,1,0:T(8,128)(2,1)S(1)}, bf16[1,128,1536]{2,1,0:T(8,128)(2,1)}, u32[]{:S(2)}) copy-start(bf16[1,128,1536]{2,1,0:T(8,128)(2,1)} %param.11) | copy-start | bytes 1179652
  1.7 5.0 %copy-start.3 = (bf16[1,128,1536]{2,1,0:T(8,128)(2,1)S(1)}, bf16[1,128,1536]{2,1,0:T(8,128)(2,1)}, u32[]{:S(2)}) copy-start(bf16[1,128,1536]{2,1,0:T(8,128)(2,1)} %param.6) | copy-start | bytes 1179652
  1.8 5.0 %copy-start.20 = (bf16[1,128,128]{2,1,0:T(8,128)(2,1)S(1)}, bf16[1,128,128]{2,1,0:T(8,128)(2,1)}, u32[]{:S(2)}) copy-start(bf16[1,128,128]{2,1,0:T(8,128)(2,1)} %param.9) | copy-start | bytes 98308
  2.8 4.2 %collective-permute-start = (bf16[128,1920]{1,0:T(8,128)(2,1)S(1)}, bf16[128,1920]{1,0:T(8,128)(2,1)S(1)}, u32[]{:S(2)}, u32[]{:S(2)}) collective-permute-start(bf16[128,1920]{1,0:T(8,128)(2,1)S(1)} %pad_maximum_fusion.2), channel_id=1, source_target_pairs={{0,1},{1,0},{2,3},{3,2},{4,5},{5,4},{6,7},{7,6},{8,9},{9,8},{10,11... | collective-permute-start | bytes 1474568 | tf_op jit(solution)/shard_map/ppermute | solution.py:23
  4.2 19.4 %collective-permute-start.1 = (bf16[128,2304]{1,0:T(8,128)(2,1)}, bf16[128,2304]{1,0:T(8,128)(2,1)S(1)}, u32[]{:S(2)}, u32[]{:S(2)}) collective-permute-start(bf16[128,2304]{1,0:T(8,128)(2,1)} %pad_maximum_fusion.1), channel_id=1, source_target_pairs={{0,2},{1,3},{2,0},{3,1},{4,6},{5,7},{6,4},{7,5},{8,10},{9,11},{10,... | collective-permute-start | bytes 1769480 | tf_op jit(solution)/shard_map/ppermute | solution.py:23
  7.0 19.9 %copy-start.5 = (bf16[384,1536]{1,0:T(8,128)(2,1)S(1)}, bf16[384,1536]{1,0:T(8,128)(2,1)}, u32[]{:S(2)}) copy-start(bf16[384,1536]{1,0:T(8,128)(2,1)} %w0.5) | copy-start | bytes 3538948
  7.0 21.7 %copy-start.27 = (bf16[16,8,8]{0,2,1:T(8,128)(2,1)S(1)}, bf16[16,8,8]{0,2,1:T(8,128)(2,1)}, u32[]{:S(2)}) copy-start(bf16[16,8,8]{0,2,1:T(8,128)(2,1)} %param.10) | copy-start | bytes 6148
  7.0 0.8 copy-start.12
  8.7 18.2 %all-to-all-start = ((bf16[32,16,384]{2,1,0:T(8,128)(2,1)}), bf16[32,16,384]{2,1,0:T(8,128)(2,1)S(1)}, u32[]{:S(2)}, u32[]{:S(2)}) async-start(bf16[32,16,384]{2,1,0:T(8,128)(2,1)} %bitcast.8), calls=%async_computation | async-start | bytes 786432 | tf_op jit(solution)/shard_map/all_to_all | solution.py:206
  23.6 5.7 %copy-start.7 = (bf16[128,2304]{1,0:T(8,128)(2,1)}, bf16[128,2304]{1,0:T(8,128)(2,1)S(1)}, u32[]{:S(2)}) copy-start(bf16[128,2304]{1,0:T(8,128)(2,1)S(1)} %collective-permute-done.1.far.refs_2_) | copy-start | bytes 1769476
  23.6 2.0 %collective-permute-start.2 = (bf16[128,2304]{1,0:T(8,128)(2,1)S(1)}, bf16[128,2304]{1,0:T(8,128)(2,1)S(1)}, u32[]{:S(2)}, u32[]{:S(2)}) collective-permute-start(bf16[128,2304]{1,0:T(8,128)(2,1)S(1)} %collective-permute-done.1.far.refs_2_), channel_id=1, source_target_pairs={{0,1},{1,0},{2,3},{3,2},{4,5},{5,4},{6,7},{7,6},{8,9},{9,8},{10,11... | collective-permute-start | bytes 1769480 | tf_op jit(solution)/shard_map/ppermute | solution.py:23
  25.6 0.8 copy-start.10
  26.9 35.2 %collective-permute-start.3 = (bf16[384,1536]{1,0:T(8,128)(2,1)S(1)}, bf16[384,1536]{1,0:T(8,128)(2,1)}, u32[]{:S(2)}, u32[]{:S(2)}) collective-permute-start(bf16[384,1536]{1,0:T(8,128)(2,1)S(1)} %copy-done.5), channel_id=1, source_target_pairs={{0,2},{1,3},{2,0},{3,1},{4,6},{5,7},{6,4},{7,5},{8,10},{9,11},{10,... | collective-permute-start | bytes 3538952 | tf_op jit(solution)/shard_map/ppermute | solution.py:23
  28.8 0.6 copy-start.25
  28.9 4.6 %copy-start.22 = (s32[3]{0:T(128)}, s32[3]{0:T(128)S(1)}, u32[]{:S(2)}) copy-start(s32[3]{0:T(128)S(1)} %pad_add_fusion.where) | copy-start | bytes 40
  29.4 4.1 %copy-start.13 = (bf16[128,1920]{1,0:T(8,128)(2,1)S(1)}, bf16[128,1920]{1,0:T(8,128)(2,1)}, u32[]{:S(2)}) copy-start(bf16[128,1920]{1,0:T(8,128)(2,1)} %copy-done.12) | copy-start | bytes 1474564
  29.6 4.0 %copy-start.2 = (bf16[384,1536]{1,0:T(8,128)(2,1)S(1)}, bf16[384,1536]{1,0:T(8,128)(2,1)}, u32[]{:S(2)}) copy-start(bf16[384,1536]{1,0:T(8,128)(2,1)} %w0.4) | copy-start | bytes 3538948
  29.6 4.0 %copy-start.8 = (bf16[128,2304]{1,0:T(8,128)(2,1)S(1)}, bf16[128,2304]{1,0:T(8,128)(2,1)}, u32[]{:S(2)}) copy-start(bf16[128,2304]{1,0:T(8,128)(2,1)} %copy-done.7) | copy-start | bytes 1769476
  29.6 4.0 %copy-start.11 = (bf16[128,2304]{1,0:T(8,128)(2,1)S(1)}, bf16[128,2304]{1,0:T(8,128)(2,1)}, u32[]{:S(2)}) copy-start(bf16[128,2304]{1,0:T(8,128)(2,1)} %copy-done.10) | copy-start | bytes 1769476
  31.8 30.4 %collective-permute-start.6 = (bf16[128,3072]{1,0:T(8,128)(2,1)}, bf16[128,3072]{1,0:T(8,128)(2,1)}, u32[]{:S(2)}, u32[]{:S(2)}) collective-permute-start(bf16[128,3072]{1,0:T(8,128)(2,1)} %pad_maximum_fusion), channel_id=1, source_target_pairs={{0,4},{4,0},{8,12},{12,8},{16,20},{20,16},{24,28},{28,24},{1,5},{5... | collective-permute-start | bytes 2359304 | tf_op jit(solution)/shard_map/ppermute | solution.py:23
  35.6 0.9 copy-start.9
  36.5 28.2 %all-to-all-start.1 = ((bf16[32,2,16,384]{3,2,1,0:T(8,128)(2,1)}), bf16[32,2,16,384]{3,2,1,0:T(8,128)(2,1)}, u32[]{:S(2)}, u32[]{:S(2)}) async-start(bf16[32,2,16,384]{3,2,1,0:T(8,128)(2,1)} %bitcast.59), calls=%async_computation.1 | async-start | bytes 1572864 | tf_op jit(solution)/shard_map/all_to_all | solution.py:206
  40.7 22.0 %collective-permute-start.4 = (bf16[384,1536]{1,0:T(8,128)(2,1)S(1)}, bf16[384,1536]{1,0:T(8,128)(2,1)}, u32[]{:S(2)}, u32[]{:S(2)}) collective-permute-start(bf16[384,1536]{1,0:T(8,128)(2,1)S(1)} %copy-done.5), channel_id=1, source_target_pairs={{0,1},{1,0},{2,3},{3,2},{4,5},{5,4},{6,7},{7,6},{8,9},{9,8},{10,11... | collective-permute-start | bytes 3538952 | tf_op jit(solution)/shard_map/ppermute | solution.py:23
  62.2 4.3 %collective-permute-start.5 = (bf16[384,1536]{1,0:T(8,128)(2,1)}, bf16[384,1536]{1,0:T(8,128)(2,1)}, u32[]{:S(2)}, u32[]{:S(2)}) collective-permute-start(bf16[384,1536]{1,0:T(8,128)(2,1)} %collective-permute-done.3.w2), channel_id=1, source_target_pairs={{0,1},{1,0},{2,3},{3,2},{4,5},{5,4},{6,7},{7,6},{8,9},{9,8},{10,11... | collective-permute-start | bytes 3538952 | tf_op jit(solution)/shard_map/ppermute | solution.py:23
  62.2 4.3 %collective-permute-start.7 = (bf16[128,3072]{1,0:T(8,128)(2,1)}, bf16[128,3072]{1,0:T(8,128)(2,1)}, u32[]{:S(2)}, u32[]{:S(2)}) collective-permute-start(bf16[128,3072]{1,0:T(8,128)(2,1)} %collective-permute-done.6.refs_4_.refs_6_), channel_id=1, source_target_pairs={{0,1},{1,0},{2,3},{3,2},{4,5},{5,4},{6,7},{7,6},{8,9},{9,8},{10,11... | collective-permute-start | bytes 2359304 | tf_op jit(solution)/shard_map/ppermute | solution.py:23
  67.6 21.0 %collective-permute-start.8 = (bf16[192,1536]{1,0:T(8,128)(2,1)}, bf16[192,1536]{1,0:T(8,128)(2,1)S(1)}, u32[]{:S(2)}, u32[]{:S(2)}) collective-permute-start(bf16[192,1536]{1,0:T(8,128)(2,1)} %get-tuple-element.66), channel_id=1, source_target_pairs={{0,2},{1,3},{2,0},{3,1},{4,6},{5,7},{6,4},{7,5},{8,10},{9,11},{10,... | collective-permute-start | bytes 1769480 | tf_op jit(solution)/shard_map/ppermute | solution.py:23
  74.3 4.6 %copy-start.26 = (bf16[16,8,8,1]{1,2,3,0:T(8,128)(2,1)S(1)}, bf16[16,8,8,1]{1,2,3,0:T(8,128)(2,1)}, u32[]{:S(2)}) copy-start(bf16[16,8,8,1]{1,2,3,0:T(8,128)(2,1)} %copy-done.25) | copy-start | bytes 6148
  74.3 14.3 %all-to-all-start.2 = ((bf16[8,192,128]{2,1,0:T(8,128)(2,1)}), bf16[8,192,128]{2,1,0:T(8,128)(2,1)S(1)}, u32[]{:S(2)}, u32[]{:S(2)}) async-start(bf16[8,192,128]{2,1,0:T(8,128)(2,1)} %get-tuple-element.46), calls=%async_computation.2 | async-start | bytes 786432 | tf_op jit(solution)/shard_map/all_to_all | solution.py:275
  88.6 6.8 %copy-start.24 = (bf16[8,192,128]{2,1,0:T(8,128)(2,1)}, bf16[8,192,128]{2,1,0:T(8,128)(2,1)S(1)}, u32[]{:S(2)}) copy-start(bf16[8,192,128]{2,1,0:T(8,128)(2,1)S(1)} %all-to-all-done.2.got) | copy-start | bytes 1179652
  88.6 6.8 %copy-start.16 = (bf16[192,1536]{1,0:T(8,128)(2,1)}, bf16[192,1536]{1,0:T(8,128)(2,1)S(1)}, u32[]{:S(2)}) copy-start(bf16[192,1536]{1,0:T(8,128)(2,1)S(1)} %collective-permute-done.8.w2) | copy-start | bytes 1769476
  88.6 21.1 %all-to-all-start.3 = ((bf16[8,4,16,384]{3,2,1,0:T(8,128)(2,1)}), bf16[8,4,16,384]{3,2,1,0:T(8,128)(2,1)S(1)}, u32[]{:S(2)}, u32[]{:S(2)}) async-start(bf16[8,4,16,384]{3,2,1,0:T(8,128)(2,1)} %bitcast.49), calls=%async_computation.3 | async-start | bytes 786432 | tf_op jit(solution)/shard_map/all_to_all | solution.py:40
  93.9 14.1 %collective-permute-start.10 = (bf16[192,1536]{1,0:T(8,128)(2,1)}, bf16[192,1536]{1,0:T(8,128)(2,1)}, u32[]{:S(2)}, u32[]{:S(2)}) collective-permute-start(bf16[192,1536]{1,0:T(8,128)(2,1)} %get-tuple-element.65), channel_id=1, source_target_pairs={{0,2},{1,3},{2,0},{3,1},{4,6},{5,7},{6,4},{7,5},{8,10},{9,11},{10,... | collective-permute-start | bytes 1769480 | tf_op jit(solution)/shard_map/ppermute | solution.py:23
  100.5 12.7 %copy-start.1 = (bf16[1,128,1536]{2,1,0:T(8,128)(2,1)S(1)}, bf16[1,128,1536]{2,1,0:T(8,128)(2,1)}, u32[]{:S(2)}) copy-start(bf16[1,128,1536]{2,1,0:T(8,128)(2,1)} %param.11) | copy-start | bytes 1179652
  100.5 12.7 %copy-start.4 = (bf16[1,128,1536]{2,1,0:T(8,128)(2,1)S(1)}, bf16[1,128,1536]{2,1,0:T(8,128)(2,1)}, u32[]{:S(2)}) copy-start(bf16[1,128,1536]{2,1,0:T(8,128)(2,1)} %param.6) | copy-start | bytes 1179652
  100.5 12.7 %copy-start.23 = (s32[3]{0:T(128)S(1)}, s32[3]{0:T(128)}, u32[]{:S(2)}) copy-start(s32[3]{0:T(128)} %copy-done.22) | copy-start | bytes 40
  100.5 9.1 %collective-permute-start.9 = (bf16[2,48,1536]{2,1,0:T(8,128)(2,1)}, bf16[2,48,1536]{2,1,0:T(8,128)(2,1)}, u32[]{:S(2)}, u32[]{:S(2)}) collective-permute-start(bf16[2,48,1536]{2,1,0:T(8,128)(2,1)} %get-tuple-element.52), channel_id=1, source_target_pairs={{0,8},{4,12},{8,0},{12,4},{16,24},{20,28},{24,16},{28,20},{1,9},{5... | collective-permute-start | bytes 884744 | tf_op jit(solution)/shard_map/ppermute | solution.py:23
  102.6 9.5 %collective-permute-start.12 = (bf16[384,1536]{1,0:T(8,128)(2,1)S(1)}, bf16[384,1536]{1,0:T(8,128)(2,1)S(1)}, u32[]{:S(2)}, u32[]{:S(2)}) collective-permute-start(bf16[384,1536]{1,0:T(8,128)(2,1)S(1)} %copy-done.2), channel_id=1, source_target_pairs={{0,1},{1,0},{2,3},{3,2},{4,5},{5,4},{6,7},{7,6},{8,9},{9,8},{10,11... | collective-permute-start | bytes 3538952 | tf_op jit(solution)/shard_map/ppermute | solution.py:23
  102.6 9.5 %collective-permute-start.13 = (bf16[192,1536]{1,0:T(8,128)(2,1)}, bf16[192,1536]{1,0:T(8,128)(2,1)}, u32[]{:S(2)}, u32[]{:S(2)}) collective-permute-start(bf16[192,1536]{1,0:T(8,128)(2,1)} %copy-done.16), channel_id=1, source_target_pairs={{0,1},{1,0},{2,3},{3,2},{4,5},{5,4},{6,7},{7,6},{8,9},{9,8},{10,11... | collective-permute-start | bytes 1769480 | tf_op jit(solution)/shard_map/ppermute | solution.py:23
  109.7 3.6 %copy-start.17 = (bf16[192,1536]{1,0:T(8,128)(2,1)S(1)}, bf16[192,1536]{1,0:T(8,128)(2,1)}, u32[]{:S(2)}) copy-start(bf16[192,1536]{1,0:T(8,128)(2,1)} %copy-done.16) | copy-start | bytes 1769476
  109.7 3.6 %copy-start.18 = (bf16[128,1536]{1,0:T(8,128)(2,1)S(1)}, bf16[128,1536]{1,0:T(8,128)(2,1)}, u32[]{:S(2)}) copy-start(bf16[128,1536]{1,0:T(8,128)(2,1)} %get-tuple-element.56.mon) | copy-start | bytes 1179652
  109.7 3.6 %collective-permute-start.14 = (bf16[192,1536]{1,0:T(8,128)(2,1)}, bf16[192,1536]{1,0:T(8,128)(2,1)S(1)}, u32[]{:S(2)}, u32[]{:S(2)}) collective-permute-start(bf16[192,1536]{1,0:T(8,128)(2,1)} %collective-permute-done.10.w3), channel_id=1, source_target_pairs={{0,1},{1,0},{2,3},{3,2},{4,5},{5,4},{6,7},{7,6},{8,9},{9,8},{10,11... | collective-permute-start | bytes 1769480 | tf_op jit(solution)/shard_map/ppermute | solution.py:23
  111.0 13.6 %collective-permute-start.11 = (bf16[1,48,1536]{2,1,0:T(8,128)(2,1)S(1)}, bf16[1,48,1536]{2,1,0:T(8,128)(2,1)S(1)}, u32[]{:S(2)}, u32[]{:S(2)}) collective-permute-start(bf16[1,48,1536]{2,1,0:T(8,128)(2,1)S(1)} %fusion.9), channel_id=1, source_target_pairs={{0,16},{4,20},{8,24},{12,28},{16,0},{20,4},{24,8},{28,12},{1,17},{... | collective-permute-start | bytes 442376 | tf_op jit(solution)/shard_map/ppermute | solution.py:23
  112.2 1.1 copy-start.14
  113.3 1.3 %copy-start.15 = (bf16[384,1536]{1,0:T(8,128)(2,1)S(1)}, bf16[384,1536]{1,0:T(8,128)(2,1)}, u32[]{:S(2)}) copy-start(bf16[384,1536]{1,0:T(8,128)(2,1)} %copy-done.14) | copy-start | bytes 3538948
  114.5 1.0 copy-start.19
  115.5 4.8 %copy-start.6 = (bf16[384,1536]{1,0:T(8,128)(2,1)S(1)}, bf16[384,1536]{1,0:T(8,128)(2,1)}, u32[]{:S(2)}) copy-start(bf16[384,1536]{1,0:T(8,128)(2,1)} %w0.5) | copy-start | bytes 3538948
  115.5 4.8 %copy-start.21 = (bf16[1,128,128]{2,1,0:T(8,128)(2,1)S(1)}, bf16[1,128,128]{2,1,0:T(8,128)(2,1)}, u32[]{:S(2)}) copy-start(bf16[1,128,128]{2,1,0:T(8,128)(2,1)} %param.9) | copy-start | bytes 98308

commit v3 on v2

--- a/solution.py
+++ b/solution.py
@@ -61,40 +61,47 @@
     return jax.ShapeDtypeStruct(dims, dtype)
 
 
-def grad_kernel(part, where, w, tok, cot, near, far, side, *refs):
+def grad_kernel(part, where, w, tok, cot, near, far, side, tok_far, tok_side, out):
     me = where[0]
     width = cot.shape[1]
-    out = refs[-1]
-    if len(refs) > 1:
-        out[:, :, 0] = refs[0][...]
     pairs = (
         (cot[...], tok[:, pl.ds(aligned(me, part), part)]),
         (near[:, :width], near[:, width:]),
-        (far[:, part : part + width], far[:, :part]),
-        (side[:, part : part + width], side[:, part + width :]),
+        (far[...], tok_far[:, :part]),
+        (side[...], tok_side[:, part:]),
     )
     for r, (x, t) in enumerate(pairs):
         grad = (dot(x, w[...], 1, 1) * jax.nn.silu(t.astype(F32))).astype(BF16)
-        if len(refs) > 1:
-            offs = out.shape[3]
+        if len(out.shape) == 4:
+            offs = out.shape[2]
             for s in range(out.shape[0]):
-                out[s, me ^ r, 1] = grad[s * offs : (s + 1) * offs]
+                out[s, me ^ r] = grad[s * offs : (s + 1) * offs]
         else:
             out[me ^ r] = grad
 
 
-def gate_kernel(part, piece, tile, where, mix, w0, w1, w2, w3, tok, mon_out, gated_out, t_out, held):
+def rows_of(refs, cols):
+    return jnp.concatenate([w[:, cols] for w in refs], axis=0) if len(refs) > 1 else refs[0][:, cols]
+
+
+def ordered(x, r, y):
+    if r < 2:
+        return x
+    n = x.shape[1] // 3
+    a, b, c = x[:, :n], x[:, n : 2 * n], x[:, 2 * n :]
+    return jnp.concatenate([jnp.where(y == 0, a, b), jnp.where(y == 0, b, a), c], axis=1)
+
+
+def gate_kernel(part, piece, tile, where, mix, tok, w0, w1, w2, w3, w4, w5, mon_out, gated_out, t_out, held):
     me, z = where[0], where[1]
     rows, width = tok.shape
-    if len(mix.shape) == 5:
-        lhs = [mix[:, pl.ds(me ^ r, 1), 0].reshape(rows, part) for r in range(4)]
-    else:
-        lhs = [mix[:, pl.ds(aligned(me ^ r, part), part)] for r in range(4)]
+    lhs = [mix[:, pl.ds(aligned(me ^ r, part), part)] for r in range(4)]
+    weights = ((w0,), (w1,), (w2, w3), (w4, w5))
     for c in range(0, width, tile):
         cols = slice(c, c + tile)
-        total = dot(lhs[0], w0[:, cols], 1, 0)
-        for x, w in zip(lhs[1:], (w1, w2, w3)):
-            total += dot(x, w[:, cols], 1, 0)
+        total = 0.0
+        for x, some in zip(lhs, weights):
+            total += dot(x, rows_of(some, cols), 1, 0)
         mon = total.astype(BF16)
         mon_out[:, cols] = mon
         wide = tok[:, cols].astype(F32)
@@ -111,7 +118,7 @@
         t_out[...] = held[...]
 
 
-def carry_kernel(part, where, back, first, term, w0, w1, w2, w3, out):
+def carry_kernel(part, where, back, first, term, w0, w1, w2, w3, w4, w5, out):
     me = where[0]
     if len(back.shape) == 4:
         nseq, ndp, offs, _ = back.shape
@@ -120,29 +127,29 @@
     else:
         back = back[...]
     grad = dot(first[...], back, 0, 0).astype(BF16)
-    for r, w in enumerate((w0, w1, w2, w3)):
+    for r, some in enumerate(((w0,), (w1,), (w2, w3), (w4, w5))):
         cols = pl.ds(aligned(me ^ r, part), part)
-        out[:, cols] = (dot(grad, w[...], 1, 1) + term[:, cols]).astype(BF16)
-
-
-def last_kernel(part, where, gated, mon, tok, cot, w0, w1, w2, w3, w4, w5, mixed, out):
-    me = where[0]
-    weights = (w0, w1, w2, w3, w4, w5)
-    half = part // 2
-    for r, some in enumerate(((w0,), (w1,), (w2, w3), (w4, w5))):
+        carried = dot(grad, rows_of(some, slice(None)), 1, 1)
+        out[:, cols] = (carried + term[:, cols]).astype(BF16)
+
+
+def last_kernel(part, where, gated, mon, tok, cot, *refs):
+    me, y = where[0], where[3]
+    mixed, out = refs[-2:]
+    weights = (refs[:1], refs[1:2], refs[2:5], refs[5:8])
+    for r, some in enumerate(weights):
         cols = pl.ds(aligned(me ^ r, part), part)
         wide = tok[:, cols].astype(F32)
         sigma = jax.nn.sigmoid(wide)
         slope = sigma * (1.0 + wide * (1.0 - sigma))
-        grad = jnp.concatenate([dot(cot[...], w[...], 1, 1) for w in some], axis=1)
+        grad = ordered(dot(cot[...], rows_of(some, slice(None)), 1, 1), r, y)
         out[:, cols] = grad * mon[:, cols].astype(F32) * slope
-    lhs = [gated[:, pl.ds(aligned(me ^ r, part), part)] for r in range(4)]
-    lhs = lhs[:2] + [x[:, h : h + half] for x in lhs[2:] for h in (0, half)]
+    lhs = [ordered(gated[:, pl.ds(aligned(me ^ r, part), part)], r, y) for r in range(4)]
     for c in range(0, mixed.shape[1], part):
         cols = slice(c, c + part)
-        total = dot(lhs[0], w0[:, cols], 1, 0)
-        for x, w in zip(lhs[1:], weights[1:]):
-            total += dot(x, w[:, cols], 1, 0)
+        total = 0.0
+        for x, some in zip(lhs, weights):
+            total += dot(x, rows_of(some, cols), 1, 0)
         mixed[:, cols] = total.astype(BF16)
 
 
@@ -196,64 +203,39 @@
     near = 2 * ndp
     outer = nseq // 2
     here = flat % near
-    where = jnp.stack([me, flat // near, here]).astype(jnp.int32)
-
-    def cut(x):
-        return x.reshape(nseq, offs, ndp, part).transpose(0, 2, 1, 3)
-
-    def exchange(x):
-        flat_x = x.reshape((nseq * ndp,) + x.shape[2:])
-        flat_x = lax.all_to_all(
-            flat_x, ("seq", "dp"), split_axis=0, concat_axis=0, tiled=True
-        )
-        return flat_x.reshape(x.shape)
-
-    cot_far = swap(jnp.concatenate([columns(inputs, 2), upstream, columns(inputs, 3)], axis=1), "dp", 2)
+    where = jnp.stack([me, flat // near, here, my_s % 2]).astype(jnp.int32)
+
+    split = offs % 16 == 0 and piece % 16 == 0
+
+    some = 2 * (part // 3)
+    far_a = swap(w_in[:some], "dp", 2)
+    arrived = spread(dot(first, inputs, 1, 0).astype(BF16).reshape(nseq, offs, width))
+    pair = swap(upstream, "seq", 1)
+    rest = w_in[some:]
+    third = part // 3
+    outs = lax.dynamic_slice_in_dim(w_out, (my_s % 2) * third, third, axis=0), w_out[some:]
+    arrived, far_a, rest, up, outs = join((arrived, far_a, rest, upstream, outs))
+
+    mix = jnp.einsum("sab,bsd->asd", second_factor, arrived, preferred_element_type=F32)
+    mix = spread(mix.astype(BF16))
+    far_b = swap(rest, "dp", 2)
+    side_a = swap(far_a, "dp", 1)
+    side_b = swap(far_b, "dp", 1)
+    w_near = swap(w_in, "dp", 1)
     cot_near = swap(jnp.concatenate([upstream, columns(inputs, 1)], axis=1), "dp", 1)
-    mix, cot_near = join((dot(first, inputs, 1, 0).astype(BF16), cot_near))
-    arrived = exchange(cut(mix))
+    tok_far = jnp.concatenate([columns(inputs, 2), columns(inputs, 3)], axis=1)
+    cot_far = swap(up, "dp", 2)
+    mix, far_b, side_a, side_b, w_near, cot_near, cot_far, tok_far, outs = join(
+        (mix, far_b, side_a, side_b, w_near, cot_near, cot_far, tok_far, outs)
+    )
+
+    w_ins = (w_in, w_near, far_a, far_b, side_a, side_b)
+    tok_far = swap(tok_far, "dp", 2)
+    pair_far = swap(cot_far, "seq", 1)
     cot_side = swap(cot_far, "dp", 1)
-    arrived, cot_near, cot_far, cot_side, w_late, up = join(
-        (arrived, cot_near, cot_far, cot_side, w_in, upstream)
-    )
-
-    mix = jnp.einsum("sab,bjsd->ajsd", second_factor, arrived, preferred_element_type=F32)
-    w_far = swap(w_late, "dp", 2)
-    w_near = swap(w_late, "dp", 1)
-    pair = jnp.concatenate([up, cot_far[:, part : part + width]], axis=1)
-    pair = swap(pair, "seq", 1)
-    pair_side = swap(pair, "dp", 1)
-    w_side = swap(w_far, "dp", 1)
-    mix = mix.astype(BF16)
-    split = offs % 16 == 0 and piece % 16 == 0
-    (both,) = call(
-        functools.partial(grad_kernel, part),
-        [shape((nseq, ndp, 2, offs, part) if split else (ndp, rows, part))],
-        where,
-        w_out,
-        inputs,
-        upstream,
-        cot_near,
-        cot_far,
-        cot_side,
-        *([mix] if split else []),
-        flops=flops,
-        room=40,
-    )
-    if not split:
-        both = both.reshape(ndp, nseq, offs, part).transpose(1, 0, 2, 3)
-        both = jnp.stack([mix, both], axis=2)
-    both = exchange(both)
-    both, w_far, w_near, w_side, pair, pair_side, w_late = join(
-        (both, w_far, w_near, w_side, pair, pair_side, w_out)
-    )
-    out_a = swap(w_late[: part // 2], "dp", 2)
-    out_b = swap(w_late[part // 2 :], "dp", 2)
-
-    mix = both if split else unchunk(both[:, :, 0])
-    back = jnp.einsum("sab,ajsc->bjsc", second_factor, both[:, :, 1], preferred_element_type=F32)
-    back = back.astype(BF16)
-    w_ins = (w_in, w_near, w_far, w_side)
+    tok_side = swap(tok_far, "dp", 1)
+    out_a = swap(outs[0], "dp", 2)
+    mix = mix.reshape(rows, width)
     monarch, gated, turned = call(
         functools.partial(gate_kernel, part, piece, part),
         [
@@ -263,8 +245,8 @@
         ],
         where,
         mix,
+        inputs,
         *w_ins,
-        inputs,
         flops=flops,
         scratch=[pltpu.VMEM((width, rows), BF16)],
     )
@@ -275,13 +257,36 @@
     got = lax.all_to_all(
         turned, ("seq", "dp"), split_axis=0, concat_axis=0, tiled=True, axis_index_groups=groups
     )
-    got, back, out_a = join((got, back, out_a))
-
-    back = spread(back)
+    (grads,) = call(
+        functools.partial(grad_kernel, part),
+        [shape((nseq, ndp, offs, part) if split else (ndp, rows, part))],
+        where,
+        w_out,
+        inputs,
+        upstream,
+        cot_near,
+        cot_far,
+        cot_side,
+        tok_far,
+        tok_side,
+        flops=flops,
+    )
+    if not split:
+        grads = grads.reshape(ndp, nseq, offs, part).transpose(1, 0, 2, 3)
+    grads = grads.reshape(nseq * ndp, offs, part)
+    got, grads, pair, pair_far, outs, out_a = join((got, grads, pair, pair_far, outs, out_a))
+    pairs = (pair, swap(pair, "dp", 1), pair_far, swap(pair_far, "dp", 1))
+    out_b = swap(out_a, "seq", 1)
+    out_c = swap(outs[1], "dp", 2)
+
+    grads = lax.all_to_all(grads, ("seq", "dp"), split_axis=0, concat_axis=0, tiled=True)
+    grads = grads.reshape(nseq, ndp, offs, part)
+    back = jnp.einsum("sab,ajsc->bjsc", second_factor, grads, preferred_element_type=F32)
+    back = back.astype(BF16)
     halves = (outer // 2, piece, width)
     total = call(
         functools.partial(
-            weight_kernel, part, (0, 0, part, part, 0, 0, width, width)
+            weight_kernel, part, (0,) * (2 * ndp)
         ),
         [shape(halves, F32), shape(halves)] if split else [shape((outer * piece, width), F32)],
         where,
@@ -290,10 +295,7 @@
         cot_near,
         cot_far,
         cot_side,
-        pair,
-        pair_side,
-        pair,
-        pair_side,
+        *pairs,
         flops=flops,
     )
     if not split:
@@ -301,18 +303,13 @@
         total = (total[:, 0], total[:, 1].astype(BF16))
     kept, sent = total
     sent = swap(sent, "seq", 2)
-    sent, back, out_b = join((sent, back, out_b))
+    sent, back, w_late, out_b, out_c = join((sent, back, w_out, out_b, out_c))
     total = kept + sent.astype(F32)
     bit = 2
 
-    w_outs = (
-        w_out,
-        swap(w_late, "dp", 1),
-        out_a,
-        out_b,
-        swap(out_a, "dp", 1),
-        swap(out_b, "dp", 1),
-    )
+    back = spread(back)
+    far = (out_a, out_b, out_c)
+    w_outs = (w_out, swap(w_late, "dp", 1), *far, *(swap(w, "dp", 1) for w in far))
     mixed, term = call(
         functools.partial(last_kernel, part),
         [shape((rows, width)), shape((rows, width), F32)],
@@ -323,7 +320,6 @@
         upstream,
         *w_outs,
         flops=2 * flops,
-        room=40,
     )
     if offs % 16 != 0:
         back = unchunk(back)
@@ -336,7 +332,6 @@
         term,
         *w_ins,
         flops=flops,
-        room=40,
     )
     ready = (mixed, input_grad)
     while total.shape[0] > 1:

time: 126 us -> 122 us (0.968)
  waiting for transfers between devices: 52.4 us -> 27.1 us
  starting transfers between devices: 32.5 us -> 45.1 us
  Pallas kernels: 21.2 us -> 24.6 us
  other arithmetic: 5.05 us -> 6.92 us
  matrix products: 0.95 us -> 2.66 us
    ppermute x15 -> x23, waiting for transfers between devices: 41.4 us -> 12.4 us  [swap(): return lax.ppermute(x, axis, [(i, i ^ bit) for i in range(n)])]
    all_to_all x1 -> x3, waiting for transfers between devices: 0.01 us -> 11.8 us  [spread(): return lax.all_to_all(x, 'seq', split_axis=0, concat_axis=0, tiled=True)]
    all_to_all x1 -> x3, starting transfers between devices: 5.31 us -> 16.1 us  [spread(): return lax.all_to_all(x, 'seq', split_axis=0, concat_axis=0, tiled=True)]
    all_to_all x1, waiting for transfers between devices: 8.48 us -> 0.98 us  [on_device(): lax.all_to_all(turned, ('seq', 'dp'), split_axis=0, concat_axis=0, tiled=...]
    ppermute x15 -> x23, starting transfers between devices: 14.3 us -> 20.6 us  [swap(): return lax.ppermute(x, axis, [(i, i ^ bit) for i in range(n)])]
    all_to_all x2 -> x1, starting transfers between devices: 9.28 us -> 4.94 us  [on_device(): lax.all_to_all(grads, ('seq', 'dp'), split_axis=0, concat_axis=0, tiled=T...]
    pallas_call x5, Pallas kernels: 21.2 us -> 24.6 us  [call(): pl.pallas_call(kernel, out_shape=list(outs), in_specs=[SMEM if x.dtype ==...]
    slice x2 -> x3, local copies, waits for them, and re-layouts: 2.27 us -> 3.91 us  [the longest x1 2.18 us: on_device(): far_a = swap(w_in[:some], 'dp', 2)]
  transfers between devices with their start and end apart: 19 -> 28, of which waited for: 9 -> 9; matrix products, arithmetic and copies ran while one was open for 7% -> 11% of each run, Pallas kernels for 17% -> 20%
where the time goes in v3:
time: 122 us; the launch traced here: 121 us
  starting transfers between devices  45.1 us (37%)
  waiting for transfers between devices  27.1 us (22%)
  Pallas kernels  24.6 us (20%)
  local copies, waits for them, and re-layouts  13.5 us (11%)
  other arithmetic  6.92 us (6%)
  matrix products  2.66 us (2%)
    pallas_call x5, Pallas kernels, call(): pl.pallas_call(kernel, out_shape=list(outs), in_specs=[SMEM if x.dtype ==...  24.6 us
    ppermute x23, starting transfers between devices, swap(): return lax.ppermute(x, axis, [(i, i ^ bit) for i in range(n)])  20.6 us
    all_to_all x3, starting transfers between devices, spread(): return lax.all_to_all(x, 'seq', split_axis=0, concat_axis=0, tiled=True)  16.1 us
    ppermute x23, waiting for transfers between devices, swap(): return lax.ppermute(x, axis, [(i, i ^ bit) for i in range(n)])  12.4 us
    all_to_all x3, waiting for transfers between devices, spread(): return lax.all_to_all(x, 'seq', split_axis=0, concat_axis=0, tiled=True)  11.8 us
    unnamed x52, local copies, waits for them, and re-layouts  7.16 us
    all_to_all x1, starting transfers between devices, on_device(): lax.all_to_all(grads, ('seq', 'dp'), split_axis=0, concat_axis=0, tiled=T...  4.94 us
    all_to_all x1, starting transfers between devices, on_device(): lax.all_to_all(turned, ('seq', 'dp'), split_axis=0, concat_axis=0, tiled=...  3.45 us
  transfers between devices with their start and end apart: 28, of which 9 were waited for; matrix products, arithmetic and copies ran while one was open for 11% of the time, Pallas kernels for 20%

profile of v3, /device:TPU:0, one launch (start us, length us, event | category | flops | bytes accessed | tf_op | source)
XLA Modules:
  0.0 120.9 jit_solution(970502791790203950)
XLA Ops:
  0.7 2.2 %slice.16 = bf16[256,1536]{1,0:T(8,128)(2,1)} slice(bf16[384,1536]{1,0:T(8,128)(2,1)} %w0.3), slice={[0:256], [0:1536]} | slice | bytes 1572864 | tf_op jit(solution)/shard_map/slice | solution.py:211
  2.9 2.9 %collective-permute-start = (bf16[256,1536]{1,0:T(8,128)(2,1)}, bf16[256,1536]{1,0:T(8,128)(2,1)S(1)}, u32[]{:S(2)}, u32[]{:S(2)}) collective-permute-start(bf16[256,1536]{1,0:T(8,128)(2,1)} %slice.16), channel_id=1, source_target_pairs={{0,2},{1,3},{2,0},{3,1},{4,6},{5,7},{6,4},{7,5},{8,10},{9,11},{10,... | collective-permute-start | bytes 2359304 | tf_op jit(solution)/shard_map/ppermute | solution.py:23
  5.8 1.0 convolution_convert_fusion.1
  6.8 5.8 %all-to-all-start = ((bf16[8,16,1536]{2,1,0:T(8,128)(2,1)}), bf16[8,16,1536]{2,1,0:T(8,128)(2,1)}, u32[]{:S(2)}, u32[]{:S(2)}) async-start(bf16[8,16,1536]{2,1,0:T(8,128)(2,1)} %bitcast.54), calls=%async_computation | async-start | bytes 786432 | tf_op jit(solution)/shard_map/all_to_all | solution.py:40
  12.8 1.0 fusion.11
  13.7 0.8 slice.17
  14.5 0.7 copy.21
  15.2 0.7 dynamic-slice_bitcast_fusion.1
  15.9 8.3 %all-to-all-done = bf16[8,16,1536]{2,1,0:T(8,128)(2,1)} async-done(((bf16[8,16,1536]{2,1,0:T(8,128)(2,1)}), bf16[8,16,1536]{2,1,0:T(8,128)(2,1)}, u32[]{:S(2)}, u32[]{:S(2)}) %all-to-all-start) | async-done | bytes 393248 | tf_op jit(solution)/shard_map/all_to_all | solution.py:40
  24.2 1.1 collective-permute-start.1
  25.3 1.3 %fusion = bf16[8,16,1536]{2,0,1:T(8,128)(2,1)S(1)} fusion(bf16[16,8,8]{2,1,0:T(8,128)(2,1)} %copy.21, bf16[8,16,1536]{2,1,0:T(8,128)(2,1)} %all-to-all-done), kind=kOutput, calls=%fused_computation.2 | convolution fusion | flops 3342336 | bytes 788480 | tf_op jit(solution)/shard_map/sab,bsd->asd/dot_general | solution.py:219
  26.6 0.9 copy.22
  27.5 5.8 %all-to-all-start.1 = ((bf16[8,16,1536]{2,1,0:T(8,128)(2,1)}), bf16[8,16,1536]{2,1,0:T(8,128)(2,1)}, u32[]{:S(2)}, u32[]{:S(2)}) async-start(bf16[8,16,1536]{2,1,0:T(8,128)(2,1)} %copy.22), calls=%async_computation.1 | async-start | bytes 786432 | tf_op jit(solution)/shard_map/all_to_all | solution.py:40
  33.3 1.7 %pad_maximum_fusion = bf16[128,1920]{1,0:T(8,128)(2,1)} fusion(bf16[128,384]{1,0:T(8,128)(2,1)} %get-tuple-element.80, bf16[128,1536]{1,0:T(8,128)(2,1)S(1)} %bitcast.51), kind=kLoop, calls=%fused_computation.5 | loop fusion | flops 983040 | bytes 983040 | tf_op jit(solution)/shard_map/concatenate | solution.py:225
  35.8 1.8 %pad_maximum_fusion.1 = bf16[128,768]{1,0:T(8,128)(2,1)} fusion(bf16[128,384]{1,0:T(8,128)(2,1)} %get-tuple-element.81, bf16[128,384]{1,0:T(8,128)(2,1)} %get-tuple-element.79), kind=kLoop, calls=%fused_computation.15 | loop fusion | flops 393216 | bytes 393216 | tf_op jit(solution)/shard_map/concatenate | solution.py:226
  37.6 1.9 %collective-permute-start.10 = (bf16[128,1536]{1,0:T(8,128)(2,1)S(1)}, bf16[128,1536]{1,0:T(8,128)(2,1)}, u32[]{:S(2)}, u32[]{:S(2)}) collective-permute-start(bf16[128,1536]{1,0:T(8,128)(2,1)S(1)} %bitcast.53), channel_id=1, source_target_pairs={{0,4},{4,0},{8,12},{12,8},{16,20},{20,16},{24,28},{28,24},{1,5},{5... | collective-permute-start | bytes 1179656 | tf_op jit(solution)/shard_map/ppermute | solution.py:23
  39.5 7.2 %collective-permute-done.6.far.refs_2_ = bf16[128,1536]{1,0:T(8,128)(2,1)} collective-permute-done((bf16[128,1536]{1,0:T(8,128)(2,1)S(1)}, bf16[128,1536]{1,0:T(8,128)(2,1)}, u32[]{:S(2)}, u32[]{:S(2)}) %collective-permute-start.6) | collective-permute-done | bytes 393248 | tf_op jit(solution)/shard_map/ppermute | solution.py:23
  47.9 2.0 %collective-permute-start.11 = (bf16[128,1536]{1,0:T(8,128)(2,1)}, bf16[128,1536]{1,0:T(8,128)(2,1)S(1)}, u32[]{:S(2)}, u32[]{:S(2)}) collective-permute-start(bf16[128,1536]{1,0:T(8,128)(2,1)} %collective-permute-done.6.far.refs_2_), channel_id=1, source_target_pairs={{0,4},{4,0},{8,12},{12,8},{16,20},{20,16},{24,28},{28,24},{1,5},{5... | collective-permute-start | bytes 1179656 | tf_op jit(solution)/shard_map/ppermute | solution.py:23
  49.9 1.5 %collective-permute-start.12 = (bf16[128,1536]{1,0:T(8,128)(2,1)}, bf16[128,1536]{1,0:T(8,128)(2,1)}, u32[]{:S(2)}, u32[]{:S(2)}) collective-permute-start(bf16[128,1536]{1,0:T(8,128)(2,1)} %get-tuple-element.55), channel_id=1, source_target_pairs={{0,2},{1,3},{2,0},{3,1},{4,6},{5,7},{6,4},{7,5},{8,10},{9,11},{10,... | collective-permute-start | bytes 1179656 | tf_op jit(solution)/shard_map/ppermute | solution.py:23
  51.4 4.8 %shard_map.85 = (bf16[128,1536]{1,0:T(8,128)(2,1)}, bf16[128,1536]{1,0:T(8,128)(2,1)}, bf16[8,192,128]{2,1,0:T(8,128)(2,1)}) custom-call(s32[4]{0:T(128)} %pad_add_fusion.where, bf16[128,1536]{1,0:T(8,128)(2,1)} %bitcast.12.mix, bf16[128,1536]{1,0:T(8,128)(2,1)} %bitcast.45, bf16[384,1536]{1,0:T(8,128)(2,1)} %w0.3, ...), custom_call_target="tpu_custom_call" | custom-call | flops 603979776 | bytes 6684688 | tf_op jit(solution)/shard_map/pallas_call | solution.py:49
  56.2 3.5 %all-to-all-start.2 = ((bf16[8,192,128]{2,1,0:T(8,128)(2,1)}), bf16[8,192,128]{2,1,0:T(8,128)(2,1)S(1)}, u32[]{:S(2)}, u32[]{:S(2)}) async-start(bf16[8,192,128]{2,1,0:T(8,128)(2,1)} %get-tuple-element.51), calls=%async_computation.2 | async-start | bytes 786432 | tf_op jit(solution)/shard_map/all_to_all | solution.py:257
  60.2 1.1 collective-permute-done.9.tok_side
  61.9 0.8 copy-done.9
  62.7 4.3 %shard_map.86 = bf16[8,4,16,384]{3,2,1,0:T(8,128)(2,1)} custom-call(s32[4]{0:T(128)} %pad_add_fusion.where, bf16[384,1536]{1,0:T(8,128)(2,1)} %refs_0_.1, bf16[128,1536]{1,0:T(8,128)(2,1)} %bitcast.46, bf16[128,1536]{1,0:T(8,128)(2,1)} %bitcast.48, bf16[128,1920]{1,0:T(8,128)(2,1)} %collective-permute-done.5.near.refs_1_, ...), custom_call_target="tpu_custom_call" | custom-call | flops 603979776 | bytes 4030480 | tf_op jit(solution)/shard_map/pallas_call | solution.py:49
  67.0 1.0 all-to-all-done.2.got
  68.0 4.9 %all-to-all-start.3 = ((bf16[32,16,384]{2,1,0:T(8,128)(2,1)}), bf16[32,16,384]{2,1,0:T(8,128)(2,1)S(1)}, u32[]{:S(2)}, u32[]{:S(2)}) async-start(bf16[32,16,384]{2,1,0:T(8,128)(2,1)} %bitcast.55), calls=%async_computation.3 | async-start | bytes 786432 | tf_op jit(solution)/shard_map/all_to_all | solution.py:282
  73.5 1.8 %collective-permute-start.17 = (bf16[128,1536]{1,0:T(8,128)(2,1)S(1)}, bf16[128,1536]{1,0:T(8,128)(2,1)S(1)}, u32[]{:S(2)}, u32[]{:S(2)}) collective-permute-start(bf16[128,1536]{1,0:T(8,128)(2,1)S(1)} %copy-done.16), channel_id=1, source_target_pairs={{0,2},{1,3},{2,0},{3,1},{4,6},{5,7},{6,4},{7,5},{8,10},{9,11},{10,... | collective-permute-start | bytes 1179656 | tf_op jit(solution)/shard_map/ppermute | solution.py:23
  75.3 1.5 %collective-permute-start.16 = (bf16[128,1536]{1,0:T(8,128)(2,1)}, bf16[128,1536]{1,0:T(8,128)(2,1)S(1)}, u32[]{:S(2)}, u32[]{:S(2)}) collective-permute-start(bf16[128,1536]{1,0:T(8,128)(2,1)} %collective-permute-done.12.refs_2_), channel_id=1, source_target_pairs={{0,4},{4,0},{8,12},{12,8},{16,20},{20,16},{24,28},{28,24},{1,5},{5... | collective-permute-start | bytes 1179656 | tf_op jit(solution)/shard_map/ppermute | solution.py:23
  76.8 0.7 copy-done.18
  77.5 0.8 copy-done.19
  78.3 4.3 %shard_map.87 = (f32[2,48,1536]{2,1,0:T(8,128)}, bf16[2,48,1536]{2,1,0:T(8,128)(2,1)}) custom-call(s32[4]{0:T(128)} %pad_add_fusion.where, bf16[8,192,128]{2,1,0:T(8,128)(2,1)} %copy-done.10, bf16[128,1536]{1,0:T(8,128)(2,1)} %bitcast.49, bf16[128,1920]{1,0:T(8,128)(2,1)} %collective-permute-done.5.near.refs_1_, ...), custom_call_target="tpu_custom_call" | custom-call | flops 603979776 | bytes 4522000 | tf_op jit(solution)/shard_map/pallas_call | solution.py:49
  82.6 1.5 %collective-permute-start.15 = (bf16[2,48,1536]{2,1,0:T(8,128)(2,1)}, bf16[2,48,1536]{2,1,0:T(8,128)(2,1)S(1)}, u32[]{:S(2)}, u32[]{:S(2)}) collective-permute-start(bf16[2,48,1536]{2,1,0:T(8,128)(2,1)} %get-tuple-element.61), channel_id=1, source_target_pairs={{0,8},{4,12},{8,0},{12,4},{16,24},{20,28},{24,16},{28,20},{1,9},{5... | collective-permute-start | bytes 884744 | tf_op jit(solution)/shard_map/ppermute | solution.py:23
  84.1 2.0 %all-to-all-done.3 = bf16[32,16,384]{2,1,0:T(8,128)(2,1)S(1)} async-done(((bf16[32,16,384]{2,1,0:T(8,128)(2,1)}), bf16[32,16,384]{2,1,0:T(8,128)(2,1)S(1)}, u32[]{:S(2)}, u32[]{:S(2)}) %all-to-all-start.3) | async-done | bytes 393248 | tf_op jit(solution)/shard_map/all_to_all | solution.py:282
  86.5 0.9 copy.36
  87.4 1.1 collective-permute-done.17.refs_4_
  88.4 0.8 collective-permute-done.16.refs_3_
  89.2 2.2 %collective-permute-done.15 = bf16[2,48,1536]{2,1,0:T(8,128)(2,1)S(1)} collective-permute-done((bf16[2,48,1536]{2,1,0:T(8,128)(2,1)}, bf16[2,48,1536]{2,1,0:T(8,128)(2,1)S(1)}, u32[]{:S(2)}, u32[]{:S(2)}) %collective-permute-start.15) | collective-permute-done | bytes 294944 | tf_op jit(solution)/shard_map/ppermute | solution.py:23
  91.4 0.7 copy-done.20
  92.7 4.5 %all-to-all-start.4 = ((bf16[8,4,16,384]{3,2,1,0:T(8,128)(2,1)}), bf16[8,4,16,384]{3,2,1,0:T(8,128)(2,1)S(1)}, u32[]{:S(2)}, u32[]{:S(2)}) async-start(bf16[8,4,16,384]{3,2,1,0:T(8,128)(2,1)} %bitcast.44), calls=%async_computation.4 | async-start | bytes 786432 | tf_op jit(solution)/shard_map/all_to_all | solution.py:40
  97.7 1.2 add_bitcast_fusion
  98.9 3.0 %collective-permute-start.18 = (bf16[1,48,1536]{2,1,0:T(8,128)(2,1)S(1)}, bf16[1,48,1536]{2,1,0:T(8,128)(2,1)}, u32[]{:S(2)}, u32[]{:S(2)}) collective-permute-start(bf16[1,48,1536]{2,1,0:T(8,128)(2,1)S(1)} %fusion.8), channel_id=1, source_target_pairs={{0,16},{4,20},{8,24},{12,28},{16,0},{20,4},{24,8},{28,12},{1,17},{... | collective-permute-start | bytes 442376 | tf_op jit(solution)/shard_map/ppermute | solution.py:23
  101.9 0.8 copy-done.15
  102.9 0.9 copy-done.11
  103.7 6.2 %shard_map.88 = (bf16[128,1536]{1,0:T(8,128)(2,1)}, f32[128,1536]{1,0:T(8,128)}) custom-call(s32[4]{0:T(128)} %pad_add_fusion.where, bf16[128,1536]{1,0:T(8,128)(2,1)} %get-tuple-element.66.gated, bf16[128,1536]{1,0:T(8,128)(2,1)} %get-tuple-element.67.mon, bf16[128,1536]{1,0:T(8,128)(2,1)} %bitcast.47, bf16[128,1536]{1,0:T(8,128)(2,1)} %bitcast.50, ...), custom_call_target="tpu_custom_call" | custom-call | flops 1207959552 | bytes 7471120 | tf_op jit(solution)/shard_map/pallas_call | solution.py:49
  109.9 3.5 %all-to-all-done.4.back = bf16[8,4,16,384]{3,2,1,0:T(8,128)(2,1)S(1)} async-done(((bf16[8,4,16,384]{3,2,1,0:T(8,128)(2,1)}), bf16[8,4,16,384]{3,2,1,0:T(8,128)(2,1)S(1)}, u32[]{:S(2)}, u32[]{:S(2)}) %all-to-all-start.4) | async-done | bytes 393248 | tf_op jit(solution)/shard_map/all_to_all | solution.py:40
  113.4 0.7 copy-done.8
  114.2 5.0 %shard_map.89 = bf16[128,1536]{1,0:T(8,128)(2,1)} custom-call(s32[4]{0:T(128)} %pad_add_fusion.where, bf16[8,4,16,384]{3,2,1,0:T(8,128)(2,1)} %copy-done.8, bf16[128,128]{1,0:T(8,128)(2,1)} %bitcast.58, f32[128,1536]{1,0:T(8,128)} %get-tuple-element.73.term, bf16[384,1536]{1,0:T(8,128)(2,1)} %w0.3, bf16[384,1536]{1,0:T(8,128)(2,1)} %collective-permute-done.4.w1, ...), custom_call_target="tpu_custom_call" | custom-call | flops 603979776 | bytes 6324240 | tf_op jit(solution)/shard_map/pallas_call | solution.py:49
  119.2 1.7 %fusion.7 = f32[48,1536]{1,0:T(8,128)} fusion(f32[1,2,48,1536]{3,2,1,0:T(8,128)S(1)} %add_bitcast_fusion, bf16[1,48,1536]{2,1,0:T(8,128)(2,1)} %collective-permute-done.18), kind=kLoop, calls=%fused_computation.13 | loop fusion | flops 221184 | bytes 737280 | tf_op jit(solution)/shard_map/div | solution.py:341
  (80 shorter events, 5.5 us)
Async XLA Ops:
  0.6 5.2 %copy-start.1 = (bf16[1,128,1536]{2,1,0:T(8,128)(2,1)S(1)}, bf16[1,128,1536]{2,1,0:T(8,128)(2,1)}, u32[]{:S(2)}) copy-start(bf16[1,128,1536]{2,1,0:T(8,128)(2,1)} %param.6) | copy-start | bytes 1179652
  0.6 5.2 %copy-start.23 = (bf16[1,128,128]{2,1,0:T(8,128)(2,1)S(1)}, bf16[1,128,128]{2,1,0:T(8,128)(2,1)}, u32[]{:S(2)}) copy-start(bf16[1,128,128]{2,1,0:T(8,128)(2,1)} %param.9) | copy-start | bytes 98308
  0.7 12.1 %copy-start.2 = (bf16[384,1536]{1,0:T(8,128)(2,1)S(1)}, bf16[384,1536]{1,0:T(8,128)(2,1)}, u32[]{:S(2)}) copy-start(bf16[384,1536]{1,0:T(8,128)(2,1)} %refs_0_.1) | copy-start | bytes 3538948
  2.9 9.8 %copy-start = (bf16[384,1536]{1,0:T(8,128)(2,1)S(1)}, bf16[384,1536]{1,0:T(8,128)(2,1)}, u32[]{:S(2)}) copy-start(bf16[384,1536]{1,0:T(8,128)(2,1)} %w0.3) | copy-start | bytes 3538948
  2.9 21.3 %collective-permute-start = (bf16[256,1536]{1,0:T(8,128)(2,1)}, bf16[256,1536]{1,0:T(8,128)(2,1)S(1)}, u32[]{:S(2)}, u32[]{:S(2)}) collective-permute-start(bf16[256,1536]{1,0:T(8,128)(2,1)} %slice.16), channel_id=1, source_target_pairs={{0,2},{1,3},{2,0},{3,1},{4,6},{5,7},{6,4},{7,5},{8,10},{9,11},{10,... | collective-permute-start | bytes 2359304 | tf_op jit(solution)/shard_map/ppermute | solution.py:23
  6.8 17.4 %all-to-all-start = ((bf16[8,16,1536]{2,1,0:T(8,128)(2,1)}), bf16[8,16,1536]{2,1,0:T(8,128)(2,1)}, u32[]{:S(2)}, u32[]{:S(2)}) async-start(bf16[8,16,1536]{2,1,0:T(8,128)(2,1)} %bitcast.54), calls=%async_computation | async-start | bytes 786432 | tf_op jit(solution)/shard_map/all_to_all | solution.py:40
  12.6 34.1 %collective-permute-start.4 = (bf16[384,1536]{1,0:T(8,128)(2,1)S(1)}, bf16[384,1536]{1,0:T(8,128)(2,1)}, u32[]{:S(2)}, u32[]{:S(2)}) collective-permute-start(bf16[384,1536]{1,0:T(8,128)(2,1)S(1)} %copy-done), channel_id=1, source_target_pairs={{0,1},{1,0},{2,3},{3,2},{4,5},{5,4},{6,7},{7,6},{8,9},{9,8},{10,11... | collective-permute-start | bytes 3538952 | tf_op jit(solution)/shard_map/ppermute | solution.py:23
  12.7 1.7 %copy-start.24 = (bf16[16,8,8]{0,2,1:T(8,128)(2,1)S(1)}, bf16[16,8,8]{0,2,1:T(8,128)(2,1)}, u32[]{:S(2)}) copy-start(bf16[16,8,8]{0,2,1:T(8,128)(2,1)} %param.10) | copy-start | bytes 6148
  24.2 3.3 %copy-start.5 = (bf16[256,1536]{1,0:T(8,128)(2,1)}, bf16[256,1536]{1,0:T(8,128)(2,1)S(1)}, u32[]{:S(2)}) copy-start(bf16[256,1536]{1,0:T(8,128)(2,1)S(1)} %collective-permute-done.w2) | copy-start | bytes 2359300
  24.2 9.1 %copy-start.4 = (bf16[1,128,1536]{2,1,0:T(8,128)(2,1)S(1)}, bf16[1,128,1536]{2,1,0:T(8,128)(2,1)}, u32[]{:S(2)}) copy-start(bf16[1,128,1536]{2,1,0:T(8,128)(2,1)} %param.11) | copy-start | bytes 1179652
  24.2 11.6 %collective-permute-start.1 = (bf16[128,1536]{1,0:T(8,128)(2,1)}, bf16[128,1536]{1,0:T(8,128)(2,1)S(1)}, u32[]{:S(2)}, u32[]{:S(2)}) collective-permute-start(bf16[128,1536]{1,0:T(8,128)(2,1)} %slice.17), channel_id=1, source_target_pairs={{0,2},{1,3},{2,0},{3,1},{4,6},{5,7},{6,4},{7,5},{8,10},{9,11},{10,... | collective-permute-start | bytes 1179656 | tf_op jit(solution)/shard_map/ppermute | solution.py:23
  25.3 21.4 %collective-permute-start.2 = (bf16[256,1536]{1,0:T(8,128)(2,1)S(1)}, bf16[256,1536]{1,0:T(8,128)(2,1)S(1)}, u32[]{:S(2)}, u32[]{:S(2)}) collective-permute-start(bf16[256,1536]{1,0:T(8,128)(2,1)S(1)} %collective-permute-done.w2), channel_id=1, source_target_pairs={{0,1},{1,0},{2,3},{3,2},{4,5},{5,4},{6,7},{7,6},{8,9},{9,8},{10,11... | collective-permute-start | bytes 2359304 | tf_op jit(solution)/shard_map/ppermute | solution.py:23
  27.5 19.2 %all-to-all-start.1 = ((bf16[8,16,1536]{2,1,0:T(8,128)(2,1)}), bf16[8,16,1536]{2,1,0:T(8,128)(2,1)}, u32[]{:S(2)}, u32[]{:S(2)}) async-start(bf16[8,16,1536]{2,1,0:T(8,128)(2,1)} %copy.22), calls=%async_computation.1 | async-start | bytes 786432 | tf_op jit(solution)/shard_map/all_to_all | solution.py:40
  35.0 2.6 %collective-permute-start.5 = (bf16[128,1920]{1,0:T(8,128)(2,1)}, bf16[128,1920]{1,0:T(8,128)(2,1)}, u32[]{:S(2)}, u32[]{:S(2)}) collective-permute-start(bf16[128,1920]{1,0:T(8,128)(2,1)} %pad_maximum_fusion), channel_id=1, source_target_pairs={{0,1},{1,0},{2,3},{3,2},{4,5},{5,4},{6,7},{7,6},{8,9},{9,8},{10,11... | collective-permute-start | bytes 1474568 | tf_op jit(solution)/shard_map/ppermute | solution.py:23
  35.3 11.4 %collective-permute-start.6 = (bf16[128,1536]{1,0:T(8,128)(2,1)S(1)}, bf16[128,1536]{1,0:T(8,128)(2,1)}, u32[]{:S(2)}, u32[]{:S(2)}) collective-permute-start(bf16[128,1536]{1,0:T(8,128)(2,1)S(1)} %bitcast.52), channel_id=1, source_target_pairs={{0,2},{1,3},{2,0},{3,1},{4,6},{5,7},{6,4},{7,5},{8,10},{9,11},{10,... | collective-permute-start | bytes 1179656 | tf_op jit(solution)/shard_map/ppermute | solution.py:23
  35.8 15.6 %copy-start.7 = (bf16[128,1536]{1,0:T(8,128)(2,1)}, bf16[128,1536]{1,0:T(8,128)(2,1)S(1)}, u32[]{:S(2)}) copy-start(bf16[128,1536]{1,0:T(8,128)(2,1)S(1)} %collective-permute-done.1.w3) | copy-start | bytes 1179652
  35.8 10.9 %collective-permute-start.3 = (bf16[128,1536]{1,0:T(8,128)(2,1)S(1)}, bf16[128,1536]{1,0:T(8,128)(2,1)}, u32[]{:S(2)}, u32[]{:S(2)}) collective-permute-start(bf16[128,1536]{1,0:T(8,128)(2,1)S(1)} %collective-permute-done.1.w3), channel_id=1, source_target_pairs={{0,1},{1,0},{2,3},{3,2},{4,5},{5,4},{6,7},{7,6},{8,9},{9,8},{10,11... | collective-permute-start | bytes 1179656 | tf_op jit(solution)/shard_map/ppermute | solution.py:23
  37.6 29.4 %collective-permute-start.10 = (bf16[128,1536]{1,0:T(8,128)(2,1)S(1)}, bf16[128,1536]{1,0:T(8,128)(2,1)}, u32[]{:S(2)}, u32[]{:S(2)}) collective-permute-start(bf16[128,1536]{1,0:T(8,128)(2,1)S(1)} %bitcast.53), channel_id=1, source_target_pairs={{0,4},{4,0},{8,12},{12,8},{16,20},{20,16},{24,28},{28,24},{1,5},{5... | collective-permute-start | bytes 1179656 | tf_op jit(solution)/shard_map/ppermute | solution.py:23
  46.7 4.7 %copy-start.6 = (bf16[256,1536]{1,0:T(8,128)(2,1)}, bf16[256,1536]{1,0:T(8,128)(2,1)S(1)}, u32[]{:S(2)}) copy-start(bf16[256,1536]{1,0:T(8,128)(2,1)S(1)} %collective-permute-done.2.w4) | copy-start | bytes 2359300
  46.7 13.0 %collective-permute-start.8 = (bf16[128,768]{1,0:T(8,128)(2,1)}, bf16[128,768]{1,0:T(8,128)(2,1)S(1)}, u32[]{:S(2)}, u32[]{:S(2)}) collective-permute-start(bf16[128,768]{1,0:T(8,128)(2,1)} %pad_maximum_fusion.1), channel_id=1, source_target_pairs={{0,2},{1,3},{2,0},{3,1},{4,6},{5,7},{6,4},{7,5},{8,10},{9,11},{10,... | collective-permute-start | bytes 589832 | tf_op jit(solution)/shard_map/ppermute | solution.py:23
  47.3 13.9 %collective-permute-start.7 = (bf16[128,1536]{1,0:T(8,128)(2,1)}, bf16[128,1536]{1,0:T(8,128)(2,1)S(1)}, u32[]{:S(2)}, u32[]{:S(2)}) collective-permute-start(bf16[128,1536]{1,0:T(8,128)(2,1)} %collective-permute-done.6.far.refs_2_), channel_id=1, source_target_pairs={{0,1},{1,0},{2,3},{3,2},{4,5},{5,4},{6,7},{7,6},{8,9},{9,8},{10,11... | collective-permute-start | bytes 1179656 | tf_op jit(solution)/shard_map/ppermute | solution.py:23
  47.9 20.0 %collective-permute-start.11 = (bf16[128,1536]{1,0:T(8,128)(2,1)}, bf16[128,1536]{1,0:T(8,128)(2,1)S(1)}, u32[]{:S(2)}, u32[]{:S(2)}) collective-permute-start(bf16[128,1536]{1,0:T(8,128)(2,1)} %collective-permute-done.6.far.refs_2_), channel_id=1, source_target_pairs={{0,4},{4,0},{8,12},{12,8},{16,20},{20,16},{24,28},{28,24},{1,5},{5... | collective-permute-start | bytes 1179656 | tf_op jit(solution)/shard_map/ppermute | solution.py:23
  49.9 18.0 %collective-permute-start.12 = (bf16[128,1536]{1,0:T(8,128)(2,1)}, bf16[128,1536]{1,0:T(8,128)(2,1)}, u32[]{:S(2)}, u32[]{:S(2)}) collective-permute-start(bf16[128,1536]{1,0:T(8,128)(2,1)} %get-tuple-element.55), channel_id=1, source_target_pairs={{0,2},{1,3},{2,0},{3,1},{4,6},{5,7},{6,4},{7,5},{8,10},{9,11},{10,... | collective-permute-start | bytes 1179656 | tf_op jit(solution)/shard_map/ppermute | solution.py:23
  56.2 11.7 %all-to-all-start.2 = ((bf16[8,192,128]{2,1,0:T(8,128)(2,1)}), bf16[8,192,128]{2,1,0:T(8,128)(2,1)S(1)}, u32[]{:S(2)}, u32[]{:S(2)}) async-start(bf16[8,192,128]{2,1,0:T(8,128)(2,1)} %get-tuple-element.51), calls=%async_computation.2 | async-start | bytes 786432 | tf_op jit(solution)/shard_map/all_to_all | solution.py:257
  59.7 13.8 %copy-start.16 = (bf16[128,1536]{1,0:T(8,128)(2,1)S(1)}, bf16[128,1536]{1,0:T(8,128)(2,1)}, u32[]{:S(2)}) copy-start(bf16[128,1536]{1,0:T(8,128)(2,1)} %get-tuple-element.64) | copy-start | bytes 1179652
  59.7 1.5 %copy-start.21 = (bf16[128,768]{1,0:T(8,128)(2,1)}, bf16[128,768]{1,0:T(8,128)(2,1)S(1)}, u32[]{:S(2)}) copy-start(bf16[128,768]{1,0:T(8,128)(2,1)S(1)} %collective-permute-done.8.tok_far) | copy-start | bytes 589828
  59.7 1.5 %collective-permute-start.9 = (bf16[128,768]{1,0:T(8,128)(2,1)S(1)}, bf16[128,768]{1,0:T(8,128)(2,1)S(1)}, u32[]{:S(2)}, u32[]{:S(2)}) collective-permute-start(bf16[128,768]{1,0:T(8,128)(2,1)S(1)} %collective-permute-done.8.tok_far), channel_id=1, source_target_pairs={{0,1},{1,0},{2,3},{3,2},{4,5},{5,4},{6,7},{7,6},{8,9},{9,8},{10,11... | collective-permute-start | bytes 589832 | tf_op jit(solution)/shard_map/ppermute | solution.py:23
  67.9 8.8 %copy-start.10 = (bf16[8,192,128]{2,1,0:T(8,128)(2,1)}, bf16[8,192,128]{2,1,0:T(8,128)(2,1)S(1)}, u32[]{:S(2)}) copy-start(bf16[8,192,128]{2,1,0:T(8,128)(2,1)S(1)} %all-to-all-done.2.got) | copy-start | bytes 1179652
  68.0 8.8 %copy-start.17 = (bf16[128,1536]{1,0:T(8,128)(2,1)}, bf16[128,1536]{1,0:T(8,128)(2,1)S(1)}, u32[]{:S(2)}) copy-start(bf16[128,1536]{1,0:T(8,128)(2,1)S(1)} %collective-permute-done.11.refs_6_) | copy-start | bytes 1179652
  68.0 18.2 %all-to-all-start.3 = ((bf16[32,16,384]{2,1,0:T(8,128)(2,1)}), bf16[32,16,384]{2,1,0:T(8,128)(2,1)S(1)}, u32[]{:S(2)}, u32[]{:S(2)}) async-start(bf16[32,16,384]{2,1,0:T(8,128)(2,1)} %bitcast.55), calls=%async_computation.3 | async-start | bytes 786432 | tf_op jit(solution)/shard_map/all_to_all | solution.py:282
  72.9 3.8 %collective-permute-start.13 = (bf16[128,1536]{1,0:T(8,128)(2,1)}, bf16[128,1536]{1,0:T(8,128)(2,1)S(1)}, u32[]{:S(2)}, u32[]{:S(2)}) collective-permute-start(bf16[128,1536]{1,0:T(8,128)(2,1)} %collective-permute-done.10.refs_4_), channel_id=1, source_target_pairs={{0,1},{1,0},{2,3},{3,2},{4,5},{5,4},{6,7},{7,6},{8,9},{9,8},{10,11... | collective-permute-start | bytes 1179656 | tf_op jit(solution)/shard_map/ppermute | solution.py:23
  73.2 3.5 %collective-permute-start.14 = (bf16[128,1536]{1,0:T(8,128)(2,1)S(1)}, bf16[128,1536]{1,0:T(8,128)(2,1)S(1)}, u32[]{:S(2)}, u32[]{:S(2)}) collective-permute-start(bf16[128,1536]{1,0:T(8,128)(2,1)S(1)} %collective-permute-done.11.refs_6_), channel_id=1, source_target_pairs={{0,1},{1,0},{2,3},{3,2},{4,5},{5,4},{6,7},{7,6},{8,9},{9,8},{10,11... | collective-permute-start | bytes 1179656 | tf_op jit(solution)/shard_map/ppermute | solution.py:23
  73.5 14.9 %collective-permute-start.17 = (bf16[128,1536]{1,0:T(8,128)(2,1)S(1)}, bf16[128,1536]{1,0:T(8,128)(2,1)S(1)}, u32[]{:S(2)}, u32[]{:S(2)}) collective-permute-start(bf16[128,1536]{1,0:T(8,128)(2,1)S(1)} %copy-done.16), channel_id=1, source_target_pairs={{0,2},{1,3},{2,0},{3,1},{4,6},{5,7},{6,4},{7,5},{8,10},{9,11},{10,... | collective-permute-start | bytes 1179656 | tf_op jit(solution)/shard_map/ppermute | solution.py:23
  75.3 13.9 %collective-permute-start.16 = (bf16[128,1536]{1,0:T(8,128)(2,1)}, bf16[128,1536]{1,0:T(8,128)(2,1)S(1)}, u32[]{:S(2)}, u32[]{:S(2)}) collective-permute-start(bf16[128,1536]{1,0:T(8,128)(2,1)} %collective-permute-done.12.refs_2_), channel_id=1, source_target_pairs={{0,4},{4,0},{8,12},{12,8},{16,20},{20,16},{24,28},{28,24},{1,5},{5... | collective-permute-start | bytes 1179656 | tf_op jit(solution)/shard_map/ppermute | solution.py:23
  77.5 0.8 copy-start.19
  82.6 9.6 %copy-start.3 = (bf16[384,1536]{1,0:T(8,128)(2,1)S(1)}, bf16[384,1536]{1,0:T(8,128)(2,1)}, u32[]{:S(2)}) copy-start(bf16[384,1536]{1,0:T(8,128)(2,1)} %refs_0_.1) | copy-start | bytes 3538948
  82.6 8.9 %collective-permute-start.15 = (bf16[2,48,1536]{2,1,0:T(8,128)(2,1)}, bf16[2,48,1536]{2,1,0:T(8,128)(2,1)S(1)}, u32[]{:S(2)}, u32[]{:S(2)}) collective-permute-start(bf16[2,48,1536]{2,1,0:T(8,128)(2,1)} %get-tuple-element.61), channel_id=1, source_target_pairs={{0,8},{4,12},{8,0},{12,4},{16,24},{20,28},{24,16},{28,20},{1,9},{5... | collective-permute-start | bytes 884744 | tf_op jit(solution)/shard_map/ppermute | solution.py:23
  88.4 4.2 %copy-start.12 = (bf16[128,1536]{1,0:T(8,128)(2,1)}, bf16[128,1536]{1,0:T(8,128)(2,1)S(1)}, u32[]{:S(2)}) copy-start(bf16[128,1536]{1,0:T(8,128)(2,1)S(1)} %collective-permute-done.17.refs_4_) | copy-start | bytes 1179652
  89.2 2.2 %copy-start.13 = (bf16[128,1536]{1,0:T(8,128)(2,1)}, bf16[128,1536]{1,0:T(8,128)(2,1)S(1)}, u32[]{:S(2)}) copy-start(bf16[128,1536]{1,0:T(8,128)(2,1)S(1)} %collective-permute-done.16.refs_3_) | copy-start | bytes 1179652
  92.1 9.8 %collective-permute-start.19 = (bf16[384,1536]{1,0:T(8,128)(2,1)S(1)}, bf16[384,1536]{1,0:T(8,128)(2,1)S(1)}, u32[]{:S(2)}, u32[]{:S(2)}) collective-permute-start(bf16[384,1536]{1,0:T(8,128)(2,1)S(1)} %copy-done.3), channel_id=1, source_target_pairs={{0,1},{1,0},{2,3},{3,2},{4,5},{5,4},{6,7},{7,6},{8,9},{9,8},{10,11... | collective-permute-start | bytes 3538952 | tf_op jit(solution)/shard_map/ppermute | solution.py:23
  92.2 9.7 %collective-permute-start.20 = (bf16[128,1536]{1,0:T(8,128)(2,1)}, bf16[128,1536]{1,0:T(8,128)(2,1)}, u32[]{:S(2)}, u32[]{:S(2)}) collective-permute-start(bf16[128,1536]{1,0:T(8,128)(2,1)} %collective-permute-done.12.refs_2_), channel_id=1, source_target_pairs={{0,1},{1,0},{2,3},{3,2},{4,5},{5,4},{6,7},{7,6},{8,9},{9,8},{10,11... | collective-permute-start | bytes 1179656 | tf_op jit(solution)/shard_map/ppermute | solution.py:23
  92.7 20.8 %all-to-all-start.4 = ((bf16[8,4,16,384]{3,2,1,0:T(8,128)(2,1)}), bf16[8,4,16,384]{3,2,1,0:T(8,128)(2,1)S(1)}, u32[]{:S(2)}, u32[]{:S(2)}) async-start(bf16[8,4,16,384]{3,2,1,0:T(8,128)(2,1)} %bitcast.44), calls=%async_computation.4 | async-start | bytes 786432 | tf_op jit(solution)/shard_map/all_to_all | solution.py:40
  97.1 4.7 %collective-permute-start.21 = (bf16[128,1536]{1,0:T(8,128)(2,1)}, bf16[128,1536]{1,0:T(8,128)(2,1)S(1)}, u32[]{:S(2)}, u32[]{:S(2)}) collective-permute-start(bf16[128,1536]{1,0:T(8,128)(2,1)} %copy-done.13), channel_id=1, source_target_pairs={{0,1},{1,0},{2,3},{3,2},{4,5},{5,4},{6,7},{7,6},{8,9},{9,8},{10,11... | collective-permute-start | bytes 1179656 | tf_op jit(solution)/shard_map/ppermute | solution.py:23
  97.2 4.7 %collective-permute-start.22 = (bf16[128,1536]{1,0:T(8,128)(2,1)}, bf16[128,1536]{1,0:T(8,128)(2,1)S(1)}, u32[]{:S(2)}, u32[]{:S(2)}) collective-permute-start(bf16[128,1536]{1,0:T(8,128)(2,1)} %copy-done.12), channel_id=1, source_target_pairs={{0,1},{1,0},{2,3},{3,2},{4,5},{5,4},{6,7},{7,6},{8,9},{9,8},{10,11... | collective-permute-start | bytes 1179656 | tf_op jit(solution)/shard_map/ppermute | solution.py:23
  98.9 20.3 %collective-permute-start.18 = (bf16[1,48,1536]{2,1,0:T(8,128)(2,1)S(1)}, bf16[1,48,1536]{2,1,0:T(8,128)(2,1)}, u32[]{:S(2)}, u32[]{:S(2)}) collective-permute-start(bf16[1,48,1536]{2,1,0:T(8,128)(2,1)S(1)} %fusion.8), channel_id=1, source_target_pairs={{0,16},{4,20},{8,24},{12,28},{16,0},{20,4},{24,8},{28,12},{1,17},{... | collective-permute-start | bytes 442376 | tf_op jit(solution)/shard_map/ppermute | solution.py:23
  101.9 1.0 copy-start.14
  101.9 0.8 copy-start.15
  102.7 1.0 copy-start.11
  (5 other events, 3.7 us)

commit v4 on v3

--- a/solution.py
+++ b/solution.py
@@ -303,7 +303,8 @@
         total = (total[:, 0], total[:, 1].astype(BF16))
     kept, sent = total
     sent = swap(sent, "seq", 2)
-    sent, back, w_late, out_b, out_c = join((sent, back, w_out, out_b, out_c))
+    sent, back = join((sent, back))
+    w_late = w_out
     total = kept + sent.astype(F32)
     bit = 2
 
@@ -332,6 +333,7 @@
         term,
         *w_ins,
         flops=flops,
+        room=40,
     )
     ready = (mixed, input_grad)
     while total.shape[0] > 1:

time: 122 us -> 120 us (0.984)
  starting transfers between devices: 45.1 us -> 43.4 us
    all_to_all x1, waiting for transfers between devices: 2.01 us -> 0.01 us  [on_device(): lax.all_to_all(grads, ('seq', 'dp'), split_axis=0, concat_axis=0, tiled=T...]
    unnamed x52 -> x54, local copies, waits for them, and re-layouts: 7.16 us -> 6.5 us
  transfers between devices with their start and end apart: 28 -> 28, of which waited for: 9 -> 8; matrix products, arithmetic and copies ran while one was open for 11% -> 14% of each run, Pallas kernels for 20% -> 20%
where the time goes in v4:
time: 120 us; the launch traced here: 119 us
  starting transfers between devices  43.4 us (36%)
  waiting for transfers between devices  26.3 us (22%)
  Pallas kernels  23.4 us (20%)
  local copies, waits for them, and re-layouts  14.7 us (12%)
  other arithmetic  7.1 us (6%)
  matrix products  3.42 us (3%)
    pallas_call x5, Pallas kernels, call(): pl.pallas_call(kernel, out_shape=list(outs), in_specs=[SMEM if x.dtype ==...  23.4 us
    ppermute x23, starting transfers between devices, swap(): return lax.ppermute(x, axis, [(i, i ^ bit) for i in range(n)])  20.1 us
    all_to_all x3, starting transfers between devices, spread(): return lax.all_to_all(x, 'seq', split_axis=0, concat_axis=0, tiled=True)  16.1 us
    ppermute x23, waiting for transfers between devices, swap(): return lax.ppermute(x, axis, [(i, i ^ bit) for i in range(n)])  12.9 us
    all_to_all x3, waiting for transfers between devices, spread(): return lax.all_to_all(x, 'seq', split_axis=0, concat_axis=0, tiled=True)  11.2 us
    unnamed x54, local copies, waits for them, and re-layouts  6.5 us
    all_to_all x1, starting transfers between devices, on_device(): lax.all_to_all(grads, ('seq', 'dp'), split_axis=0, concat_axis=0, tiled=T...  3.73 us
    all_to_all x1, starting transfers between devices, on_device(): lax.all_to_all(turned, ('seq', 'dp'), split_axis=0, concat_axis=0, tiled=...  3.45 us
  transfers between devices with their start and end apart: 28, of which 8 were waited for; matrix products, arithmetic and copies ran while one was open for 14% of the time, Pallas kernels for 20%

profile of v4, /device:TPU:0, one launch (start us, length us, event | category | flops | bytes accessed | tf_op | source)
XLA Modules:
  0.0 119.3 jit_solution(7728057398751896987)
XLA Ops:
  0.7 2.2 %slice.16 = bf16[256,1536]{1,0:T(8,128)(2,1)} slice(bf16[384,1536]{1,0:T(8,128)(2,1)} %w0.3), slice={[0:256], [0:1536]} | slice | bytes 1572864 | tf_op jit(solution)/shard_map/slice | solution.py:211
  2.8 2.9 %collective-permute-start = (bf16[256,1536]{1,0:T(8,128)(2,1)}, bf16[256,1536]{1,0:T(8,128)(2,1)S(1)}, u32[]{:S(2)}, u32[]{:S(2)}) collective-permute-start(bf16[256,1536]{1,0:T(8,128)(2,1)} %slice.16), channel_id=1, source_target_pairs={{0,2},{1,3},{2,0},{3,1},{4,6},{5,7},{6,4},{7,5},{8,10},{9,11},{10,... | collective-permute-start | bytes 2359304 | tf_op jit(solution)/shard_map/ppermute | solution.py:23
  5.8 1.0 convolution_convert_fusion.1
  6.8 5.8 %all-to-all-start = ((bf16[8,16,1536]{2,1,0:T(8,128)(2,1)}), bf16[8,16,1536]{2,1,0:T(8,128)(2,1)}, u32[]{:S(2)}, u32[]{:S(2)}) async-start(bf16[8,16,1536]{2,1,0:T(8,128)(2,1)} %bitcast.6), calls=%async_computation | async-start | bytes 786432 | tf_op jit(solution)/shard_map/all_to_all | solution.py:40
  12.7 2.1 %fusion.11 = (bf16[128,1536]{1,0:T(8,128)(2,1)}, bf16[128,1536]{1,0:T(8,128)(2,1)}) fusion(bf16[384,1536]{1,0:T(8,128)(2,1)} %refs_0_.1, s32[]{:T(128)S(6)} %select_n.32), kind=kLoop, calls=%fused_computation.24 | loop fusion | bytes 1572868 | tf_op jit(solution)/shard_map/slice | solution.py:216
  14.8 0.8 slice.17
  15.5 0.7 copy.21
  16.2 0.7 dynamic-slice_bitcast_fusion.1
  16.9 7.2 %all-to-all-done = bf16[8,16,1536]{2,1,0:T(8,128)(2,1)} async-done(((bf16[8,16,1536]{2,1,0:T(8,128)(2,1)}), bf16[8,16,1536]{2,1,0:T(8,128)(2,1)}, u32[]{:S(2)}, u32[]{:S(2)}) %all-to-all-start) | async-done | bytes 393248 | tf_op jit(solution)/shard_map/all_to_all | solution.py:40
  24.1 1.1 collective-permute-start.1
  25.2 1.3 %fusion = bf16[8,16,1536]{2,0,1:T(8,128)(2,1)S(1)} fusion(bf16[16,8,8]{2,1,0:T(8,128)(2,1)} %copy.21, bf16[8,16,1536]{2,1,0:T(8,128)(2,1)} %all-to-all-done), kind=kOutput, calls=%fused_computation.2 | convolution fusion | flops 3342336 | bytes 788480 | tf_op jit(solution)/shard_map/sab,bsd->asd/dot_general | solution.py:219
  26.6 0.9 copy.22
  27.4 5.8 %all-to-all-start.1 = ((bf16[8,16,1536]{2,1,0:T(8,128)(2,1)}), bf16[8,16,1536]{2,1,0:T(8,128)(2,1)}, u32[]{:S(2)}, u32[]{:S(2)}) async-start(bf16[8,16,1536]{2,1,0:T(8,128)(2,1)} %copy.22), calls=%async_computation.1 | async-start | bytes 786432 | tf_op jit(solution)/shard_map/all_to_all | solution.py:40
  33.3 1.9 %pad_maximum_fusion = bf16[128,1920]{1,0:T(8,128)(2,1)} fusion(bf16[128,384]{1,0:T(8,128)(2,1)} %get-tuple-element.74, bf16[128,1536]{1,0:T(8,128)(2,1)} %bitcast.49), kind=kLoop, calls=%fused_computation.5 | loop fusion | flops 983040 | bytes 983040 | tf_op jit(solution)/shard_map/concatenate | solution.py:225
  36.0 1.8 %pad_maximum_fusion.1 = bf16[128,768]{1,0:T(8,128)(2,1)} fusion(bf16[128,384]{1,0:T(8,128)(2,1)} %get-tuple-element.75, bf16[128,384]{1,0:T(8,128)(2,1)} %get-tuple-element.73), kind=kLoop, calls=%fused_computation.15 | loop fusion | flops 393216 | bytes 393216 | tf_op jit(solution)/shard_map/concatenate | solution.py:226
  37.7 1.9 %collective-permute-start.10 = (bf16[128,1536]{1,0:T(8,128)(2,1)}, bf16[128,1536]{1,0:T(8,128)(2,1)}, u32[]{:S(2)}, u32[]{:S(2)}) collective-permute-start(bf16[128,1536]{1,0:T(8,128)(2,1)} %bitcast.51), channel_id=1, source_target_pairs={{0,4},{4,0},{8,12},{12,8},{16,20},{20,16},{24,28},{28,24},{1,5},{5... | collective-permute-start | bytes 1179656 | tf_op jit(solution)/shard_map/ppermute | solution.py:23
  39.6 7.4 %collective-permute-done.6.far.refs_2_ = bf16[128,1536]{1,0:T(8,128)(2,1)} collective-permute-done((bf16[128,1536]{1,0:T(8,128)(2,1)}, bf16[128,1536]{1,0:T(8,128)(2,1)}, u32[]{:S(2)}, u32[]{:S(2)}) %collective-permute-start.6) | collective-permute-done | bytes 393248 | tf_op jit(solution)/shard_map/ppermute | solution.py:23
  47.7 0.6 pad_add_fusion.where
  48.3 2.0 %collective-permute-start.11 = (bf16[128,1536]{1,0:T(8,128)(2,1)}, bf16[128,1536]{1,0:T(8,128)(2,1)S(1)}, u32[]{:S(2)}, u32[]{:S(2)}) collective-permute-start(bf16[128,1536]{1,0:T(8,128)(2,1)} %collective-permute-done.6.far.refs_2_), channel_id=1, source_target_pairs={{0,4},{4,0},{8,12},{12,8},{16,20},{20,16},{24,28},{28,24},{1,5},{5... | collective-permute-start | bytes 1179656 | tf_op jit(solution)/shard_map/ppermute | solution.py:23
  50.3 1.5 %collective-permute-start.12 = (bf16[128,1536]{1,0:T(8,128)(2,1)}, bf16[128,1536]{1,0:T(8,128)(2,1)}, u32[]{:S(2)}, u32[]{:S(2)}) collective-permute-start(bf16[128,1536]{1,0:T(8,128)(2,1)} %get-tuple-element.52), channel_id=1, source_target_pairs={{0,2},{1,3},{2,0},{3,1},{4,6},{5,7},{6,4},{7,5},{8,10},{9,11},{10,... | collective-permute-start | bytes 1179656 | tf_op jit(solution)/shard_map/ppermute | solution.py:23
  51.8 4.8 %shard_map.85 = (bf16[128,1536]{1,0:T(8,128)(2,1)}, bf16[128,1536]{1,0:T(8,128)(2,1)}, bf16[8,192,128]{2,1,0:T(8,128)(2,1)}) custom-call(s32[4]{0:T(128)} %pad_add_fusion.where, bf16[128,1536]{1,0:T(8,128)(2,1)} %bitcast.12.mix, bf16[128,1536]{1,0:T(8,128)(2,1)} %bitcast.46, bf16[384,1536]{1,0:T(8,128)(2,1)} %w0.3, bf16[384,1536]{1,0:T(8,128)(2,1)} %copy-done.2, ...), custom_call_target="tpu_custom_call" | custom-call | flops 603979776 | bytes 6684688 | tf_op jit(solution)/shard_map/pallas_call | solution.py:49
  56.6 3.5 %all-to-all-start.2 = ((bf16[8,192,128]{2,1,0:T(8,128)(2,1)}), bf16[8,192,128]{2,1,0:T(8,128)(2,1)S(1)}, u32[]{:S(2)}, u32[]{:S(2)}) async-start(bf16[8,192,128]{2,1,0:T(8,128)(2,1)} %get-tuple-element.48), calls=%async_computation.2 | async-start | bytes 786432 | tf_op jit(solution)/shard_map/all_to_all | solution.py:257
  60.6 1.1 collective-permute-done.9.tok_side
  61.6 0.7 copy-done.24
  62.3 4.2 %shard_map.86 = bf16[8,4,16,384]{3,2,1,0:T(8,128)(2,1)} custom-call(s32[4]{0:T(128)} %pad_add_fusion.where, bf16[384,1536]{1,0:T(8,128)(2,1)} %refs_0_.1, bf16[128,1536]{1,0:T(8,128)(2,1)} %bitcast.47, bf16[128,1536]{1,0:T(8,128)(2,1)} %bitcast.52, bf16[128,1920]{1,0:T(8,128)(2,1)} %collective-permute-done.5.near.refs_1_, ...), custom_call_target="tpu_custom_call" | custom-call | flops 603979776 | bytes 4030480 | tf_op jit(solution)/shard_map/pallas_call | solution.py:49
  66.5 2.2 %all-to-all-done.2.got = bf16[8,192,128]{2,1,0:T(8,128)(2,1)S(1)} async-done(((bf16[8,192,128]{2,1,0:T(8,128)(2,1)}), bf16[8,192,128]{2,1,0:T(8,128)(2,1)S(1)}, u32[]{:S(2)}, u32[]{:S(2)}) %all-to-all-start.2) | async-done | bytes 393248 | tf_op jit(solution)/shard_map/all_to_all | solution.py:257
  68.7 3.7 %all-to-all-start.3 = ((bf16[32,16,384]{2,1,0:T(8,128)(2,1)}), bf16[32,16,384]{2,1,0:T(8,128)(2,1)S(1)}, u32[]{:S(2)}, u32[]{:S(2)}) async-start(bf16[32,16,384]{2,1,0:T(8,128)(2,1)} %bitcast.55), calls=%async_computation.3 | async-start | bytes 786432 | tf_op jit(solution)/shard_map/all_to_all | solution.py:282
  73.1 1.8 %collective-permute-start.18 = (bf16[128,1536]{1,0:T(8,128)(2,1)}, bf16[128,1536]{1,0:T(8,128)(2,1)S(1)}, u32[]{:S(2)}, u32[]{:S(2)}) collective-permute-start(bf16[128,1536]{1,0:T(8,128)(2,1)} %collective-permute-done.12.refs_2_), channel_id=1, source_target_pairs={{0,4},{4,0},{8,12},{12,8},{16,20},{20,16},{24,28},{28,24},{1,5},{5... | collective-permute-start | bytes 1179656 | tf_op jit(solution)/shard_map/ppermute | solution.py:23
  74.8 1.5 %collective-permute-start.19 = (bf16[128,1536]{1,0:T(8,128)(2,1)}, bf16[128,1536]{1,0:T(8,128)(2,1)}, u32[]{:S(2)}, u32[]{:S(2)}) collective-permute-start(bf16[128,1536]{1,0:T(8,128)(2,1)} %get-tuple-element.64), channel_id=1, source_target_pairs={{0,2},{1,3},{2,0},{3,1},{4,6},{5,7},{6,4},{7,5},{8,10},{9,11},{10,... | collective-permute-start | bytes 1179656 | tf_op jit(solution)/shard_map/ppermute | solution.py:23
  76.3 0.7 copy-done.21
  77.1 0.8 copy-done.22
  77.8 4.3 %shard_map.87 = (f32[2,48,1536]{2,1,0:T(8,128)}, bf16[2,48,1536]{2,1,0:T(8,128)(2,1)}) custom-call(s32[4]{0:T(128)} %pad_add_fusion.where, bf16[8,192,128]{2,1,0:T(8,128)(2,1)} %copy-done.17, bf16[128,1536]{1,0:T(8,128)(2,1)} %bitcast.53, bf16[128,1920]{1,0:T(8,128)(2,1)} %collective-permute-done.5.near.refs_1_, ...), custom_call_target="tpu_custom_call" | custom-call | flops 603979776 | bytes 4522000 | tf_op jit(solution)/shard_map/pallas_call | solution.py:49
  82.1 1.5 %collective-permute-start.15 = (bf16[2,48,1536]{2,1,0:T(8,128)(2,1)}, bf16[2,48,1536]{2,1,0:T(8,128)(2,1)}, u32[]{:S(2)}, u32[]{:S(2)}) collective-permute-start(bf16[2,48,1536]{2,1,0:T(8,128)(2,1)} %get-tuple-element.58), channel_id=1, source_target_pairs={{0,8},{4,12},{8,0},{12,4},{16,24},{20,28},{24,16},{28,20},{1,9},{5... | collective-permute-start | bytes 884744 | tf_op jit(solution)/shard_map/ppermute | solution.py:23
  83.6 0.7 copy.26
  84.8 3.5 %collective-permute-done.18.refs_3_ = bf16[128,1536]{1,0:T(8,128)(2,1)S(1)} collective-permute-done((bf16[128,1536]{1,0:T(8,128)(2,1)}, bf16[128,1536]{1,0:T(8,128)(2,1)S(1)}, u32[]{:S(2)}, u32[]{:S(2)}) %collective-permute-start.18) | collective-permute-done | bytes 393248 | tf_op jit(solution)/shard_map/ppermute | solution.py:23
  88.9 1.1 fusion.2
  90.0 0.9 copy.36
  91.1 4.5 %all-to-all-start.4 = ((bf16[8,4,16,384]{3,2,1,0:T(8,128)(2,1)}), bf16[8,4,16,384]{3,2,1,0:T(8,128)(2,1)}, u32[]{:S(2)}, u32[]{:S(2)}) async-start(bf16[8,4,16,384]{3,2,1,0:T(8,128)(2,1)} %bitcast.44), calls=%async_computation.4 | async-start | bytes 786432 | tf_op jit(solution)/shard_map/all_to_all | solution.py:40
  95.6 1.2 add_bitcast_fusion
  96.8 0.7 fusion.8
  97.5 2.9 %collective-permute-start.16 = (bf16[1,48,1536]{2,1,0:T(8,128)(2,1)}, bf16[1,48,1536]{2,1,0:T(8,128)(2,1)}, u32[]{:S(2)}, u32[]{:S(2)}) collective-permute-start(bf16[1,48,1536]{2,1,0:T(8,128)(2,1)} %fusion.8), channel_id=1, source_target_pairs={{0,16},{4,20},{8,24},{12,28},{16,0},{20,4},{24,8},{28,12},{1,17},{... | collective-permute-start | bytes 442376 | tf_op jit(solution)/shard_map/ppermute | solution.py:23
  100.5 1.0 copy-done.18
  101.5 6.4 %shard_map.88 = (bf16[128,1536]{1,0:T(8,128)(2,1)}, f32[128,1536]{1,0:T(8,128)}) custom-call(s32[4]{0:T(128)} %pad_add_fusion.where, bf16[128,1536]{1,0:T(8,128)(2,1)} %get-tuple-element.61.gated, bf16[128,1536]{1,0:T(8,128)(2,1)} %get-tuple-element.62.mon, bf16[128,1536]{1,0:T(8,128)(2,1)} %bitcast.48, bf16[128,1536]{1,0:T(8,128)(2,1)} %bitcast.54, ...), custom_call_target="tpu_custom_call" | custom-call | flops 1207959552 | bytes 7471120 | tf_op jit(solution)/shard_map/pallas_call | solution.py:49
  107.9 4.0 %all-to-all-done.4.back = bf16[8,4,16,384]{3,2,1,0:T(8,128)(2,1)} async-done(((bf16[8,4,16,384]{3,2,1,0:T(8,128)(2,1)}), bf16[8,4,16,384]{3,2,1,0:T(8,128)(2,1)}, u32[]{:S(2)}, u32[]{:S(2)}) %all-to-all-start.4) | async-done | bytes 393248 | tf_op jit(solution)/shard_map/all_to_all | solution.py:40
  111.9 1.1 copy-done.8
  113.1 0.8 copy-done.10
  113.8 3.8 %shard_map.89 = bf16[128,1536]{1,0:T(8,128)(2,1)} custom-call(s32[4]{0:T(128)S(1)} %copy-done.11, bf16[8,4,16,384]{3,2,1,0:T(8,128)(2,1)} %all-to-all-done.4.back, bf16[128,128]{1,0:T(8,128)(2,1)S(1)} %bitcast.45, f32[128,1536]{1,0:T(8,128)S(1)} %copy-done.8, bf16[384,1536]{1,0:T(8,128)(2,1)S(1)} %copy-done.1, bf16[384,1536]{1,0:T(8,128)(2,1)S(1)} %copy-done.3, ...), custom_call_target="tpu_custom_call" | custom-call | flops 603979776 | bytes 6324240 | tf_op jit(solution)/shard_map/pallas_call | solution.py:49
  117.6 1.7 %fusion.7 = f32[48,1536]{1,0:T(8,128)} fusion(f32[1,2,48,1536]{3,2,1,0:T(8,128)S(1)} %copy-done.15, bf16[1,48,1536]{2,1,0:T(8,128)(2,1)} %collective-permute-done.16), kind=kLoop, calls=%fused_computation.13 | loop fusion | flops 221184 | bytes 737280 | tf_op jit(solution)/shard_map/div | solution.py:343
  (82 shorter events, 4.1 us)
Async XLA Ops:
  0.6 5.1 %copy-start.12 = (bf16[1,128,1536]{2,1,0:T(8,128)(2,1)S(1)}, bf16[1,128,1536]{2,1,0:T(8,128)(2,1)}, u32[]{:S(2)}) copy-start(bf16[1,128,1536]{2,1,0:T(8,128)(2,1)} %param.6) | copy-start | bytes 1179652
  0.6 5.1 %copy-start.9 = (bf16[1,128,128]{2,1,0:T(8,128)(2,1)S(1)}, bf16[1,128,128]{2,1,0:T(8,128)(2,1)}, u32[]{:S(2)}) copy-start(bf16[1,128,128]{2,1,0:T(8,128)(2,1)} %param.9) | copy-start | bytes 98308
  2.8 9.8 %copy-start = (bf16[384,1536]{1,0:T(8,128)(2,1)S(1)}, bf16[384,1536]{1,0:T(8,128)(2,1)}, u32[]{:S(2)}) copy-start(bf16[384,1536]{1,0:T(8,128)(2,1)} %w0.3) | copy-start | bytes 3538948
  2.8 21.3 %collective-permute-start = (bf16[256,1536]{1,0:T(8,128)(2,1)}, bf16[256,1536]{1,0:T(8,128)(2,1)S(1)}, u32[]{:S(2)}, u32[]{:S(2)}) collective-permute-start(bf16[256,1536]{1,0:T(8,128)(2,1)} %slice.16), channel_id=1, source_target_pairs={{0,2},{1,3},{2,0},{3,1},{4,6},{5,7},{6,4},{7,5},{8,10},{9,11},{10,... | collective-permute-start | bytes 2359304 | tf_op jit(solution)/shard_map/ppermute | solution.py:23
  6.8 17.4 %all-to-all-start = ((bf16[8,16,1536]{2,1,0:T(8,128)(2,1)}), bf16[8,16,1536]{2,1,0:T(8,128)(2,1)}, u32[]{:S(2)}, u32[]{:S(2)}) async-start(bf16[8,16,1536]{2,1,0:T(8,128)(2,1)} %bitcast.6), calls=%async_computation | async-start | bytes 786432 | tf_op jit(solution)/shard_map/all_to_all | solution.py:40
  12.6 27.0 %collective-permute-start.4 = (bf16[384,1536]{1,0:T(8,128)(2,1)S(1)}, bf16[384,1536]{1,0:T(8,128)(2,1)S(1)}, u32[]{:S(2)}, u32[]{:S(2)}) collective-permute-start(bf16[384,1536]{1,0:T(8,128)(2,1)S(1)} %copy-done), channel_id=1, source_target_pairs={{0,1},{1,0},{2,3},{3,2},{4,5},{5,4},{6,7},{7,6},{8,9},{9,8},{10,11... | collective-permute-start | bytes 3538952 | tf_op jit(solution)/shard_map/ppermute | solution.py:23
  12.7 2.8 %copy-start.25 = (bf16[16,8,8]{0,2,1:T(8,128)(2,1)S(1)}, bf16[16,8,8]{0,2,1:T(8,128)(2,1)}, u32[]{:S(2)}) copy-start(bf16[16,8,8]{0,2,1:T(8,128)(2,1)} %param.10) | copy-start | bytes 6148
  24.1 3.3 %copy-start.4 = (bf16[256,1536]{1,0:T(8,128)(2,1)}, bf16[256,1536]{1,0:T(8,128)(2,1)S(1)}, u32[]{:S(2)}) copy-start(bf16[256,1536]{1,0:T(8,128)(2,1)S(1)} %collective-permute-done.w2) | copy-start | bytes 2359300
  24.1 11.8 %collective-permute-start.1 = (bf16[128,1536]{1,0:T(8,128)(2,1)}, bf16[128,1536]{1,0:T(8,128)(2,1)S(1)}, u32[]{:S(2)}, u32[]{:S(2)}) collective-permute-start(bf16[128,1536]{1,0:T(8,128)(2,1)} %slice.17), channel_id=1, source_target_pairs={{0,2},{1,3},{2,0},{3,1},{4,6},{5,7},{6,4},{7,5},{8,10},{9,11},{10,... | collective-permute-start | bytes 1179656 | tf_op jit(solution)/shard_map/ppermute | solution.py:23
  25.2 21.8 %collective-permute-start.2 = (bf16[256,1536]{1,0:T(8,128)(2,1)S(1)}, bf16[256,1536]{1,0:T(8,128)(2,1)}, u32[]{:S(2)}, u32[]{:S(2)}) collective-permute-start(bf16[256,1536]{1,0:T(8,128)(2,1)S(1)} %collective-permute-done.w2), channel_id=1, source_target_pairs={{0,1},{1,0},{2,3},{3,2},{4,5},{5,4},{6,7},{7,6},{8,9},{9,8},{10,11... | collective-permute-start | bytes 2359304 | tf_op jit(solution)/shard_map/ppermute | solution.py:23
  27.4 19.6 %all-to-all-start.1 = ((bf16[8,16,1536]{2,1,0:T(8,128)(2,1)}), bf16[8,16,1536]{2,1,0:T(8,128)(2,1)}, u32[]{:S(2)}, u32[]{:S(2)}) async-start(bf16[8,16,1536]{2,1,0:T(8,128)(2,1)} %copy.22), calls=%async_computation.1 | async-start | bytes 786432 | tf_op jit(solution)/shard_map/all_to_all | solution.py:40
  35.2 2.6 %collective-permute-start.5 = (bf16[128,1920]{1,0:T(8,128)(2,1)}, bf16[128,1920]{1,0:T(8,128)(2,1)}, u32[]{:S(2)}, u32[]{:S(2)}) collective-permute-start(bf16[128,1920]{1,0:T(8,128)(2,1)} %pad_maximum_fusion), channel_id=1, source_target_pairs={{0,1},{1,0},{2,3},{3,2},{4,5},{5,4},{6,7},{7,6},{8,9},{9,8},{10,11... | collective-permute-start | bytes 1474568 | tf_op jit(solution)/shard_map/ppermute | solution.py:23
  35.4 11.6 %collective-permute-start.6 = (bf16[128,1536]{1,0:T(8,128)(2,1)}, bf16[128,1536]{1,0:T(8,128)(2,1)}, u32[]{:S(2)}, u32[]{:S(2)}) collective-permute-start(bf16[128,1536]{1,0:T(8,128)(2,1)} %bitcast.50), channel_id=1, source_target_pairs={{0,2},{1,3},{2,0},{3,1},{4,6},{5,7},{6,4},{7,5},{8,10},{9,11},{10,... | collective-permute-start | bytes 1179656 | tf_op jit(solution)/shard_map/ppermute | solution.py:23
  35.9 15.9 %copy-start.6 = (bf16[128,1536]{1,0:T(8,128)(2,1)}, bf16[128,1536]{1,0:T(8,128)(2,1)S(1)}, u32[]{:S(2)}) copy-start(bf16[128,1536]{1,0:T(8,128)(2,1)S(1)} %collective-permute-done.1.w3) | copy-start | bytes 1179652
  35.9 11.1 %collective-permute-start.3 = (bf16[128,1536]{1,0:T(8,128)(2,1)S(1)}, bf16[128,1536]{1,0:T(8,128)(2,1)}, u32[]{:S(2)}, u32[]{:S(2)}) collective-permute-start(bf16[128,1536]{1,0:T(8,128)(2,1)S(1)} %collective-permute-done.1.w3), channel_id=1, source_target_pairs={{0,1},{1,0},{2,3},{3,2},{4,5},{5,4},{6,7},{7,6},{8,9},{9,8},{10,11... | collective-permute-start | bytes 1179656 | tf_op jit(solution)/shard_map/ppermute | solution.py:23
  37.7 28.8 %collective-permute-start.10 = (bf16[128,1536]{1,0:T(8,128)(2,1)}, bf16[128,1536]{1,0:T(8,128)(2,1)}, u32[]{:S(2)}, u32[]{:S(2)}) collective-permute-start(bf16[128,1536]{1,0:T(8,128)(2,1)} %bitcast.51), channel_id=1, source_target_pairs={{0,4},{4,0},{8,12},{12,8},{16,20},{20,16},{24,28},{28,24},{1,5},{5... | collective-permute-start | bytes 1179656 | tf_op jit(solution)/shard_map/ppermute | solution.py:23
  39.6 12.2 %copy-start.2 = (bf16[384,1536]{1,0:T(8,128)(2,1)}, bf16[384,1536]{1,0:T(8,128)(2,1)S(1)}, u32[]{:S(2)}) copy-start(bf16[384,1536]{1,0:T(8,128)(2,1)S(1)} %collective-permute-done.4.w1) | copy-start | bytes 3538948
  47.0 13.5 %collective-permute-start.7 = (bf16[128,1536]{1,0:T(8,128)(2,1)}, bf16[128,1536]{1,0:T(8,128)(2,1)S(1)}, u32[]{:S(2)}, u32[]{:S(2)}) collective-permute-start(bf16[128,1536]{1,0:T(8,128)(2,1)} %collective-permute-done.6.far.refs_2_), channel_id=1, source_target_pairs={{0,1},{1,0},{2,3},{3,2},{4,5},{5,4},{6,7},{7,6},{8,9},{9,8},{10,11... | collective-permute-start | bytes 1179656 | tf_op jit(solution)/shard_map/ppermute | solution.py:23
  47.1 13.0 %collective-permute-start.8 = (bf16[128,768]{1,0:T(8,128)(2,1)}, bf16[128,768]{1,0:T(8,128)(2,1)S(1)}, u32[]{:S(2)}, u32[]{:S(2)}) collective-permute-start(bf16[128,768]{1,0:T(8,128)(2,1)} %pad_maximum_fusion.1), channel_id=1, source_target_pairs={{0,2},{1,3},{2,0},{3,1},{4,6},{5,7},{6,4},{7,5},{8,10},{9,11},{10,... | collective-permute-start | bytes 589832 | tf_op jit(solution)/shard_map/ppermute | solution.py:23
  48.3 20.4 %collective-permute-start.11 = (bf16[128,1536]{1,0:T(8,128)(2,1)}, bf16[128,1536]{1,0:T(8,128)(2,1)S(1)}, u32[]{:S(2)}, u32[]{:S(2)}) collective-permute-start(bf16[128,1536]{1,0:T(8,128)(2,1)} %collective-permute-done.6.far.refs_2_), channel_id=1, source_target_pairs={{0,4},{4,0},{8,12},{12,8},{16,20},{20,16},{24,28},{28,24},{1,5},{5... | collective-permute-start | bytes 1179656 | tf_op jit(solution)/shard_map/ppermute | solution.py:23
  50.3 18.4 %collective-permute-start.12 = (bf16[128,1536]{1,0:T(8,128)(2,1)}, bf16[128,1536]{1,0:T(8,128)(2,1)}, u32[]{:S(2)}, u32[]{:S(2)}) collective-permute-start(bf16[128,1536]{1,0:T(8,128)(2,1)} %get-tuple-element.52), channel_id=1, source_target_pairs={{0,2},{1,3},{2,0},{3,1},{4,6},{5,7},{6,4},{7,5},{8,10},{9,11},{10,... | collective-permute-start | bytes 1179656 | tf_op jit(solution)/shard_map/ppermute | solution.py:23
  56.6 12.1 %all-to-all-start.2 = ((bf16[8,192,128]{2,1,0:T(8,128)(2,1)}), bf16[8,192,128]{2,1,0:T(8,128)(2,1)S(1)}, u32[]{:S(2)}, u32[]{:S(2)}) async-start(bf16[8,192,128]{2,1,0:T(8,128)(2,1)} %get-tuple-element.48), calls=%async_computation.2 | async-start | bytes 786432 | tf_op jit(solution)/shard_map/all_to_all | solution.py:257
  60.1 1.5 %copy-start.23 = (bf16[128,768]{1,0:T(8,128)(2,1)}, bf16[128,768]{1,0:T(8,128)(2,1)S(1)}, u32[]{:S(2)}) copy-start(bf16[128,768]{1,0:T(8,128)(2,1)S(1)} %collective-permute-done.8.tok_far) | copy-start | bytes 589828
  60.1 1.5 %collective-permute-start.9 = (bf16[128,768]{1,0:T(8,128)(2,1)S(1)}, bf16[128,768]{1,0:T(8,128)(2,1)S(1)}, u32[]{:S(2)}, u32[]{:S(2)}) collective-permute-start(bf16[128,768]{1,0:T(8,128)(2,1)S(1)} %collective-permute-done.8.tok_far), channel_id=1, source_target_pairs={{0,1},{1,0},{2,3},{3,2},{4,5},{5,4},{6,7},{7,6},{8,9},{9,8},{10,11... | collective-permute-start | bytes 589832 | tf_op jit(solution)/shard_map/ppermute | solution.py:23
  68.7 7.6 %copy-start.17 = (bf16[8,192,128]{2,1,0:T(8,128)(2,1)}, bf16[8,192,128]{2,1,0:T(8,128)(2,1)S(1)}, u32[]{:S(2)}) copy-start(bf16[8,192,128]{2,1,0:T(8,128)(2,1)S(1)} %all-to-all-done.2.got) | copy-start | bytes 1179652
  68.7 7.6 %copy-start.20 = (bf16[128,1536]{1,0:T(8,128)(2,1)}, bf16[128,1536]{1,0:T(8,128)(2,1)S(1)}, u32[]{:S(2)}) copy-start(bf16[128,1536]{1,0:T(8,128)(2,1)S(1)} %collective-permute-done.11.refs_6_) | copy-start | bytes 1179652
  68.7 20.1 %all-to-all-start.3 = ((bf16[32,16,384]{2,1,0:T(8,128)(2,1)}), bf16[32,16,384]{2,1,0:T(8,128)(2,1)S(1)}, u32[]{:S(2)}, u32[]{:S(2)}) async-start(bf16[32,16,384]{2,1,0:T(8,128)(2,1)} %bitcast.55), calls=%async_computation.3 | async-start | bytes 786432 | tf_op jit(solution)/shard_map/all_to_all | solution.py:282
  72.5 11.1 %copy-start.13 = (bf16[384,1536]{1,0:T(8,128)(2,1)S(1)}, bf16[384,1536]{1,0:T(8,128)(2,1)}, u32[]{:S(2)}) copy-start(bf16[384,1536]{1,0:T(8,128)(2,1)} %refs_0_.1) | copy-start | bytes 3538948
  72.5 3.8 %collective-permute-start.13 = (bf16[128,1536]{1,0:T(8,128)(2,1)}, bf16[128,1536]{1,0:T(8,128)(2,1)S(1)}, u32[]{:S(2)}, u32[]{:S(2)}) collective-permute-start(bf16[128,1536]{1,0:T(8,128)(2,1)} %collective-permute-done.10.refs_4_), channel_id=1, source_target_pairs={{0,1},{1,0},{2,3},{3,2},{4,5},{5,4},{6,7},{7,6},{8,9},{9,8},{10,11... | collective-permute-start | bytes 1179656 | tf_op jit(solution)/shard_map/ppermute | solution.py:23
  72.8 3.5 %collective-permute-start.14 = (bf16[128,1536]{1,0:T(8,128)(2,1)S(1)}, bf16[128,1536]{1,0:T(8,128)(2,1)S(1)}, u32[]{:S(2)}, u32[]{:S(2)}) collective-permute-start(bf16[128,1536]{1,0:T(8,128)(2,1)S(1)} %collective-permute-done.11.refs_6_), channel_id=1, source_target_pairs={{0,1},{1,0},{2,3},{3,2},{4,5},{5,4},{6,7},{7,6},{8,9},{9,8},{10,11... | collective-permute-start | bytes 1179656 | tf_op jit(solution)/shard_map/ppermute | solution.py:23
  73.1 15.2 %collective-permute-start.18 = (bf16[128,1536]{1,0:T(8,128)(2,1)}, bf16[128,1536]{1,0:T(8,128)(2,1)S(1)}, u32[]{:S(2)}, u32[]{:S(2)}) collective-permute-start(bf16[128,1536]{1,0:T(8,128)(2,1)} %collective-permute-done.12.refs_2_), channel_id=1, source_target_pairs={{0,4},{4,0},{8,12},{12,8},{16,20},{20,16},{24,28},{28,24},{1,5},{5... | collective-permute-start | bytes 1179656 | tf_op jit(solution)/shard_map/ppermute | solution.py:23
  74.8 14.0 %collective-permute-start.19 = (bf16[128,1536]{1,0:T(8,128)(2,1)}, bf16[128,1536]{1,0:T(8,128)(2,1)}, u32[]{:S(2)}, u32[]{:S(2)}) collective-permute-start(bf16[128,1536]{1,0:T(8,128)(2,1)} %get-tuple-element.64), channel_id=1, source_target_pairs={{0,2},{1,3},{2,0},{3,1},{4,6},{5,7},{6,4},{7,5},{8,10},{9,11},{10,... | collective-permute-start | bytes 1179656 | tf_op jit(solution)/shard_map/ppermute | solution.py:23
  82.1 9.0 %collective-permute-start.15 = (bf16[2,48,1536]{2,1,0:T(8,128)(2,1)}, bf16[2,48,1536]{2,1,0:T(8,128)(2,1)}, u32[]{:S(2)}, u32[]{:S(2)}) collective-permute-start(bf16[2,48,1536]{2,1,0:T(8,128)(2,1)} %get-tuple-element.58), channel_id=1, source_target_pairs={{0,8},{4,12},{8,0},{12,4},{16,24},{20,28},{24,16},{28,20},{1,9},{5... | collective-permute-start | bytes 884744 | tf_op jit(solution)/shard_map/ppermute | solution.py:23
  83.6 16.9 %collective-permute-start.17 = (bf16[384,1536]{1,0:T(8,128)(2,1)S(1)}, bf16[384,1536]{1,0:T(8,128)(2,1)S(1)}, u32[]{:S(2)}, u32[]{:S(2)}) collective-permute-start(bf16[384,1536]{1,0:T(8,128)(2,1)S(1)} %copy-done.13), channel_id=1, source_target_pairs={{0,1},{1,0},{2,3},{3,2},{4,5},{5,4},{6,7},{7,6},{8,9},{9,8},{10,11... | collective-permute-start | bytes 3538952 | tf_op jit(solution)/shard_map/ppermute | solution.py:23
  84.3 16.2 %collective-permute-start.20 = (bf16[128,1536]{1,0:T(8,128)(2,1)}, bf16[128,1536]{1,0:T(8,128)(2,1)}, u32[]{:S(2)}, u32[]{:S(2)}) collective-permute-start(bf16[128,1536]{1,0:T(8,128)(2,1)} %collective-permute-done.12.refs_2_), channel_id=1, source_target_pairs={{0,1},{1,0},{2,3},{3,2},{4,5},{5,4},{6,7},{7,6},{8,9},{9,8},{10,11... | collective-permute-start | bytes 1179656 | tf_op jit(solution)/shard_map/ppermute | solution.py:23
  88.3 2.8 %copy-start.19 = (bf16[128,1536]{1,0:T(8,128)(2,1)}, bf16[128,1536]{1,0:T(8,128)(2,1)S(1)}, u32[]{:S(2)}) copy-start(bf16[128,1536]{1,0:T(8,128)(2,1)S(1)} %collective-permute-done.18.refs_3_) | copy-start | bytes 1179652
  88.3 12.2 %collective-permute-start.21 = (bf16[128,1536]{1,0:T(8,128)(2,1)S(1)}, bf16[128,1536]{1,0:T(8,128)(2,1)}, u32[]{:S(2)}, u32[]{:S(2)}) collective-permute-start(bf16[128,1536]{1,0:T(8,128)(2,1)S(1)} %collective-permute-done.18.refs_3_), channel_id=1, source_target_pairs={{0,1},{1,0},{2,3},{3,2},{4,5},{5,4},{6,7},{7,6},{8,9},{9,8},{10,11... | collective-permute-start | bytes 1179656 | tf_op jit(solution)/shard_map/ppermute | solution.py:23
  88.9 11.6 %collective-permute-start.22 = (bf16[128,1536]{1,0:T(8,128)(2,1)}, bf16[128,1536]{1,0:T(8,128)(2,1)}, u32[]{:S(2)}, u32[]{:S(2)}) collective-permute-start(bf16[128,1536]{1,0:T(8,128)(2,1)} %collective-permute-done.19.refs_4_), channel_id=1, source_target_pairs={{0,1},{1,0},{2,3},{3,2},{4,5},{5,4},{6,7},{7,6},{8,9},{9,8},{10,11... | collective-permute-start | bytes 1179656 | tf_op jit(solution)/shard_map/ppermute | solution.py:23
  91.1 20.8 %all-to-all-start.4 = ((bf16[8,4,16,384]{3,2,1,0:T(8,128)(2,1)}), bf16[8,4,16,384]{3,2,1,0:T(8,128)(2,1)}, u32[]{:S(2)}, u32[]{:S(2)}) async-start(bf16[8,4,16,384]{3,2,1,0:T(8,128)(2,1)} %bitcast.44), calls=%async_computation.4 | async-start | bytes 786432 | tf_op jit(solution)/shard_map/all_to_all | solution.py:40
  96.8 3.7 %copy-start.14 = (f32[1,2,48,1536]{3,2,1,0:T(8,128)}, f32[1,2,48,1536]{3,2,1,0:T(8,128)S(1)}, u32[]{:S(2)}) copy-start(f32[1,2,48,1536]{3,2,1,0:T(8,128)S(1)} %add_bitcast_fusion) | copy-start | bytes 1769476
  97.5 20.1 %collective-permute-start.16 = (bf16[1,48,1536]{2,1,0:T(8,128)(2,1)}, bf16[1,48,1536]{2,1,0:T(8,128)(2,1)}, u32[]{:S(2)}, u32[]{:S(2)}) collective-permute-start(bf16[1,48,1536]{2,1,0:T(8,128)(2,1)} %fusion.8), channel_id=1, source_target_pairs={{0,16},{4,20},{8,24},{12,28},{16,0},{20,4},{24,8},{28,12},{1,17},{... | collective-permute-start | bytes 442376 | tf_op jit(solution)/shard_map/ppermute | solution.py:23
  101.5 10.4 %copy-start.1 = (bf16[384,1536]{1,0:T(8,128)(2,1)S(1)}, bf16[384,1536]{1,0:T(8,128)(2,1)}, u32[]{:S(2)}) copy-start(bf16[384,1536]{1,0:T(8,128)(2,1)} %w0.3) | copy-start | bytes 3538948
  101.5 10.4 %copy-start.3 = (bf16[384,1536]{1,0:T(8,128)(2,1)S(1)}, bf16[384,1536]{1,0:T(8,128)(2,1)}, u32[]{:S(2)}) copy-start(bf16[384,1536]{1,0:T(8,128)(2,1)} %copy-done.2) | copy-start | bytes 3538948
  101.5 10.4 %copy-start.5 = (bf16[256,1536]{1,0:T(8,128)(2,1)S(1)}, bf16[256,1536]{1,0:T(8,128)(2,1)}, u32[]{:S(2)}) copy-start(bf16[256,1536]{1,0:T(8,128)(2,1)} %copy-done.4) | copy-start | bytes 2359300
  101.5 10.4 %copy-start.7 = (bf16[128,1536]{1,0:T(8,128)(2,1)S(1)}, bf16[128,1536]{1,0:T(8,128)(2,1)}, u32[]{:S(2)}) copy-start(bf16[128,1536]{1,0:T(8,128)(2,1)} %copy-done.6) | copy-start | bytes 1179652
  101.5 10.4 %copy-start.11 = (s32[4]{0:T(128)S(1)}, s32[4]{0:T(128)}, u32[]{:S(2)}) copy-start(s32[4]{0:T(128)} %pad_add_fusion.where) | copy-start | bytes 52
  111.9 1.1 copy-start.8
  113.8 3.8 %copy-start.15 = (f32[1,2,48,1536]{3,2,1,0:T(8,128)S(1)}, f32[1,2,48,1536]{3,2,1,0:T(8,128)}, u32[]{:S(2)}) copy-start(f32[1,2,48,1536]{3,2,1,0:T(8,128)} %copy-done.14) | copy-start | bytes 1769476
  (6 other events, 5.0 us)

commit v5 on v4

--- a/solution.py
+++ b/solution.py
@@ -225,14 +225,14 @@
     cot_near = swap(jnp.concatenate([upstream, columns(inputs, 1)], axis=1), "dp", 1)
     tok_far = jnp.concatenate([columns(inputs, 2), columns(inputs, 3)], axis=1)
     cot_far = swap(up, "dp", 2)
-    mix, far_b, side_a, side_b, w_near, cot_near, cot_far, tok_far, outs = join(
-        (mix, far_b, side_a, side_b, w_near, cot_near, cot_far, tok_far, outs)
+    cot_side = swap(cot_far, "dp", 1)
+    mix, far_b, side_a, side_b, w_near, cot_near, cot_far, cot_side, tok_far, outs, pair = join(
+        (mix, far_b, side_a, side_b, w_near, cot_near, cot_far, cot_side, tok_far, outs, pair)
     )
 
     w_ins = (w_in, w_near, far_a, far_b, side_a, side_b)
     tok_far = swap(tok_far, "dp", 2)
     pair_far = swap(cot_far, "seq", 1)
-    cot_side = swap(cot_far, "dp", 1)
     tok_side = swap(tok_far, "dp", 1)
     out_a = swap(outs[0], "dp", 2)
     mix = mix.reshape(rows, width)

time: 120 us -> 118 us (0.983)
  waiting for transfers between devices: 26.3 us -> 25 us
    unnamed x54 -> x52, local copies, waits for them, and re-layouts: 6.5 us -> 6.52 us
  transfers between devices with their start and end apart: 28 -> 28, of which waited for: 8 -> 10; matrix products, arithmetic and copies ran while one was open for 14% -> 14% of each run, Pallas kernels for 20% -> 20%
where the time goes in v5:
time: 118 us; the launch traced here: 117 us
  starting transfers between devices  42.7 us (36%)
  waiting for transfers between devices  25 us (21%)
  Pallas kernels  23.5 us (20%)
  local copies, waits for them, and re-layouts  14.7 us (12%)
  other arithmetic  6.96 us (6%)
  matrix products  3.42 us (3%)
    pallas_call x5, Pallas kernels, call(): pl.pallas_call(kernel, out_shape=list(outs), in_specs=[SMEM if x.dtype ==...  23.5 us
    ppermute x23, starting transfers between devices, swap(): return lax.ppermute(x, axis, [(i, i ^ bit) for i in range(n)])  19.8 us
    all_to_all x3, starting transfers between devices, spread(): return lax.all_to_all(x, 'seq', split_axis=0, concat_axis=0, tiled=True)  15.7 us
    ppermute x23, waiting for transfers between devices, swap(): return lax.ppermute(x, axis, [(i, i ^ bit) for i in range(n)])  12.4 us
    all_to_all x3, waiting for transfers between devices, spread(): return lax.all_to_all(x, 'seq', split_axis=0, concat_axis=0, tiled=True)  10.9 us
    unnamed x52, local copies, waits for them, and re-layouts  6.52 us
    all_to_all x1, starting transfers between devices, on_device(): lax.all_to_all(grads, ('seq', 'dp'), split_axis=0, concat_axis=0, tiled=T...  3.69 us
    all_to_all x1, starting transfers between devices, on_device(): lax.all_to_all(turned, ('seq', 'dp'), split_axis=0, concat_axis=0, tiled=...  3.45 us
  transfers between devices with their start and end apart: 28, of which 10 were waited for; matrix products, arithmetic and copies ran while one was open for 14% of the time, Pallas kernels for 20%

profile of v5, /device:TPU:0, one launch (start us, length us, event | category | flops | bytes accessed | tf_op | source)
XLA Modules:
  0.0 117.2 jit_solution(13100826384276594502)
XLA Ops:
  0.7 2.2 %slice.16 = bf16[256,1536]{1,0:T(8,128)(2,1)} slice(bf16[384,1536]{1,0:T(8,128)(2,1)} %w0.3), slice={[0:256], [0:1536]} | slice | bytes 1572864 | tf_op jit(solution)/shard_map/slice | solution.py:211
  2.8 2.9 %collective-permute-start = (bf16[256,1536]{1,0:T(8,128)(2,1)}, bf16[256,1536]{1,0:T(8,128)(2,1)S(1)}, u32[]{:S(2)}, u32[]{:S(2)}) collective-permute-start(bf16[256,1536]{1,0:T(8,128)(2,1)} %slice.16), channel_id=1, source_target_pairs={{0,2},{1,3},{2,0},{3,1},{4,6},{5,7},{6,4},{7,5},{8,10},{9,11},{10,... | collective-permute-start | bytes 2359304 | tf_op jit(solution)/shard_map/ppermute | solution.py:23
  5.8 1.0 convolution_convert_fusion.1
  6.8 5.8 %all-to-all-start = ((bf16[8,16,1536]{2,1,0:T(8,128)(2,1)}), bf16[8,16,1536]{2,1,0:T(8,128)(2,1)}, u32[]{:S(2)}, u32[]{:S(2)}) async-start(bf16[8,16,1536]{2,1,0:T(8,128)(2,1)} %bitcast.6), calls=%async_computation | async-start | bytes 786432 | tf_op jit(solution)/shard_map/all_to_all | solution.py:40
  12.7 2.0 %collective-permute-start.8 = (bf16[128,1536]{1,0:T(8,128)(2,1)}, bf16[128,1536]{1,0:T(8,128)(2,1)}, u32[]{:S(2)}, u32[]{:S(2)}) collective-permute-start(bf16[128,1536]{1,0:T(8,128)(2,1)} %bitcast.49), channel_id=1, source_target_pairs={{0,4},{4,0},{8,12},{12,8},{16,20},{20,16},{24,28},{28,24},{1,5},{5... | collective-permute-start | bytes 1179656 | tf_op jit(solution)/shard_map/ppermute | solution.py:23
  14.7 2.1 %fusion.11 = (bf16[128,1536]{1,0:T(8,128)(2,1)}, bf16[128,1536]{1,0:T(8,128)(2,1)}) fusion(bf16[384,1536]{1,0:T(8,128)(2,1)} %refs_0_.1, s32[]{:T(128)S(6)} %select_n.32), kind=kLoop, calls=%fused_computation.24 | loop fusion | bytes 1572868 | tf_op jit(solution)/shard_map/slice | solution.py:216
  16.8 0.8 slice.17
  17.5 0.7 copy.21
  18.2 0.7 dynamic-slice_bitcast_fusion.1
  18.9 5.2 %all-to-all-done = bf16[8,16,1536]{2,1,0:T(8,128)(2,1)} async-done(((bf16[8,16,1536]{2,1,0:T(8,128)(2,1)}), bf16[8,16,1536]{2,1,0:T(8,128)(2,1)}, u32[]{:S(2)}, u32[]{:S(2)}) %all-to-all-start) | async-done | bytes 393248 | tf_op jit(solution)/shard_map/all_to_all | solution.py:40
  24.1 1.1 collective-permute-start.1
  25.3 0.9 collective-permute-start.6
  26.2 1.3 %fusion = bf16[8,16,1536]{2,0,1:T(8,128)(2,1)S(1)} fusion(bf16[16,8,8]{2,1,0:T(8,128)(2,1)} %copy.21, bf16[8,16,1536]{2,1,0:T(8,128)(2,1)} %all-to-all-done), kind=kOutput, calls=%fused_computation.2 | convolution fusion | flops 3342336 | bytes 788480 | tf_op jit(solution)/shard_map/sab,bsd->asd/dot_general | solution.py:219
  27.5 0.9 copy.22
  28.4 5.4 %all-to-all-start.1 = ((bf16[8,16,1536]{2,1,0:T(8,128)(2,1)}), bf16[8,16,1536]{2,1,0:T(8,128)(2,1)}, u32[]{:S(2)}, u32[]{:S(2)}) async-start(bf16[8,16,1536]{2,1,0:T(8,128)(2,1)} %copy.22), calls=%async_computation.1 | async-start | bytes 786432 | tf_op jit(solution)/shard_map/all_to_all | solution.py:40
  33.8 1.9 %pad_maximum_fusion = bf16[128,1920]{1,0:T(8,128)(2,1)} fusion(bf16[128,384]{1,0:T(8,128)(2,1)} %get-tuple-element.78, bf16[128,1536]{1,0:T(8,128)(2,1)} %bitcast.51), kind=kLoop, calls=%fused_computation.5 | loop fusion | flops 983040 | bytes 983040 | tf_op jit(solution)/shard_map/concatenate | solution.py:225
  36.4 6.2 %collective-permute-done.6.far.refs_2_ = bf16[128,1536]{1,0:T(8,128)(2,1)} collective-permute-done((bf16[128,1536]{1,0:T(8,128)(2,1)}, bf16[128,1536]{1,0:T(8,128)(2,1)}, u32[]{:S(2)}, u32[]{:S(2)}) %collective-permute-start.6) | collective-permute-done | bytes 393248 | tf_op jit(solution)/shard_map/ppermute | solution.py:23
  42.7 1.6 %pad_maximum_fusion.1 = bf16[128,768]{1,0:T(8,128)(2,1)} fusion(bf16[128,384]{1,0:T(8,128)(2,1)} %get-tuple-element.79, bf16[128,384]{1,0:T(8,128)(2,1)} %get-tuple-element.77), kind=kLoop, calls=%fused_computation.15 | loop fusion | flops 393216 | bytes 393216 | tf_op jit(solution)/shard_map/concatenate | solution.py:226
  44.3 1.7 %all-to-all-done.1 = bf16[8,16,1536]{2,1,0:T(8,128)(2,1)} async-done(((bf16[8,16,1536]{2,1,0:T(8,128)(2,1)}), bf16[8,16,1536]{2,1,0:T(8,128)(2,1)}, u32[]{:S(2)}, u32[]{:S(2)}) %all-to-all-start.1) | async-done | bytes 393248 | tf_op jit(solution)/shard_map/all_to_all | solution.py:40
  46.0 1.6 %collective-permute-start.9 = (bf16[128,768]{1,0:T(8,128)(2,1)}, bf16[128,768]{1,0:T(8,128)(2,1)S(1)}, u32[]{:S(2)}, u32[]{:S(2)}) collective-permute-start(bf16[128,768]{1,0:T(8,128)(2,1)} %pad_maximum_fusion.1), channel_id=1, source_target_pairs={{0,2},{1,3},{2,0},{3,1},{4,6},{5,7},{6,4},{7,5},{8,10},{9,11},{10,... | collective-permute-start | bytes 589832 | tf_op jit(solution)/shard_map/ppermute | solution.py:23
  48.2 1.5 %collective-permute-start.11 = (bf16[128,1536]{1,0:T(8,128)(2,1)}, bf16[128,1536]{1,0:T(8,128)(2,1)S(1)}, u32[]{:S(2)}, u32[]{:S(2)}) collective-permute-start(bf16[128,1536]{1,0:T(8,128)(2,1)} %collective-permute-done.6.far.refs_2_), channel_id=1, source_target_pairs={{0,4},{4,0},{8,12},{12,8},{16,20},{20,16},{24,28},{28,24},{1,5},{5... | collective-permute-start | bytes 1179656 | tf_op jit(solution)/shard_map/ppermute | solution.py:23
  50.2 4.8 %shard_map.85 = (bf16[128,1536]{1,0:T(8,128)(2,1)}, bf16[128,1536]{1,0:T(8,128)(2,1)}, bf16[8,192,128]{2,1,0:T(8,128)(2,1)}) custom-call(s32[4]{0:T(128)} %pad_add_fusion.where, bf16[128,1536]{1,0:T(8,128)(2,1)} %bitcast.12.mix, bf16[128,1536]{1,0:T(8,128)(2,1)} %bitcast.46, bf16[384,1536]{1,0:T(8,128)(2,1)} %w0.3, bf16[384,1536]{1,0:T(8,128)(2,1)} %copy-done.2, ...), custom_call_target="tpu_custom_call" | custom-call | flops 603979776 | bytes 6684688 | tf_op jit(solution)/shard_map/pallas_call | solution.py:49
  54.9 3.5 %all-to-all-start.2 = ((bf16[8,192,128]{2,1,0:T(8,128)(2,1)}), bf16[8,192,128]{2,1,0:T(8,128)(2,1)S(1)}, u32[]{:S(2)}, u32[]{:S(2)}) async-start(bf16[8,192,128]{2,1,0:T(8,128)(2,1)} %get-tuple-element.50), calls=%async_computation.2 | async-start | bytes 786432 | tf_op jit(solution)/shard_map/all_to_all | solution.py:257
  58.9 1.1 collective-permute-done.10.tok_side
  60.6 4.3 %shard_map.86 = bf16[8,4,16,384]{3,2,1,0:T(8,128)(2,1)} custom-call(s32[4]{0:T(128)} %pad_add_fusion.where, bf16[384,1536]{1,0:T(8,128)(2,1)} %refs_0_.1, bf16[128,1536]{1,0:T(8,128)(2,1)} %bitcast.47, bf16[128,1536]{1,0:T(8,128)(2,1)} %bitcast.52, bf16[128,1920]{1,0:T(8,128)(2,1)} %collective-permute-done.5.near.refs_1_, ...), custom_call_target="tpu_custom_call" | custom-call | flops 603979776 | bytes 4030480 | tf_op jit(solution)/shard_map/pallas_call | solution.py:49
  64.9 1.8 %all-to-all-done.2.got = bf16[8,192,128]{2,1,0:T(8,128)(2,1)S(1)} async-done(((bf16[8,192,128]{2,1,0:T(8,128)(2,1)}), bf16[8,192,128]{2,1,0:T(8,128)(2,1)S(1)}, u32[]{:S(2)}, u32[]{:S(2)}) %all-to-all-start.2) | async-done | bytes 393248 | tf_op jit(solution)/shard_map/all_to_all | solution.py:257
  66.7 3.7 %all-to-all-start.3 = ((bf16[32,16,384]{2,1,0:T(8,128)(2,1)}), bf16[32,16,384]{2,1,0:T(8,128)(2,1)S(1)}, u32[]{:S(2)}, u32[]{:S(2)}) async-start(bf16[32,16,384]{2,1,0:T(8,128)(2,1)} %bitcast.55), calls=%async_computation.3 | async-start | bytes 786432 | tf_op jit(solution)/shard_map/all_to_all | solution.py:282
  71.0 1.8 %collective-permute-start.18 = (bf16[128,1536]{1,0:T(8,128)(2,1)}, bf16[128,1536]{1,0:T(8,128)(2,1)S(1)}, u32[]{:S(2)}, u32[]{:S(2)}) collective-permute-start(bf16[128,1536]{1,0:T(8,128)(2,1)} %collective-permute-done.12.refs_2_), channel_id=1, source_target_pairs={{0,4},{4,0},{8,12},{12,8},{16,20},{20,16},{24,28},{28,24},{1,5},{5... | collective-permute-start | bytes 1179656 | tf_op jit(solution)/shard_map/ppermute | solution.py:23
  72.7 1.5 %collective-permute-start.19 = (bf16[128,1536]{1,0:T(8,128)(2,1)}, bf16[128,1536]{1,0:T(8,128)(2,1)}, u32[]{:S(2)}, u32[]{:S(2)}) collective-permute-start(bf16[128,1536]{1,0:T(8,128)(2,1)} %get-tuple-element.68), channel_id=1, source_target_pairs={{0,2},{1,3},{2,0},{3,1},{4,6},{5,7},{6,4},{7,5},{8,10},{9,11},{10,... | collective-permute-start | bytes 1179656 | tf_op jit(solution)/shard_map/ppermute | solution.py:23
  74.2 0.7 copy-done.20
  75.0 0.8 copy-done.21
  75.7 4.3 %shard_map.87 = (f32[2,48,1536]{2,1,0:T(8,128)}, bf16[2,48,1536]{2,1,0:T(8,128)(2,1)}) custom-call(s32[4]{0:T(128)} %pad_add_fusion.where, bf16[8,192,128]{2,1,0:T(8,128)(2,1)} %copy-done.16, bf16[128,1536]{1,0:T(8,128)(2,1)} %bitcast.53, bf16[128,1920]{1,0:T(8,128)(2,1)} %collective-permute-done.5.near.refs_1_, ...), custom_call_target="tpu_custom_call" | custom-call | flops 603979776 | bytes 4522000 | tf_op jit(solution)/shard_map/pallas_call | solution.py:49
  80.0 1.5 %collective-permute-start.15 = (bf16[2,48,1536]{2,1,0:T(8,128)(2,1)}, bf16[2,48,1536]{2,1,0:T(8,128)(2,1)}, u32[]{:S(2)}, u32[]{:S(2)}) collective-permute-start(bf16[2,48,1536]{2,1,0:T(8,128)(2,1)} %get-tuple-element.62), channel_id=1, source_target_pairs={{0,8},{4,12},{8,0},{12,4},{16,24},{20,28},{24,16},{28,20},{1,9},{5... | collective-permute-start | bytes 884744 | tf_op jit(solution)/shard_map/ppermute | solution.py:23
  81.5 0.7 copy.26
  82.7 3.5 %collective-permute-done.18.refs_3_ = bf16[128,1536]{1,0:T(8,128)(2,1)S(1)} collective-permute-done((bf16[128,1536]{1,0:T(8,128)(2,1)}, bf16[128,1536]{1,0:T(8,128)(2,1)S(1)}, u32[]{:S(2)}, u32[]{:S(2)}) %collective-permute-start.18) | collective-permute-done | bytes 393248 | tf_op jit(solution)/shard_map/ppermute | solution.py:23
  86.8 1.1 fusion.2
  87.9 0.9 copy.36
  89.0 4.5 %all-to-all-start.4 = ((bf16[8,4,16,384]{3,2,1,0:T(8,128)(2,1)}), bf16[8,4,16,384]{3,2,1,0:T(8,128)(2,1)}, u32[]{:S(2)}, u32[]{:S(2)}) async-start(bf16[8,4,16,384]{3,2,1,0:T(8,128)(2,1)} %bitcast.44), calls=%async_computation.4 | async-start | bytes 786432 | tf_op jit(solution)/shard_map/all_to_all | solution.py:40
  93.5 1.2 %add_bitcast_fusion = f32[1,2,48,1536]{3,2,1,0:T(8,128)S(1)} fusion(f32[2,48,1536]{2,1,0:T(8,128)} %get-tuple-element.61, bf16[2,48,1536]{2,1,0:T(8,128)(2,1)} %collective-permute-done.15), kind=kLoop, calls=%fused_computation.4 | loop fusion | flops 294912 | bytes 1474560 | tf_op jit(solution)/shard_map/reshape | solution.py:197
  94.7 0.7 fusion.8
  95.4 2.9 %collective-permute-start.16 = (bf16[1,48,1536]{2,1,0:T(8,128)(2,1)}, bf16[1,48,1536]{2,1,0:T(8,128)(2,1)}, u32[]{:S(2)}, u32[]{:S(2)}) collective-permute-start(bf16[1,48,1536]{2,1,0:T(8,128)(2,1)} %fusion.8), channel_id=1, source_target_pairs={{0,16},{4,20},{8,24},{12,28},{16,0},{20,4},{24,8},{28,12},{1,17},{... | collective-permute-start | bytes 442376 | tf_op jit(solution)/shard_map/ppermute | solution.py:23
  98.4 1.0 copy-done.17
  99.4 6.4 %shard_map.88 = (bf16[128,1536]{1,0:T(8,128)(2,1)}, f32[128,1536]{1,0:T(8,128)}) custom-call(s32[4]{0:T(128)} %pad_add_fusion.where, bf16[128,1536]{1,0:T(8,128)(2,1)} %get-tuple-element.65.gated, bf16[128,1536]{1,0:T(8,128)(2,1)} %get-tuple-element.66.mon, bf16[128,1536]{1,0:T(8,128)(2,1)} %bitcast.48, bf16[128,1536]{1,0:T(8,128)(2,1)} %bitcast.54, ...), custom_call_target="tpu_custom_call" | custom-call | flops 1207959552 | bytes 7471120 | tf_op jit(solution)/shard_map/pallas_call | solution.py:49
  105.8 4.0 %all-to-all-done.4.back = bf16[8,4,16,384]{3,2,1,0:T(8,128)(2,1)} async-done(((bf16[8,4,16,384]{3,2,1,0:T(8,128)(2,1)}), bf16[8,4,16,384]{3,2,1,0:T(8,128)(2,1)}, u32[]{:S(2)}, u32[]{:S(2)}) %all-to-all-start.4) | async-done | bytes 393248 | tf_op jit(solution)/shard_map/all_to_all | solution.py:40
  109.8 1.1 copy-done.8
  111.0 0.8 copy-done.10
  111.7 3.8 %shard_map.89 = bf16[128,1536]{1,0:T(8,128)(2,1)} custom-call(s32[4]{0:T(128)S(1)} %copy-done.11, bf16[8,4,16,384]{3,2,1,0:T(8,128)(2,1)} %all-to-all-done.4.back, bf16[128,128]{1,0:T(8,128)(2,1)S(1)} %bitcast.45, f32[128,1536]{1,0:T(8,128)S(1)} %copy-done.8, bf16[384,1536]{1,0:T(8,128)(2,1)S(1)} %copy-done.1, bf16[384,1536]{1,0:T(8,128)(2,1)S(1)} %copy-done.3, ...), custom_call_target="tpu_custom_call" | custom-call | flops 603979776 | bytes 6324240 | tf_op jit(solution)/shard_map/pallas_call | solution.py:49
  115.5 1.7 %fusion.7 = f32[48,1536]{1,0:T(8,128)} fusion(f32[1,2,48,1536]{3,2,1,0:T(8,128)S(1)} %copy-done.15, bf16[1,48,1536]{2,1,0:T(8,128)(2,1)} %collective-permute-done.16), kind=kLoop, calls=%fused_computation.13 | loop fusion | flops 221184 | bytes 737280 | tf_op jit(solution)/shard_map/div | solution.py:343
  (80 shorter events, 5.1 us)
Async XLA Ops:
  0.6 5.1 %copy-start.12 = (bf16[1,128,1536]{2,1,0:T(8,128)(2,1)S(1)}, bf16[1,128,1536]{2,1,0:T(8,128)(2,1)}, u32[]{:S(2)}) copy-start(bf16[1,128,1536]{2,1,0:T(8,128)(2,1)} %param.6) | copy-start | bytes 1179652
  0.6 5.1 %copy-start.9 = (bf16[1,128,128]{2,1,0:T(8,128)(2,1)S(1)}, bf16[1,128,128]{2,1,0:T(8,128)(2,1)}, u32[]{:S(2)}) copy-start(bf16[1,128,128]{2,1,0:T(8,128)(2,1)} %param.9) | copy-start | bytes 98308
  2.8 9.8 %copy-start = (bf16[384,1536]{1,0:T(8,128)(2,1)S(1)}, bf16[384,1536]{1,0:T(8,128)(2,1)}, u32[]{:S(2)}) copy-start(bf16[384,1536]{1,0:T(8,128)(2,1)} %w0.3) | copy-start | bytes 3538948
  2.8 21.3 %collective-permute-start = (bf16[256,1536]{1,0:T(8,128)(2,1)}, bf16[256,1536]{1,0:T(8,128)(2,1)S(1)}, u32[]{:S(2)}, u32[]{:S(2)}) collective-permute-start(bf16[256,1536]{1,0:T(8,128)(2,1)} %slice.16), channel_id=1, source_target_pairs={{0,2},{1,3},{2,0},{3,1},{4,6},{5,7},{6,4},{7,5},{8,10},{9,11},{10,... | collective-permute-start | bytes 2359304 | tf_op jit(solution)/shard_map/ppermute | solution.py:23
  6.8 17.4 %all-to-all-start = ((bf16[8,16,1536]{2,1,0:T(8,128)(2,1)}), bf16[8,16,1536]{2,1,0:T(8,128)(2,1)}, u32[]{:S(2)}, u32[]{:S(2)}) async-start(bf16[8,16,1536]{2,1,0:T(8,128)(2,1)} %bitcast.6), calls=%async_computation | async-start | bytes 786432 | tf_op jit(solution)/shard_map/all_to_all | solution.py:40
  12.6 31.7 %collective-permute-start.4 = (bf16[384,1536]{1,0:T(8,128)(2,1)S(1)}, bf16[384,1536]{1,0:T(8,128)(2,1)S(1)}, u32[]{:S(2)}, u32[]{:S(2)}) collective-permute-start(bf16[384,1536]{1,0:T(8,128)(2,1)S(1)} %copy-done), channel_id=1, source_target_pairs={{0,1},{1,0},{2,3},{3,2},{4,5},{5,4},{6,7},{7,6},{8,9},{9,8},{10,11... | collective-permute-start | bytes 3538952 | tf_op jit(solution)/shard_map/ppermute | solution.py:23
  12.7 23.0 %collective-permute-start.8 = (bf16[128,1536]{1,0:T(8,128)(2,1)}, bf16[128,1536]{1,0:T(8,128)(2,1)}, u32[]{:S(2)}, u32[]{:S(2)}) collective-permute-start(bf16[128,1536]{1,0:T(8,128)(2,1)} %bitcast.49), channel_id=1, source_target_pairs={{0,4},{4,0},{8,12},{12,8},{16,20},{20,16},{24,28},{28,24},{1,5},{5... | collective-permute-start | bytes 1179656 | tf_op jit(solution)/shard_map/ppermute | solution.py:23
  14.7 2.8 %copy-start.24 = (bf16[16,8,8]{0,2,1:T(8,128)(2,1)S(1)}, bf16[16,8,8]{0,2,1:T(8,128)(2,1)}, u32[]{:S(2)}) copy-start(bf16[16,8,8]{0,2,1:T(8,128)(2,1)} %param.10) | copy-start | bytes 6148
  24.1 4.2 %copy-start.4 = (bf16[256,1536]{1,0:T(8,128)(2,1)}, bf16[256,1536]{1,0:T(8,128)(2,1)S(1)}, u32[]{:S(2)}) copy-start(bf16[256,1536]{1,0:T(8,128)(2,1)S(1)} %collective-permute-done.w2) | copy-start | bytes 2359300
  24.1 12.3 %collective-permute-start.1 = (bf16[128,1536]{1,0:T(8,128)(2,1)}, bf16[128,1536]{1,0:T(8,128)(2,1)S(1)}, u32[]{:S(2)}, u32[]{:S(2)}) collective-permute-start(bf16[128,1536]{1,0:T(8,128)(2,1)} %slice.17), channel_id=1, source_target_pairs={{0,2},{1,3},{2,0},{3,1},{4,6},{5,7},{6,4},{7,5},{8,10},{9,11},{10,... | collective-permute-start | bytes 1179656 | tf_op jit(solution)/shard_map/ppermute | solution.py:23
  25.3 20.8 %collective-permute-start.2 = (bf16[256,1536]{1,0:T(8,128)(2,1)S(1)}, bf16[256,1536]{1,0:T(8,128)(2,1)}, u32[]{:S(2)}, u32[]{:S(2)}) collective-permute-start(bf16[256,1536]{1,0:T(8,128)(2,1)S(1)} %collective-permute-done.w2), channel_id=1, source_target_pairs={{0,1},{1,0},{2,3},{3,2},{4,5},{5,4},{6,7},{7,6},{8,9},{9,8},{10,11... | collective-permute-start | bytes 2359304 | tf_op jit(solution)/shard_map/ppermute | solution.py:23
  25.3 17.4 %collective-permute-start.6 = (bf16[128,1536]{1,0:T(8,128)(2,1)}, bf16[128,1536]{1,0:T(8,128)(2,1)}, u32[]{:S(2)}, u32[]{:S(2)}) collective-permute-start(bf16[128,1536]{1,0:T(8,128)(2,1)} %bitcast.50), channel_id=1, source_target_pairs={{0,2},{1,3},{2,0},{3,1},{4,6},{5,7},{6,4},{7,5},{8,10},{9,11},{10,... | collective-permute-start | bytes 1179656 | tf_op jit(solution)/shard_map/ppermute | solution.py:23
  28.4 17.6 %all-to-all-start.1 = ((bf16[8,16,1536]{2,1,0:T(8,128)(2,1)}), bf16[8,16,1536]{2,1,0:T(8,128)(2,1)}, u32[]{:S(2)}, u32[]{:S(2)}) async-start(bf16[8,16,1536]{2,1,0:T(8,128)(2,1)} %copy.22), calls=%async_computation.1 | async-start | bytes 786432 | tf_op jit(solution)/shard_map/all_to_all | solution.py:40
  35.7 8.6 %collective-permute-start.5 = (bf16[128,1920]{1,0:T(8,128)(2,1)}, bf16[128,1920]{1,0:T(8,128)(2,1)}, u32[]{:S(2)}, u32[]{:S(2)}) collective-permute-start(bf16[128,1920]{1,0:T(8,128)(2,1)} %pad_maximum_fusion), channel_id=1, source_target_pairs={{0,1},{1,0},{2,3},{3,2},{4,5},{5,4},{6,7},{7,6},{8,9},{9,8},{10,11... | collective-permute-start | bytes 1474568 | tf_op jit(solution)/shard_map/ppermute | solution.py:23
  36.4 13.7 %copy-start.6 = (bf16[128,1536]{1,0:T(8,128)(2,1)}, bf16[128,1536]{1,0:T(8,128)(2,1)S(1)}, u32[]{:S(2)}) copy-start(bf16[128,1536]{1,0:T(8,128)(2,1)S(1)} %collective-permute-done.1.w3) | copy-start | bytes 1179652
  36.4 9.6 %collective-permute-start.3 = (bf16[128,1536]{1,0:T(8,128)(2,1)S(1)}, bf16[128,1536]{1,0:T(8,128)(2,1)}, u32[]{:S(2)}, u32[]{:S(2)}) collective-permute-start(bf16[128,1536]{1,0:T(8,128)(2,1)S(1)} %collective-permute-done.1.w3), channel_id=1, source_target_pairs={{0,1},{1,0},{2,3},{3,2},{4,5},{5,4},{6,7},{7,6},{8,9},{9,8},{10,11... | collective-permute-start | bytes 1179656 | tf_op jit(solution)/shard_map/ppermute | solution.py:23
  42.7 3.4 %collective-permute-start.7 = (bf16[128,1536]{1,0:T(8,128)(2,1)}, bf16[128,1536]{1,0:T(8,128)(2,1)}, u32[]{:S(2)}, u32[]{:S(2)}) collective-permute-start(bf16[128,1536]{1,0:T(8,128)(2,1)} %collective-permute-done.6.far.refs_2_), channel_id=1, source_target_pairs={{0,1},{1,0},{2,3},{3,2},{4,5},{5,4},{6,7},{7,6},{8,9},{9,8},{10,11... | collective-permute-start | bytes 1179656 | tf_op jit(solution)/shard_map/ppermute | solution.py:23
  44.3 5.9 %copy-start.2 = (bf16[384,1536]{1,0:T(8,128)(2,1)}, bf16[384,1536]{1,0:T(8,128)(2,1)S(1)}, u32[]{:S(2)}) copy-start(bf16[384,1536]{1,0:T(8,128)(2,1)S(1)} %collective-permute-done.4.w1) | copy-start | bytes 3538948
  46.0 12.4 %collective-permute-start.9 = (bf16[128,768]{1,0:T(8,128)(2,1)}, bf16[128,768]{1,0:T(8,128)(2,1)S(1)}, u32[]{:S(2)}, u32[]{:S(2)}) collective-permute-start(bf16[128,768]{1,0:T(8,128)(2,1)} %pad_maximum_fusion.1), channel_id=1, source_target_pairs={{0,2},{1,3},{2,0},{3,1},{4,6},{5,7},{6,4},{7,5},{8,10},{9,11},{10,... | collective-permute-start | bytes 589832 | tf_op jit(solution)/shard_map/ppermute | solution.py:23
  48.2 18.5 %collective-permute-start.11 = (bf16[128,1536]{1,0:T(8,128)(2,1)}, bf16[128,1536]{1,0:T(8,128)(2,1)S(1)}, u32[]{:S(2)}, u32[]{:S(2)}) collective-permute-start(bf16[128,1536]{1,0:T(8,128)(2,1)} %collective-permute-done.6.far.refs_2_), channel_id=1, source_target_pairs={{0,4},{4,0},{8,12},{12,8},{16,20},{20,16},{24,28},{28,24},{1,5},{5... | collective-permute-start | bytes 1179656 | tf_op jit(solution)/shard_map/ppermute | solution.py:23
  49.6 17.1 %collective-permute-start.12 = (bf16[128,1536]{1,0:T(8,128)(2,1)}, bf16[128,1536]{1,0:T(8,128)(2,1)}, u32[]{:S(2)}, u32[]{:S(2)}) collective-permute-start(bf16[128,1536]{1,0:T(8,128)(2,1)} %get-tuple-element.56), channel_id=1, source_target_pairs={{0,2},{1,3},{2,0},{3,1},{4,6},{5,7},{6,4},{7,5},{8,10},{9,11},{10,... | collective-permute-start | bytes 1179656 | tf_op jit(solution)/shard_map/ppermute | solution.py:23
  54.9 11.7 %all-to-all-start.2 = ((bf16[8,192,128]{2,1,0:T(8,128)(2,1)}), bf16[8,192,128]{2,1,0:T(8,128)(2,1)S(1)}, u32[]{:S(2)}, u32[]{:S(2)}) async-start(bf16[8,192,128]{2,1,0:T(8,128)(2,1)} %get-tuple-element.50), calls=%async_computation.2 | async-start | bytes 786432 | tf_op jit(solution)/shard_map/all_to_all | solution.py:257
  58.4 1.5 %copy-start.22 = (bf16[128,768]{1,0:T(8,128)(2,1)}, bf16[128,768]{1,0:T(8,128)(2,1)S(1)}, u32[]{:S(2)}) copy-start(bf16[128,768]{1,0:T(8,128)(2,1)S(1)} %collective-permute-done.9.tok_far) | copy-start | bytes 589828
  58.4 1.5 %collective-permute-start.10 = (bf16[128,768]{1,0:T(8,128)(2,1)S(1)}, bf16[128,768]{1,0:T(8,128)(2,1)S(1)}, u32[]{:S(2)}, u32[]{:S(2)}) collective-permute-start(bf16[128,768]{1,0:T(8,128)(2,1)S(1)} %collective-permute-done.9.tok_far), channel_id=1, source_target_pairs={{0,1},{1,0},{2,3},{3,2},{4,5},{5,4},{6,7},{7,6},{8,9},{9,8},{10,11... | collective-permute-start | bytes 589832 | tf_op jit(solution)/shard_map/ppermute | solution.py:23
  66.7 7.5 %copy-start.16 = (bf16[8,192,128]{2,1,0:T(8,128)(2,1)}, bf16[8,192,128]{2,1,0:T(8,128)(2,1)S(1)}, u32[]{:S(2)}) copy-start(bf16[8,192,128]{2,1,0:T(8,128)(2,1)S(1)} %all-to-all-done.2.got) | copy-start | bytes 1179652
  66.7 7.5 %copy-start.19 = (bf16[128,1536]{1,0:T(8,128)(2,1)}, bf16[128,1536]{1,0:T(8,128)(2,1)S(1)}, u32[]{:S(2)}) copy-start(bf16[128,1536]{1,0:T(8,128)(2,1)S(1)} %collective-permute-done.11.refs_6_) | copy-start | bytes 1179652
  66.7 20.1 %all-to-all-start.3 = ((bf16[32,16,384]{2,1,0:T(8,128)(2,1)}), bf16[32,16,384]{2,1,0:T(8,128)(2,1)S(1)}, u32[]{:S(2)}, u32[]{:S(2)}) async-start(bf16[32,16,384]{2,1,0:T(8,128)(2,1)} %bitcast.55), calls=%async_computation.3 | async-start | bytes 786432 | tf_op jit(solution)/shard_map/all_to_all | solution.py:282
  70.4 11.1 %copy-start.13 = (bf16[384,1536]{1,0:T(8,128)(2,1)S(1)}, bf16[384,1536]{1,0:T(8,128)(2,1)}, u32[]{:S(2)}) copy-start(bf16[384,1536]{1,0:T(8,128)(2,1)} %refs_0_.1) | copy-start | bytes 3538948
  70.4 3.8 %collective-permute-start.13 = (bf16[128,1536]{1,0:T(8,128)(2,1)}, bf16[128,1536]{1,0:T(8,128)(2,1)S(1)}, u32[]{:S(2)}, u32[]{:S(2)}) collective-permute-start(bf16[128,1536]{1,0:T(8,128)(2,1)} %collective-permute-done.8.refs_4_), channel_id=1, source_target_pairs={{0,1},{1,0},{2,3},{3,2},{4,5},{5,4},{6,7},{7,6},{8,9},{9,8},{10,11... | collective-permute-start | bytes 1179656 | tf_op jit(solution)/shard_map/ppermute | solution.py:23
  70.7 3.5 %collective-permute-start.14 = (bf16[128,1536]{1,0:T(8,128)(2,1)S(1)}, bf16[128,1536]{1,0:T(8,128)(2,1)S(1)}, u32[]{:S(2)}, u32[]{:S(2)}) collective-permute-start(bf16[128,1536]{1,0:T(8,128)(2,1)S(1)} %collective-permute-done.11.refs_6_), channel_id=1, source_target_pairs={{0,1},{1,0},{2,3},{3,2},{4,5},{5,4},{6,7},{7,6},{8,9},{9,8},{10,11... | collective-permute-start | bytes 1179656 | tf_op jit(solution)/shard_map/ppermute | solution.py:23
  71.0 15.2 %collective-permute-start.18 = (bf16[128,1536]{1,0:T(8,128)(2,1)}, bf16[128,1536]{1,0:T(8,128)(2,1)S(1)}, u32[]{:S(2)}, u32[]{:S(2)}) collective-permute-start(bf16[128,1536]{1,0:T(8,128)(2,1)} %collective-permute-done.12.refs_2_), channel_id=1, source_target_pairs={{0,4},{4,0},{8,12},{12,8},{16,20},{20,16},{24,28},{28,24},{1,5},{5... | collective-permute-start | bytes 1179656 | tf_op jit(solution)/shard_map/ppermute | solution.py:23
  72.7 14.0 %collective-permute-start.19 = (bf16[128,1536]{1,0:T(8,128)(2,1)}, bf16[128,1536]{1,0:T(8,128)(2,1)}, u32[]{:S(2)}, u32[]{:S(2)}) collective-permute-start(bf16[128,1536]{1,0:T(8,128)(2,1)} %get-tuple-element.68), channel_id=1, source_target_pairs={{0,2},{1,3},{2,0},{3,1},{4,6},{5,7},{6,4},{7,5},{8,10},{9,11},{10,... | collective-permute-start | bytes 1179656 | tf_op jit(solution)/shard_map/ppermute | solution.py:23
  80.0 9.0 %collective-permute-start.15 = (bf16[2,48,1536]{2,1,0:T(8,128)(2,1)}, bf16[2,48,1536]{2,1,0:T(8,128)(2,1)}, u32[]{:S(2)}, u32[]{:S(2)}) collective-permute-start(bf16[2,48,1536]{2,1,0:T(8,128)(2,1)} %get-tuple-element.62), channel_id=1, source_target_pairs={{0,8},{4,12},{8,0},{12,4},{16,24},{20,28},{24,16},{28,20},{1,9},{5... | collective-permute-start | bytes 884744 | tf_op jit(solution)/shard_map/ppermute | solution.py:23
  81.5 16.9 %collective-permute-start.17 = (bf16[384,1536]{1,0:T(8,128)(2,1)S(1)}, bf16[384,1536]{1,0:T(8,128)(2,1)S(1)}, u32[]{:S(2)}, u32[]{:S(2)}) collective-permute-start(bf16[384,1536]{1,0:T(8,128)(2,1)S(1)} %copy-done.13), channel_id=1, source_target_pairs={{0,1},{1,0},{2,3},{3,2},{4,5},{5,4},{6,7},{7,6},{8,9},{9,8},{10,11... | collective-permute-start | bytes 3538952 | tf_op jit(solution)/shard_map/ppermute | solution.py:23
  82.2 16.2 %collective-permute-start.20 = (bf16[128,1536]{1,0:T(8,128)(2,1)}, bf16[128,1536]{1,0:T(8,128)(2,1)}, u32[]{:S(2)}, u32[]{:S(2)}) collective-permute-start(bf16[128,1536]{1,0:T(8,128)(2,1)} %collective-permute-done.12.refs_2_), channel_id=1, source_target_pairs={{0,1},{1,0},{2,3},{3,2},{4,5},{5,4},{6,7},{7,6},{8,9},{9,8},{10,11... | collective-permute-start | bytes 1179656 | tf_op jit(solution)/shard_map/ppermute | solution.py:23
  86.2 2.8 %copy-start.18 = (bf16[128,1536]{1,0:T(8,128)(2,1)}, bf16[128,1536]{1,0:T(8,128)(2,1)S(1)}, u32[]{:S(2)}) copy-start(bf16[128,1536]{1,0:T(8,128)(2,1)S(1)} %collective-permute-done.18.refs_3_) | copy-start | bytes 1179652
  86.2 12.2 %collective-permute-start.21 = (bf16[128,1536]{1,0:T(8,128)(2,1)S(1)}, bf16[128,1536]{1,0:T(8,128)(2,1)}, u32[]{:S(2)}, u32[]{:S(2)}) collective-permute-start(bf16[128,1536]{1,0:T(8,128)(2,1)S(1)} %collective-permute-done.18.refs_3_), channel_id=1, source_target_pairs={{0,1},{1,0},{2,3},{3,2},{4,5},{5,4},{6,7},{7,6},{8,9},{9,8},{10,11... | collective-permute-start | bytes 1179656 | tf_op jit(solution)/shard_map/ppermute | solution.py:23
  86.8 11.6 %collective-permute-start.22 = (bf16[128,1536]{1,0:T(8,128)(2,1)}, bf16[128,1536]{1,0:T(8,128)(2,1)}, u32[]{:S(2)}, u32[]{:S(2)}) collective-permute-start(bf16[128,1536]{1,0:T(8,128)(2,1)} %collective-permute-done.19.refs_4_), channel_id=1, source_target_pairs={{0,1},{1,0},{2,3},{3,2},{4,5},{5,4},{6,7},{7,6},{8,9},{9,8},{10,11... | collective-permute-start | bytes 1179656 | tf_op jit(solution)/shard_map/ppermute | solution.py:23
  89.0 20.8 %all-to-all-start.4 = ((bf16[8,4,16,384]{3,2,1,0:T(8,128)(2,1)}), bf16[8,4,16,384]{3,2,1,0:T(8,128)(2,1)}, u32[]{:S(2)}, u32[]{:S(2)}) async-start(bf16[8,4,16,384]{3,2,1,0:T(8,128)(2,1)} %bitcast.44), calls=%async_computation.4 | async-start | bytes 786432 | tf_op jit(solution)/shard_map/all_to_all | solution.py:40
  94.7 3.7 %copy-start.14 = (f32[1,2,48,1536]{3,2,1,0:T(8,128)}, f32[1,2,48,1536]{3,2,1,0:T(8,128)S(1)}, u32[]{:S(2)}) copy-start(f32[1,2,48,1536]{3,2,1,0:T(8,128)S(1)} %add_bitcast_fusion) | copy-start | bytes 1769476
  95.4 20.1 %collective-permute-start.16 = (bf16[1,48,1536]{2,1,0:T(8,128)(2,1)}, bf16[1,48,1536]{2,1,0:T(8,128)(2,1)}, u32[]{:S(2)}, u32[]{:S(2)}) collective-permute-start(bf16[1,48,1536]{2,1,0:T(8,128)(2,1)} %fusion.8), channel_id=1, source_target_pairs={{0,16},{4,20},{8,24},{12,28},{16,0},{20,4},{24,8},{28,12},{1,17},{... | collective-permute-start | bytes 442376 | tf_op jit(solution)/shard_map/ppermute | solution.py:23
  99.4 10.4 %copy-start.1 = (bf16[384,1536]{1,0:T(8,128)(2,1)S(1)}, bf16[384,1536]{1,0:T(8,128)(2,1)}, u32[]{:S(2)}) copy-start(bf16[384,1536]{1,0:T(8,128)(2,1)} %w0.3) | copy-start | bytes 3538948
  99.4 10.4 %copy-start.3 = (bf16[384,1536]{1,0:T(8,128)(2,1)S(1)}, bf16[384,1536]{1,0:T(8,128)(2,1)}, u32[]{:S(2)}) copy-start(bf16[384,1536]{1,0:T(8,128)(2,1)} %copy-done.2) | copy-start | bytes 3538948
  99.4 10.4 %copy-start.5 = (bf16[256,1536]{1,0:T(8,128)(2,1)S(1)}, bf16[256,1536]{1,0:T(8,128)(2,1)}, u32[]{:S(2)}) copy-start(bf16[256,1536]{1,0:T(8,128)(2,1)} %copy-done.4) | copy-start | bytes 2359300
  99.4 10.4 %copy-start.7 = (bf16[128,1536]{1,0:T(8,128)(2,1)S(1)}, bf16[128,1536]{1,0:T(8,128)(2,1)}, u32[]{:S(2)}) copy-start(bf16[128,1536]{1,0:T(8,128)(2,1)} %copy-done.6) | copy-start | bytes 1179652
  99.4 10.4 %copy-start.11 = (s32[4]{0:T(128)S(1)}, s32[4]{0:T(128)}, u32[]{:S(2)}) copy-start(s32[4]{0:T(128)} %pad_add_fusion.where) | copy-start | bytes 52
  109.8 1.1 copy-start.8
  111.7 3.8 %copy-start.15 = (f32[1,2,48,1536]{3,2,1,0:T(8,128)S(1)}, f32[1,2,48,1536]{3,2,1,0:T(8,128)}, u32[]{:S(2)}) copy-start(f32[1,2,48,1536]{3,2,1,0:T(8,128)} %copy-done.14) | copy-start | bytes 1769476
  (5 other events, 4.0 us)

commit v6 on v5

--- a/solution.py
+++ b/solution.py
@@ -270,6 +270,7 @@
         tok_far,
         tok_side,
         flops=flops,
+        room=40,
     )
     if not split:
         grads = grads.reshape(ndp, nseq, offs, part).transpose(1, 0, 2, 3)

time: 118 us -> 117 us (level)
  waiting for transfers between devices: 25 us -> 30 us
  local copies, waits for them, and re-layouts: 14.7 us -> 10.6 us
    unnamed x52, local copies, waits for them, and re-layouts: 6.52 us -> 4.22 us
    all_to_all x3, waiting for transfers between devices: 10.9 us -> 12.9 us  [spread(): return lax.all_to_all(x, 'seq', split_axis=0, concat_axis=0, tiled=True)]
    ppermute x23, waiting for transfers between devices: 12.4 us -> 13.9 us  [swap(): return lax.ppermute(x, axis, [(i, i ^ bit) for i in range(n)])]
    all_to_all x1, waiting for transfers between devices: 1.76 us -> 3.16 us  [on_device(): lax.all_to_all(turned, ('seq', 'dp'), split_axis=0, concat_axis=0, tiled=...]
  transfers between devices with their start and end apart: 28 -> 28, of which waited for: 10 -> 10; matrix products, arithmetic and copies ran while one was open for 14% -> 11% of each run, Pallas kernels for 20% -> 20%
where the time goes in v6:
time: 117 us; the launch traced here: 116 us
  starting transfers between devices  43 us (37%)
  waiting for transfers between devices  30 us (26%)
  Pallas kernels  23.2 us (20%)
  local copies, waits for them, and re-layouts  10.6 us (9%)
  other arithmetic  5.79 us (5%)
  matrix products  2.42 us (2%)
    pallas_call x5, Pallas kernels, call(): pl.pallas_call(kernel, out_shape=list(outs), in_specs=[SMEM if x.dtype ==...  23.2 us
    ppermute x23, starting transfers between devices, swap(): return lax.ppermute(x, axis, [(i, i ^ bit) for i in range(n)])  20 us
    all_to_all x3, starting transfers between devices, spread(): return lax.all_to_all(x, 'seq', split_axis=0, concat_axis=0, tiled=True)  15.9 us
    ppermute x23, waiting for transfers between devices, swap(): return lax.ppermute(x, axis, [(i, i ^ bit) for i in range(n)])  13.9 us
    all_to_all x3, waiting for transfers between devices, spread(): return lax.all_to_all(x, 'seq', split_axis=0, concat_axis=0, tiled=True)  12.9 us
    unnamed x52, local copies, waits for them, and re-layouts  4.22 us
    all_to_all x1, starting transfers between devices, on_device(): lax.all_to_all(grads, ('seq', 'dp'), split_axis=0, concat_axis=0, tiled=T...  3.68 us
    all_to_all x1, starting transfers between devices, on_device(): lax.all_to_all(turned, ('seq', 'dp'), split_axis=0, concat_axis=0, tiled=...  3.45 us
  transfers between devices with their start and end apart: 28, of which 10 were waited for; matrix products, arithmetic and copies ran while one was open for 11% of the time, Pallas kernels for 20%

profile of v6, /device:TPU:0, one launch (start us, length us, event | category | flops | bytes accessed | tf_op | source)
XLA Modules:
  0.0 115.9 jit_solution(1086018511426868922)
XLA Ops:
  0.7 2.2 %slice.16 = bf16[256,1536]{1,0:T(8,128)(2,1)} slice(bf16[384,1536]{1,0:T(8,128)(2,1)} %w0.3), slice={[0:256], [0:1536]} | slice | bytes 1572864 | tf_op jit(solution)/shard_map/slice | solution.py:211
  2.9 2.9 %collective-permute-start = (bf16[256,1536]{1,0:T(8,128)(2,1)}, bf16[256,1536]{1,0:T(8,128)(2,1)}, u32[]{:S(2)}, u32[]{:S(2)}) collective-permute-start(bf16[256,1536]{1,0:T(8,128)(2,1)} %slice.16), channel_id=1, source_target_pairs={{0,2},{1,3},{2,0},{3,1},{4,6},{5,7},{6,4},{7,5},{8,10},{9,11},{10,... | collective-permute-start | bytes 2359304 | tf_op jit(solution)/shard_map/ppermute | solution.py:23
  5.8 1.0 convolution_convert_fusion.1
  6.8 5.8 %all-to-all-start = ((bf16[8,16,1536]{2,1,0:T(8,128)(2,1)}), bf16[8,16,1536]{2,1,0:T(8,128)(2,1)S(1)}, u32[]{:S(2)}, u32[]{:S(2)}) async-start(bf16[8,16,1536]{2,1,0:T(8,128)(2,1)} %bitcast.55), calls=%async_computation | async-start | bytes 786432 | tf_op jit(solution)/shard_map/all_to_all | solution.py:40
  12.7 2.0 %collective-permute-start.8 = (bf16[128,1536]{1,0:T(8,128)(2,1)S(1)}, bf16[128,1536]{1,0:T(8,128)(2,1)}, u32[]{:S(2)}, u32[]{:S(2)}) collective-permute-start(bf16[128,1536]{1,0:T(8,128)(2,1)S(1)} %bitcast.50), channel_id=1, source_target_pairs={{0,4},{4,0},{8,12},{12,8},{16,20},{20,16},{24,28},{28,24},{1,5},{5... | collective-permute-start | bytes 1179656 | tf_op jit(solution)/shard_map/ppermute | solution.py:23
  14.7 0.9 fusion.11
  15.7 0.8 slice.17
  16.4 0.7 copy.21
  17.1 0.7 dynamic-slice_bitcast_fusion.1
  17.8 6.2 %all-to-all-done = bf16[8,16,1536]{2,1,0:T(8,128)(2,1)S(1)} async-done(((bf16[8,16,1536]{2,1,0:T(8,128)(2,1)}), bf16[8,16,1536]{2,1,0:T(8,128)(2,1)S(1)}, u32[]{:S(2)}, u32[]{:S(2)}) %all-to-all-start) | async-done | bytes 393248 | tf_op jit(solution)/shard_map/all_to_all | solution.py:40
  24.1 1.3 %collective-permute-start.1 = (bf16[128,1536]{1,0:T(8,128)(2,1)}, bf16[128,1536]{1,0:T(8,128)(2,1)S(1)}, u32[]{:S(2)}, u32[]{:S(2)}) collective-permute-start(bf16[128,1536]{1,0:T(8,128)(2,1)} %slice.17), channel_id=1, source_target_pairs={{0,2},{1,3},{2,0},{3,1},{4,6},{5,7},{6,4},{7,5},{8,10},{9,11},{10,... | collective-permute-start | bytes 1179656 | tf_op jit(solution)/shard_map/ppermute | solution.py:23
  25.4 0.7 collective-permute-start.6
  26.1 1.1 fusion
  27.2 0.9 copy.22
  28.1 5.7 %all-to-all-start.1 = ((bf16[8,16,1536]{2,1,0:T(8,128)(2,1)}), bf16[8,16,1536]{2,1,0:T(8,128)(2,1)}, u32[]{:S(2)}, u32[]{:S(2)}) async-start(bf16[8,16,1536]{2,1,0:T(8,128)(2,1)} %copy.22), calls=%async_computation.1 | async-start | bytes 786432 | tf_op jit(solution)/shard_map/all_to_all | solution.py:40
  33.7 1.7 %pad_maximum_fusion = bf16[128,1920]{1,0:T(8,128)(2,1)} fusion(bf16[128,384]{1,0:T(8,128)(2,1)} %get-tuple-element.78, bf16[128,1536]{1,0:T(8,128)(2,1)S(1)} %bitcast.52), kind=kLoop, calls=%fused_computation.5 | loop fusion | flops 983040 | bytes 983040 | tf_op jit(solution)/shard_map/concatenate | solution.py:225
  35.4 0.9 collective-permute-done.1.w3
  36.3 6.3 %collective-permute-done.6.far.refs_2_ = bf16[128,1536]{1,0:T(8,128)(2,1)} collective-permute-done((bf16[128,1536]{1,0:T(8,128)(2,1)S(1)}, bf16[128,1536]{1,0:T(8,128)(2,1)}, u32[]{:S(2)}, u32[]{:S(2)}) %collective-permute-start.6) | collective-permute-done | bytes 393248 | tf_op jit(solution)/shard_map/ppermute | solution.py:23
  42.7 1.6 %pad_maximum_fusion.1 = bf16[128,768]{1,0:T(8,128)(2,1)} fusion(bf16[128,384]{1,0:T(8,128)(2,1)} %get-tuple-element.79, bf16[128,384]{1,0:T(8,128)(2,1)} %get-tuple-element.77), kind=kLoop, calls=%fused_computation.15 | loop fusion | flops 393216 | bytes 393216 | tf_op jit(solution)/shard_map/concatenate | solution.py:226
  44.3 1.6 %all-to-all-done.1 = bf16[8,16,1536]{2,1,0:T(8,128)(2,1)} async-done(((bf16[8,16,1536]{2,1,0:T(8,128)(2,1)}), bf16[8,16,1536]{2,1,0:T(8,128)(2,1)}, u32[]{:S(2)}, u32[]{:S(2)}) %all-to-all-start.1) | async-done | bytes 393248 | tf_op jit(solution)/shard_map/all_to_all | solution.py:40
  45.9 1.6 %collective-permute-start.9 = (bf16[128,768]{1,0:T(8,128)(2,1)}, bf16[128,768]{1,0:T(8,128)(2,1)S(1)}, u32[]{:S(2)}, u32[]{:S(2)}) collective-permute-start(bf16[128,768]{1,0:T(8,128)(2,1)} %pad_maximum_fusion.1), channel_id=1, source_target_pairs={{0,2},{1,3},{2,0},{3,1},{4,6},{5,7},{6,4},{7,5},{8,10},{9,11},{10,... | collective-permute-start | bytes 589832 | tf_op jit(solution)/shard_map/ppermute | solution.py:23
  47.5 0.7 pad_add_fusion.where
  48.1 1.5 %collective-permute-start.11 = (bf16[128,1536]{1,0:T(8,128)(2,1)}, bf16[128,1536]{1,0:T(8,128)(2,1)}, u32[]{:S(2)}, u32[]{:S(2)}) collective-permute-start(bf16[128,1536]{1,0:T(8,128)(2,1)} %collective-permute-done.6.far.refs_2_), channel_id=1, source_target_pairs={{0,4},{4,0},{8,12},{12,8},{16,20},{20,16},{24,28},{28,24},{1,5},{5... | collective-permute-start | bytes 1179656 | tf_op jit(solution)/shard_map/ppermute | solution.py:23
  50.2 4.8 %shard_map.85 = (bf16[128,1536]{1,0:T(8,128)(2,1)}, bf16[128,1536]{1,0:T(8,128)(2,1)}, bf16[8,192,128]{2,1,0:T(8,128)(2,1)}) custom-call(s32[4]{0:T(128)} %pad_add_fusion.where, bf16[128,1536]{1,0:T(8,128)(2,1)} %bitcast.12.mix, bf16[128,1536]{1,0:T(8,128)(2,1)} %bitcast.45, bf16[384,1536]{1,0:T(8,128)(2,1)} %w0.3, ...), custom_call_target="tpu_custom_call" | custom-call | flops 603979776 | bytes 6684688 | tf_op jit(solution)/shard_map/pallas_call | solution.py:49
  55.0 3.5 %all-to-all-start.2 = ((bf16[8,192,128]{2,1,0:T(8,128)(2,1)}), bf16[8,192,128]{2,1,0:T(8,128)(2,1)S(1)}, u32[]{:S(2)}, u32[]{:S(2)}) async-start(bf16[8,192,128]{2,1,0:T(8,128)(2,1)} %get-tuple-element.50), calls=%async_computation.2 | async-start | bytes 786432 | tf_op jit(solution)/shard_map/all_to_all | solution.py:257
  58.9 1.1 collective-permute-done.10.tok_side
  60.0 3.6 %shard_map.86 = bf16[8,4,16,384]{3,2,1,0:T(8,128)(2,1)} custom-call(s32[4]{0:T(128)S(1)} %copy-done.13, bf16[384,1536]{1,0:T(8,128)(2,1)S(1)} %copy-done.4, bf16[128,1536]{1,0:T(8,128)(2,1)S(1)} %bitcast.47, bf16[128,1536]{1,0:T(8,128)(2,1)S(1)} %bitcast.53, bf16[128,1920]{1,0:T(8,128)(2,1)} %collective-permute-done.5.near.refs_1_, ...), custom_call_target="tpu_custom_call" | custom-call | flops 603979776 | bytes 4030480 | tf_op jit(solution)/shard_map/pallas_call | solution.py:49
  63.6 3.2 %all-to-all-done.2.got = bf16[8,192,128]{2,1,0:T(8,128)(2,1)S(1)} async-done(((bf16[8,192,128]{2,1,0:T(8,128)(2,1)}), bf16[8,192,128]{2,1,0:T(8,128)(2,1)S(1)}, u32[]{:S(2)}, u32[]{:S(2)}) %all-to-all-start.2) | async-done | bytes 393248 | tf_op jit(solution)/shard_map/all_to_all | solution.py:257
  66.7 3.7 %all-to-all-start.3 = ((bf16[32,16,384]{2,1,0:T(8,128)(2,1)}), bf16[32,16,384]{2,1,0:T(8,128)(2,1)S(1)}, u32[]{:S(2)}, u32[]{:S(2)}) async-start(bf16[32,16,384]{2,1,0:T(8,128)(2,1)} %bitcast.13), calls=%async_computation.3 | async-start | bytes 786432 | tf_op jit(solution)/shard_map/all_to_all | solution.py:283
  71.0 1.8 %collective-permute-start.18 = (bf16[128,1536]{1,0:T(8,128)(2,1)}, bf16[128,1536]{1,0:T(8,128)(2,1)S(1)}, u32[]{:S(2)}, u32[]{:S(2)}) collective-permute-start(bf16[128,1536]{1,0:T(8,128)(2,1)} %collective-permute-done.12.refs_2_), channel_id=1, source_target_pairs={{0,4},{4,0},{8,12},{12,8},{16,20},{20,16},{24,28},{28,24},{1,5},{5... | collective-permute-start | bytes 1179656 | tf_op jit(solution)/shard_map/ppermute | solution.py:23
  72.8 1.5 %collective-permute-start.19 = (bf16[128,1536]{1,0:T(8,128)(2,1)S(1)}, bf16[128,1536]{1,0:T(8,128)(2,1)}, u32[]{:S(2)}, u32[]{:S(2)}) collective-permute-start(bf16[128,1536]{1,0:T(8,128)(2,1)S(1)} %copy-done.21), channel_id=1, source_target_pairs={{0,2},{1,3},{2,0},{3,1},{4,6},{5,7},{6,4},{7,5},{8,10},{9,11},{10,... | collective-permute-start | bytes 1179656 | tf_op jit(solution)/shard_map/ppermute | solution.py:23
  74.3 0.7 copy-done.22
  75.0 0.7 copy-done.23
  75.7 4.3 %shard_map.87 = (f32[2,48,1536]{2,1,0:T(8,128)}, bf16[2,48,1536]{2,1,0:T(8,128)(2,1)}) custom-call(s32[4]{0:T(128)} %pad_add_fusion.where, bf16[8,192,128]{2,1,0:T(8,128)(2,1)} %copy-done.17, bf16[128,1536]{1,0:T(8,128)(2,1)} %bitcast.48, bf16[128,1920]{1,0:T(8,128)(2,1)} %collective-permute-done.5.near.refs_1_, ...), custom_call_target="tpu_custom_call" | custom-call | flops 603979776 | bytes 4522000 | tf_op jit(solution)/shard_map/pallas_call | solution.py:49
  80.0 1.5 %collective-permute-start.15 = (bf16[2,48,1536]{2,1,0:T(8,128)(2,1)}, bf16[2,48,1536]{2,1,0:T(8,128)(2,1)}, u32[]{:S(2)}, u32[]{:S(2)}) collective-permute-start(bf16[2,48,1536]{2,1,0:T(8,128)(2,1)} %get-tuple-element.62), channel_id=1, source_target_pairs={{0,8},{4,12},{8,0},{12,4},{16,24},{20,28},{24,16},{28,20},{1,9},{5... | collective-permute-start | bytes 884744 | tf_op jit(solution)/shard_map/ppermute | solution.py:23
  81.6 0.6 collective-permute-start.20
  82.1 4.1 %collective-permute-done.18.refs_3_ = bf16[128,1536]{1,0:T(8,128)(2,1)S(1)} collective-permute-done((bf16[128,1536]{1,0:T(8,128)(2,1)}, bf16[128,1536]{1,0:T(8,128)(2,1)S(1)}, u32[]{:S(2)}, u32[]{:S(2)}) %collective-permute-start.18) | collective-permute-done | bytes 393248 | tf_op jit(solution)/shard_map/ppermute | solution.py:23
  87.1 0.9 copy.36
  88.0 1.1 collective-permute-done.15
  89.0 4.4 %all-to-all-start.4 = ((bf16[8,4,16,384]{3,2,1,0:T(8,128)(2,1)}), bf16[8,4,16,384]{3,2,1,0:T(8,128)(2,1)S(1)}, u32[]{:S(2)}, u32[]{:S(2)}) async-start(bf16[8,4,16,384]{3,2,1,0:T(8,128)(2,1)} %bitcast.44), calls=%async_computation.4 | async-start | bytes 786432 | tf_op jit(solution)/shard_map/all_to_all | solution.py:40
  93.5 1.0 add_bitcast_fusion
  94.5 3.0 %collective-permute-start.16 = (bf16[1,48,1536]{2,1,0:T(8,128)(2,1)S(1)}, bf16[1,48,1536]{2,1,0:T(8,128)(2,1)S(1)}, u32[]{:S(2)}, u32[]{:S(2)}) collective-permute-start(bf16[1,48,1536]{2,1,0:T(8,128)(2,1)S(1)} %fusion.8), channel_id=1, source_target_pairs={{0,16},{4,20},{8,24},{12,28},{16,0},{20,4},{24,8},{28,12},{1,17},{... | collective-permute-start | bytes 442376 | tf_op jit(solution)/shard_map/ppermute | solution.py:23
  97.5 0.7 copy-done.20
  98.3 6.4 %shard_map.88 = (bf16[128,1536]{1,0:T(8,128)(2,1)}, f32[128,1536]{1,0:T(8,128)}) custom-call(s32[4]{0:T(128)} %pad_add_fusion.where, bf16[128,1536]{1,0:T(8,128)(2,1)} %get-tuple-element.65.gated, bf16[128,1536]{1,0:T(8,128)(2,1)} %get-tuple-element.66.mon, bf16[128,1536]{1,0:T(8,128)(2,1)} %bitcast.46, bf16[128,1536]{1,0:T(8,128)(2,1)} %bitcast.49, ...), custom_call_target="tpu_custom_call" | custom-call | flops 1207959552 | bytes 7471120 | tf_op jit(solution)/shard_map/pallas_call | solution.py:49
  104.7 5.1 %all-to-all-done.4.back = bf16[8,4,16,384]{3,2,1,0:T(8,128)(2,1)S(1)} async-done(((bf16[8,4,16,384]{3,2,1,0:T(8,128)(2,1)}), bf16[8,4,16,384]{3,2,1,0:T(8,128)(2,1)S(1)}, u32[]{:S(2)}, u32[]{:S(2)}) %all-to-all-start.4) | async-done | bytes 393248 | tf_op jit(solution)/shard_map/all_to_all | solution.py:40
  109.8 1.1 copy-done.10
  110.9 4.2 %shard_map.89 = bf16[128,1536]{1,0:T(8,128)(2,1)} custom-call(s32[4]{0:T(128)S(1)} %copy-done.14, bf16[8,4,16,384]{3,2,1,0:T(8,128)(2,1)S(1)} %all-to-all-done.4.back, bf16[128,128]{1,0:T(8,128)(2,1)S(1)} %bitcast.54, f32[128,1536]{1,0:T(8,128)S(1)} %copy-done.10, bf16[384,1536]{1,0:T(8,128)(2,1)S(1)} %copy-done.1, ...), custom_call_target="tpu_custom_call" | custom-call | flops 603979776 | bytes 6324240 | tf_op jit(solution)/shard_map/pallas_call | solution.py:49
  115.1 0.8 fusion.7
  (80 shorter events, 2.8 us)
Async XLA Ops:
  0.6 5.2 %copy-start.2 = (bf16[1,128,1536]{2,1,0:T(8,128)(2,1)S(1)}, bf16[1,128,1536]{2,1,0:T(8,128)(2,1)}, u32[]{:S(2)}) copy-start(bf16[1,128,1536]{2,1,0:T(8,128)(2,1)} %param.6) | copy-start | bytes 1179652
  0.6 5.2 %copy-start.11 = (bf16[1,128,128]{2,1,0:T(8,128)(2,1)S(1)}, bf16[1,128,128]{2,1,0:T(8,128)(2,1)}, u32[]{:S(2)}) copy-start(bf16[1,128,128]{2,1,0:T(8,128)(2,1)} %param.9) | copy-start | bytes 98308
  0.7 14.1 %copy-start.4 = (bf16[384,1536]{1,0:T(8,128)(2,1)S(1)}, bf16[384,1536]{1,0:T(8,128)(2,1)}, u32[]{:S(2)}) copy-start(bf16[384,1536]{1,0:T(8,128)(2,1)} %refs_0_.1) | copy-start | bytes 3538948
  2.9 9.8 %copy-start = (bf16[384,1536]{1,0:T(8,128)(2,1)S(1)}, bf16[384,1536]{1,0:T(8,128)(2,1)}, u32[]{:S(2)}) copy-start(bf16[384,1536]{1,0:T(8,128)(2,1)} %w0.3) | copy-start | bytes 3538948
  2.9 9.9 %copy-start.5 = (bf16[1,128,1536]{2,1,0:T(8,128)(2,1)S(1)}, bf16[1,128,1536]{2,1,0:T(8,128)(2,1)}, u32[]{:S(2)}) copy-start(bf16[1,128,1536]{2,1,0:T(8,128)(2,1)} %param.11) | copy-start | bytes 1179652
  2.9 21.2 %collective-permute-start = (bf16[256,1536]{1,0:T(8,128)(2,1)}, bf16[256,1536]{1,0:T(8,128)(2,1)}, u32[]{:S(2)}, u32[]{:S(2)}) collective-permute-start(bf16[256,1536]{1,0:T(8,128)(2,1)} %slice.16), channel_id=1, source_target_pairs={{0,2},{1,3},{2,0},{3,1},{4,6},{5,7},{6,4},{7,5},{8,10},{9,11},{10,... | collective-permute-start | bytes 2359304 | tf_op jit(solution)/shard_map/ppermute | solution.py:23
  6.8 17.3 %all-to-all-start = ((bf16[8,16,1536]{2,1,0:T(8,128)(2,1)}), bf16[8,16,1536]{2,1,0:T(8,128)(2,1)S(1)}, u32[]{:S(2)}, u32[]{:S(2)}) async-start(bf16[8,16,1536]{2,1,0:T(8,128)(2,1)} %bitcast.55), calls=%async_computation | async-start | bytes 786432 | tf_op jit(solution)/shard_map/all_to_all | solution.py:40
  12.6 31.7 %collective-permute-start.4 = (bf16[384,1536]{1,0:T(8,128)(2,1)S(1)}, bf16[384,1536]{1,0:T(8,128)(2,1)}, u32[]{:S(2)}, u32[]{:S(2)}) collective-permute-start(bf16[384,1536]{1,0:T(8,128)(2,1)S(1)} %copy-done), channel_id=1, source_target_pairs={{0,1},{1,0},{2,3},{3,2},{4,5},{5,4},{6,7},{7,6},{8,9},{9,8},{10,11... | collective-permute-start | bytes 3538952 | tf_op jit(solution)/shard_map/ppermute | solution.py:23
  12.7 22.7 %collective-permute-start.8 = (bf16[128,1536]{1,0:T(8,128)(2,1)S(1)}, bf16[128,1536]{1,0:T(8,128)(2,1)}, u32[]{:S(2)}, u32[]{:S(2)}) collective-permute-start(bf16[128,1536]{1,0:T(8,128)(2,1)S(1)} %bitcast.50), channel_id=1, source_target_pairs={{0,4},{4,0},{8,12},{12,8},{16,20},{20,16},{24,28},{28,24},{1,5},{5... | collective-permute-start | bytes 1179656 | tf_op jit(solution)/shard_map/ppermute | solution.py:23
  24.1 12.3 %collective-permute-start.1 = (bf16[128,1536]{1,0:T(8,128)(2,1)}, bf16[128,1536]{1,0:T(8,128)(2,1)S(1)}, u32[]{:S(2)}, u32[]{:S(2)}) collective-permute-start(bf16[128,1536]{1,0:T(8,128)(2,1)} %slice.17), channel_id=1, source_target_pairs={{0,2},{1,3},{2,0},{3,1},{4,6},{5,7},{6,4},{7,5},{8,10},{9,11},{10,... | collective-permute-start | bytes 1179656 | tf_op jit(solution)/shard_map/ppermute | solution.py:23
  25.4 20.5 %collective-permute-start.2 = (bf16[256,1536]{1,0:T(8,128)(2,1)}, bf16[256,1536]{1,0:T(8,128)(2,1)}, u32[]{:S(2)}, u32[]{:S(2)}) collective-permute-start(bf16[256,1536]{1,0:T(8,128)(2,1)} %collective-permute-done.w2), channel_id=1, source_target_pairs={{0,1},{1,0},{2,3},{3,2},{4,5},{5,4},{6,7},{7,6},{8,9},{9,8},{10,11... | collective-permute-start | bytes 2359304 | tf_op jit(solution)/shard_map/ppermute | solution.py:23
  25.4 17.3 %collective-permute-start.6 = (bf16[128,1536]{1,0:T(8,128)(2,1)S(1)}, bf16[128,1536]{1,0:T(8,128)(2,1)}, u32[]{:S(2)}, u32[]{:S(2)}) collective-permute-start(bf16[128,1536]{1,0:T(8,128)(2,1)S(1)} %bitcast.51), channel_id=1, source_target_pairs={{0,2},{1,3},{2,0},{3,1},{4,6},{5,7},{6,4},{7,5},{8,10},{9,11},{10,... | collective-permute-start | bytes 1179656 | tf_op jit(solution)/shard_map/ppermute | solution.py:23
  28.1 17.8 %all-to-all-start.1 = ((bf16[8,16,1536]{2,1,0:T(8,128)(2,1)}), bf16[8,16,1536]{2,1,0:T(8,128)(2,1)}, u32[]{:S(2)}, u32[]{:S(2)}) async-start(bf16[8,16,1536]{2,1,0:T(8,128)(2,1)} %copy.22), calls=%async_computation.1 | async-start | bytes 786432 | tf_op jit(solution)/shard_map/all_to_all | solution.py:40
  35.4 8.9 %collective-permute-start.5 = (bf16[128,1920]{1,0:T(8,128)(2,1)}, bf16[128,1920]{1,0:T(8,128)(2,1)}, u32[]{:S(2)}, u32[]{:S(2)}) collective-permute-start(bf16[128,1920]{1,0:T(8,128)(2,1)} %pad_maximum_fusion), channel_id=1, source_target_pairs={{0,1},{1,0},{2,3},{3,2},{4,5},{5,4},{6,7},{7,6},{8,9},{9,8},{10,11... | collective-permute-start | bytes 1474568 | tf_op jit(solution)/shard_map/ppermute | solution.py:23
  36.3 13.8 %copy-start.6 = (bf16[128,1536]{1,0:T(8,128)(2,1)}, bf16[128,1536]{1,0:T(8,128)(2,1)S(1)}, u32[]{:S(2)}) copy-start(bf16[128,1536]{1,0:T(8,128)(2,1)S(1)} %collective-permute-done.1.w3) | copy-start | bytes 1179652
  36.3 9.6 %collective-permute-start.3 = (bf16[128,1536]{1,0:T(8,128)(2,1)S(1)}, bf16[128,1536]{1,0:T(8,128)(2,1)S(1)}, u32[]{:S(2)}, u32[]{:S(2)}) collective-permute-start(bf16[128,1536]{1,0:T(8,128)(2,1)S(1)} %collective-permute-done.1.w3), channel_id=1, source_target_pairs={{0,1},{1,0},{2,3},{3,2},{4,5},{5,4},{6,7},{7,6},{8,9},{9,8},{10,11... | collective-permute-start | bytes 1179656 | tf_op jit(solution)/shard_map/ppermute | solution.py:23
  42.7 3.2 %collective-permute-start.7 = (bf16[128,1536]{1,0:T(8,128)(2,1)}, bf16[128,1536]{1,0:T(8,128)(2,1)}, u32[]{:S(2)}, u32[]{:S(2)}) collective-permute-start(bf16[128,1536]{1,0:T(8,128)(2,1)} %collective-permute-done.6.far.refs_2_), channel_id=1, source_target_pairs={{0,1},{1,0},{2,3},{3,2},{4,5},{5,4},{6,7},{7,6},{8,9},{9,8},{10,11... | collective-permute-start | bytes 1179656 | tf_op jit(solution)/shard_map/ppermute | solution.py:23
  45.9 4.2 %copy-start.8 = (bf16[128,1536]{1,0:T(8,128)(2,1)}, bf16[128,1536]{1,0:T(8,128)(2,1)S(1)}, u32[]{:S(2)}) copy-start(bf16[128,1536]{1,0:T(8,128)(2,1)S(1)} %collective-permute-done.3.w5) | copy-start | bytes 1179652
  45.9 12.5 %collective-permute-start.9 = (bf16[128,768]{1,0:T(8,128)(2,1)}, bf16[128,768]{1,0:T(8,128)(2,1)S(1)}, u32[]{:S(2)}, u32[]{:S(2)}) collective-permute-start(bf16[128,768]{1,0:T(8,128)(2,1)} %pad_maximum_fusion.1), channel_id=1, source_target_pairs={{0,2},{1,3},{2,0},{3,1},{4,6},{5,7},{6,4},{7,5},{8,10},{9,11},{10,... | collective-permute-start | bytes 589832 | tf_op jit(solution)/shard_map/ppermute | solution.py:23
  48.1 18.6 %collective-permute-start.11 = (bf16[128,1536]{1,0:T(8,128)(2,1)}, bf16[128,1536]{1,0:T(8,128)(2,1)}, u32[]{:S(2)}, u32[]{:S(2)}) collective-permute-start(bf16[128,1536]{1,0:T(8,128)(2,1)} %collective-permute-done.6.far.refs_2_), channel_id=1, source_target_pairs={{0,4},{4,0},{8,12},{12,8},{16,20},{20,16},{24,28},{28,24},{1,5},{5... | collective-permute-start | bytes 1179656 | tf_op jit(solution)/shard_map/ppermute | solution.py:23
  49.6 17.1 %collective-permute-start.12 = (bf16[128,1536]{1,0:T(8,128)(2,1)}, bf16[128,1536]{1,0:T(8,128)(2,1)}, u32[]{:S(2)}, u32[]{:S(2)}) collective-permute-start(bf16[128,1536]{1,0:T(8,128)(2,1)} %get-tuple-element.56), channel_id=1, source_target_pairs={{0,2},{1,3},{2,0},{3,1},{4,6},{5,7},{6,4},{7,5},{8,10},{9,11},{10,... | collective-permute-start | bytes 1179656 | tf_op jit(solution)/shard_map/ppermute | solution.py:23
  50.1 9.9 %copy-start.3 = (bf16[1,128,1536]{2,1,0:T(8,128)(2,1)S(1)}, bf16[1,128,1536]{2,1,0:T(8,128)(2,1)}, u32[]{:S(2)}) copy-start(bf16[1,128,1536]{2,1,0:T(8,128)(2,1)} %param.6) | copy-start | bytes 1179652
  50.1 9.9 %copy-start.13 = (s32[4]{0:T(128)S(1)}, s32[4]{0:T(128)}, u32[]{:S(2)}) copy-start(s32[4]{0:T(128)} %pad_add_fusion.where) | copy-start | bytes 52
  55.0 11.7 %all-to-all-start.2 = ((bf16[8,192,128]{2,1,0:T(8,128)(2,1)}), bf16[8,192,128]{2,1,0:T(8,128)(2,1)S(1)}, u32[]{:S(2)}, u32[]{:S(2)}) async-start(bf16[8,192,128]{2,1,0:T(8,128)(2,1)} %get-tuple-element.50), calls=%async_computation.2 | async-start | bytes 786432 | tf_op jit(solution)/shard_map/all_to_all | solution.py:257
  58.5 14.3 %copy-start.21 = (bf16[128,1536]{1,0:T(8,128)(2,1)S(1)}, bf16[128,1536]{1,0:T(8,128)(2,1)}, u32[]{:S(2)}) copy-start(bf16[128,1536]{1,0:T(8,128)(2,1)} %get-tuple-element.68) | copy-start | bytes 1179652
  58.5 1.5 %collective-permute-start.10 = (bf16[128,768]{1,0:T(8,128)(2,1)S(1)}, bf16[128,768]{1,0:T(8,128)(2,1)S(1)}, u32[]{:S(2)}, u32[]{:S(2)}) collective-permute-start(bf16[128,768]{1,0:T(8,128)(2,1)S(1)} %collective-permute-done.9.tok_far), channel_id=1, source_target_pairs={{0,1},{1,0},{2,3},{3,2},{4,5},{5,4},{6,7},{7,6},{8,9},{9,8},{10,11... | collective-permute-start | bytes 589832 | tf_op jit(solution)/shard_map/ppermute | solution.py:23
  66.7 7.5 %copy-start.17 = (bf16[8,192,128]{2,1,0:T(8,128)(2,1)}, bf16[8,192,128]{2,1,0:T(8,128)(2,1)S(1)}, u32[]{:S(2)}) copy-start(bf16[8,192,128]{2,1,0:T(8,128)(2,1)S(1)} %all-to-all-done.2.got) | copy-start | bytes 1179652
  66.7 20.0 %all-to-all-start.3 = ((bf16[32,16,384]{2,1,0:T(8,128)(2,1)}), bf16[32,16,384]{2,1,0:T(8,128)(2,1)S(1)}, u32[]{:S(2)}, u32[]{:S(2)}) async-start(bf16[32,16,384]{2,1,0:T(8,128)(2,1)} %bitcast.13), calls=%async_computation.3 | async-start | bytes 786432 | tf_op jit(solution)/shard_map/all_to_all | solution.py:283
  70.4 3.8 %collective-permute-start.13 = (bf16[128,1536]{1,0:T(8,128)(2,1)}, bf16[128,1536]{1,0:T(8,128)(2,1)S(1)}, u32[]{:S(2)}, u32[]{:S(2)}) collective-permute-start(bf16[128,1536]{1,0:T(8,128)(2,1)} %collective-permute-done.8.refs_4_), channel_id=1, source_target_pairs={{0,1},{1,0},{2,3},{3,2},{4,5},{5,4},{6,7},{7,6},{8,9},{9,8},{10,11... | collective-permute-start | bytes 1179656 | tf_op jit(solution)/shard_map/ppermute | solution.py:23
  70.7 3.5 %collective-permute-start.14 = (bf16[128,1536]{1,0:T(8,128)(2,1)}, bf16[128,1536]{1,0:T(8,128)(2,1)S(1)}, u32[]{:S(2)}, u32[]{:S(2)}) collective-permute-start(bf16[128,1536]{1,0:T(8,128)(2,1)} %collective-permute-done.11.refs_6_), channel_id=1, source_target_pairs={{0,1},{1,0},{2,3},{3,2},{4,5},{5,4},{6,7},{7,6},{8,9},{9,8},{10,11... | collective-permute-start | bytes 1179656 | tf_op jit(solution)/shard_map/ppermute | solution.py:23
  71.0 15.2 %collective-permute-start.18 = (bf16[128,1536]{1,0:T(8,128)(2,1)}, bf16[128,1536]{1,0:T(8,128)(2,1)S(1)}, u32[]{:S(2)}, u32[]{:S(2)}) collective-permute-start(bf16[128,1536]{1,0:T(8,128)(2,1)} %collective-permute-done.12.refs_2_), channel_id=1, source_target_pairs={{0,4},{4,0},{8,12},{12,8},{16,20},{20,16},{24,28},{28,24},{1,5},{5... | collective-permute-start | bytes 1179656 | tf_op jit(solution)/shard_map/ppermute | solution.py:23
  72.8 13.9 %collective-permute-start.19 = (bf16[128,1536]{1,0:T(8,128)(2,1)S(1)}, bf16[128,1536]{1,0:T(8,128)(2,1)}, u32[]{:S(2)}, u32[]{:S(2)}) collective-permute-start(bf16[128,1536]{1,0:T(8,128)(2,1)S(1)} %copy-done.21), channel_id=1, source_target_pairs={{0,2},{1,3},{2,0},{3,1},{4,6},{5,7},{6,4},{7,5},{8,10},{9,11},{10,... | collective-permute-start | bytes 1179656 | tf_op jit(solution)/shard_map/ppermute | solution.py:23
  80.0 9.0 %collective-permute-start.15 = (bf16[2,48,1536]{2,1,0:T(8,128)(2,1)}, bf16[2,48,1536]{2,1,0:T(8,128)(2,1)}, u32[]{:S(2)}, u32[]{:S(2)}) collective-permute-start(bf16[2,48,1536]{2,1,0:T(8,128)(2,1)} %get-tuple-element.62), channel_id=1, source_target_pairs={{0,8},{4,12},{8,0},{12,4},{16,24},{20,28},{24,16},{28,20},{1,9},{5... | collective-permute-start | bytes 884744 | tf_op jit(solution)/shard_map/ppermute | solution.py:23
  81.5 16.0 %collective-permute-start.17 = (bf16[384,1536]{1,0:T(8,128)(2,1)S(1)}, bf16[384,1536]{1,0:T(8,128)(2,1)}, u32[]{:S(2)}, u32[]{:S(2)}) collective-permute-start(bf16[384,1536]{1,0:T(8,128)(2,1)S(1)} %copy-done.4), channel_id=1, source_target_pairs={{0,1},{1,0},{2,3},{3,2},{4,5},{5,4},{6,7},{7,6},{8,9},{9,8},{10,11... | collective-permute-start | bytes 3538952 | tf_op jit(solution)/shard_map/ppermute | solution.py:23
  81.6 15.9 %collective-permute-start.20 = (bf16[128,1536]{1,0:T(8,128)(2,1)}, bf16[128,1536]{1,0:T(8,128)(2,1)S(1)}, u32[]{:S(2)}, u32[]{:S(2)}) collective-permute-start(bf16[128,1536]{1,0:T(8,128)(2,1)} %collective-permute-done.12.refs_2_), channel_id=1, source_target_pairs={{0,1},{1,0},{2,3},{3,2},{4,5},{5,4},{6,7},{7,6},{8,9},{9,8},{10,11... | collective-permute-start | bytes 1179656 | tf_op jit(solution)/shard_map/ppermute | solution.py:23
  86.2 2.8 %copy-start.19 = (bf16[128,1536]{1,0:T(8,128)(2,1)}, bf16[128,1536]{1,0:T(8,128)(2,1)S(1)}, u32[]{:S(2)}) copy-start(bf16[128,1536]{1,0:T(8,128)(2,1)S(1)} %collective-permute-done.18.refs_3_) | copy-start | bytes 1179652
  86.2 11.3 %collective-permute-start.21 = (bf16[128,1536]{1,0:T(8,128)(2,1)S(1)}, bf16[128,1536]{1,0:T(8,128)(2,1)}, u32[]{:S(2)}, u32[]{:S(2)}) collective-permute-start(bf16[128,1536]{1,0:T(8,128)(2,1)S(1)} %collective-permute-done.18.refs_3_), channel_id=1, source_target_pairs={{0,1},{1,0},{2,3},{3,2},{4,5},{5,4},{6,7},{7,6},{8,9},{9,8},{10,11... | collective-permute-start | bytes 1179656 | tf_op jit(solution)/shard_map/ppermute | solution.py:23
  86.6 10.9 %collective-permute-start.22 = (bf16[128,1536]{1,0:T(8,128)(2,1)}, bf16[128,1536]{1,0:T(8,128)(2,1)}, u32[]{:S(2)}, u32[]{:S(2)}) collective-permute-start(bf16[128,1536]{1,0:T(8,128)(2,1)} %collective-permute-done.19.refs_4_), channel_id=1, source_target_pairs={{0,1},{1,0},{2,3},{3,2},{4,5},{5,4},{6,7},{7,6},{8,9},{9,8},{10,11... | collective-permute-start | bytes 1179656 | tf_op jit(solution)/shard_map/ppermute | solution.py:23
  86.7 6.7 %copy-start.18 = (f32[2,48,1536]{2,1,0:T(8,128)S(1)}, f32[2,48,1536]{2,1,0:T(8,128)}, u32[]{:S(2)}) copy-start(f32[2,48,1536]{2,1,0:T(8,128)} %get-tuple-element.61) | copy-start | bytes 1769476
  89.0 20.7 %all-to-all-start.4 = ((bf16[8,4,16,384]{3,2,1,0:T(8,128)(2,1)}), bf16[8,4,16,384]{3,2,1,0:T(8,128)(2,1)S(1)}, u32[]{:S(2)}, u32[]{:S(2)}) async-start(bf16[8,4,16,384]{3,2,1,0:T(8,128)(2,1)} %bitcast.44), calls=%async_computation.4 | async-start | bytes 786432 | tf_op jit(solution)/shard_map/all_to_all | solution.py:40
  94.5 3.1 %copy-start.15 = (f32[1,2,48,1536]{3,2,1,0:T(8,128)}, f32[1,2,48,1536]{3,2,1,0:T(8,128)S(1)}, u32[]{:S(2)}) copy-start(f32[1,2,48,1536]{3,2,1,0:T(8,128)S(1)} %add_bitcast_fusion) | copy-start | bytes 1769476
  94.5 20.6 %collective-permute-start.16 = (bf16[1,48,1536]{2,1,0:T(8,128)(2,1)S(1)}, bf16[1,48,1536]{2,1,0:T(8,128)(2,1)S(1)}, u32[]{:S(2)}, u32[]{:S(2)}) collective-permute-start(bf16[1,48,1536]{2,1,0:T(8,128)(2,1)S(1)} %fusion.8), channel_id=1, source_target_pairs={{0,16},{4,20},{8,24},{12,28},{16,0},{20,4},{24,8},{28,12},{1,17},{... | collective-permute-start | bytes 442376 | tf_op jit(solution)/shard_map/ppermute | solution.py:23
  98.3 11.5 %copy-start.1 = (bf16[384,1536]{1,0:T(8,128)(2,1)S(1)}, bf16[384,1536]{1,0:T(8,128)(2,1)}, u32[]{:S(2)}) copy-start(bf16[384,1536]{1,0:T(8,128)(2,1)} %w0.3) | copy-start | bytes 3538948
  98.3 11.5 %copy-start.7 = (bf16[128,1536]{1,0:T(8,128)(2,1)S(1)}, bf16[128,1536]{1,0:T(8,128)(2,1)}, u32[]{:S(2)}) copy-start(bf16[128,1536]{1,0:T(8,128)(2,1)} %copy-done.6) | copy-start | bytes 1179652
  98.3 11.5 %copy-start.9 = (bf16[128,1536]{1,0:T(8,128)(2,1)S(1)}, bf16[128,1536]{1,0:T(8,128)(2,1)}, u32[]{:S(2)}) copy-start(bf16[128,1536]{1,0:T(8,128)(2,1)} %copy-done.8) | copy-start | bytes 1179652
  98.3 11.5 %copy-start.12 = (bf16[1,128,128]{2,1,0:T(8,128)(2,1)S(1)}, bf16[1,128,128]{2,1,0:T(8,128)(2,1)}, u32[]{:S(2)}) copy-start(bf16[1,128,128]{2,1,0:T(8,128)(2,1)} %param.9) | copy-start | bytes 98308
  98.3 11.5 %copy-start.14 = (s32[4]{0:T(128)S(1)}, s32[4]{0:T(128)}, u32[]{:S(2)}) copy-start(s32[4]{0:T(128)} %pad_add_fusion.where) | copy-start | bytes 52
  110.9 4.2 %copy-start.16 = (f32[1,2,48,1536]{3,2,1,0:T(8,128)S(1)}, f32[1,2,48,1536]{3,2,1,0:T(8,128)}, u32[]{:S(2)}) copy-start(f32[1,2,48,1536]{3,2,1,0:T(8,128)} %copy-done.15) | copy-start | bytes 1769476
  (5 other events, 5.1 us)
